TPU v7x, 128 devices: a whole 4x4x4 slice. The times are simulated.
128 devices in a mesh: fsdp: 8 (over y, x_hi), seq: 16 (over x_lo, z, core).
Axes of the slice: x: 4 (x_hi: 2, x_lo: 2; x = x_hi * 2 + x_lo), y: 4, z: 4, core: 2. Of those that a mesh axis runs over, the one named last changes fastest.
Arguments:
- hidden_in: bfloat16 [8, 4096, 4096], P('fsdp', 'seq'), may hold values from -6 to 6
- queries: bfloat16 [8, 4096, 2048], P('fsdp', 'seq'), may hold values from -8 to 8
- keys: bfloat16 [8, 4096, 2048], P('fsdp', 'seq'), may hold values from -8 to 8
- values: bfloat16 [8, 4096, 2048], P('fsdp', 'seq'), may hold values from -6 to 6
- block_start: int32 [32], P('seq'), may hold values from 0 to 3968, as said below
- out_weight: bfloat16 [2048, 4096], P('fsdp'), may hold values from -0.125 to 0.125
Outputs:
- mixed: bfloat16 [8, 4096, 4096], P('fsdp', 'seq')
Inputs may be any that keep to these rules, and one draw needn't show every extreme that they name: block_start is 128 times a permutation of 0 to 31.
All inputs are finite; a program needn't handle non-finite values.
Results may differ from a plain program's by a relative error of at most 0.006.
Values may be sent and summed in bfloat16 or wider, within the bound.
No kernel may reach another device: no remote copies, remote signals or barrier semaphores. Data moves between devices by JAX's collectives and lax.ppermute only.
A program may use at most 192 MiB of HBM per device.

v0:
```python
import math

import jax
import jax.numpy as jnp
from jax import lax
from jax.sharding import PartitionSpec as P

HEADS = 16
HEAD_DIM = 128


def rotate(source, positions):
    rows_here = source.shape[0]
    width = source.shape[1]
    half_dim = HEAD_DIM // 2
    spread = source.astype(jnp.float32).reshape(rows_here, width // HEAD_DIM, HEAD_DIM)
    frequency = 10000.0 ** (-jnp.arange(half_dim, dtype=jnp.float32) / half_dim)
    angles = positions.astype(jnp.float32)[:, None] * frequency[None, :]
    cosine = jnp.cos(angles)[:, None, :]
    sine = jnp.sin(angles)[:, None, :]
    first_half = spread[:, :, :half_dim]
    second_half = spread[:, :, half_dim:]
    turned = jnp.concatenate(
        [first_half * cosine - second_half * sine, second_half * cosine + first_half * sine],
        axis=-1,
    )
    return turned.reshape(rows_here, width).astype(jnp.bfloat16)


def block_rows(total_rows, half):
    common = math.gcd(total_rows, half)
    return max((divisor for divisor in range(1, min(common, 512) + 1) if common % divisor == 0))


def shards(hidden_in, queries, keys, values, block_start, out_weight):
    tok_rows = queries.shape[1]
    half = tok_rows // 2
    width = queries.shape[2]
    local_rows = jnp.arange(tok_rows, dtype=jnp.int32)
    own_pos = jnp.where(local_rows < half, block_start[0], block_start[1]) + local_rows % half
    starts_all = lax.all_gather(block_start, "seq", axis=0, tiled=True)
    q_rot = rotate(queries[0], own_pos).reshape(tok_rows, HEADS, HEAD_DIM)
    k_rot = rotate(keys[0], own_pos)
    table = jnp.arange(starts_all.shape[0], dtype=jnp.int32)
    scale = 1.0 / math.sqrt(HEAD_DIM)
    latest = jnp.max(own_pos)

    def attend_block(carry, key_block, value_block, key_pos):
        highest, total, accum = carry
        rows_here = key_block.shape[0]
        scores = (
            jnp.einsum(
                "qhd,khd->hqk",
                q_rot,
                key_block.reshape(rows_here, HEADS, HEAD_DIM),
                preferred_element_type=jnp.float32,
            )
            * scale
        )
        allowed = key_pos[None, :] <= own_pos[:, None]
        scores = jnp.where(allowed[None], scores, -1e30)
        new_high = jnp.maximum(highest, jnp.max(scores, axis=2))
        factor = jnp.exp(highest - new_high)
        weights = jnp.where(allowed[None], jnp.exp(scores - new_high[:, :, None]), 0.0)
        total = total * factor + jnp.sum(weights, axis=2)
        weighted = jnp.einsum(
            "hqk,khd->qhd",
            weights.astype(jnp.bfloat16),
            value_block.reshape(rows_here, HEADS, HEAD_DIM),
            preferred_element_type=jnp.float32,
        )
        accum = accum * jnp.transpose(factor)[:, :, None] + weighted
        return (new_high, total, accum)

    start_state = (
        jnp.full((HEADS, tok_rows), -1e30, jnp.float32),
        jnp.zeros((HEADS, tok_rows), jnp.float32),
        jnp.zeros((tok_rows, HEADS, HEAD_DIM), jnp.float32),
    )
    key_piece = lax.all_gather(k_rot, "seq", axis=0, tiled=True)
    value_piece = lax.all_gather(values[0], "seq", axis=0, tiled=True)
    rows_here = key_piece.shape[0]
    global_rows = jnp.arange(rows_here, dtype=jnp.int32)
    owner = global_rows // half
    key_pos = (
        jnp.sum(jnp.where(owner[:, None] == table[None, :], starts_all[None, :], 0), axis=1)
        + global_rows % half
    )
    step_rows = block_rows(rows_here, half)
    count_blocks = rows_here // step_rows

    def scan_step(state, items):
        key_block, value_block, block_pos = items
        result = lax.cond(
            jnp.min(block_pos) <= latest,
            lambda inner: attend_block(inner, key_block, value_block, block_pos),
            lambda inner: inner,
            state,
        )
        return (result, None)

    result, unused = lax.scan(
        scan_step,
        start_state,
        (
            key_piece.reshape(count_blocks, step_rows, width),
            value_piece.reshape(count_blocks, step_rows, width),
            key_pos.reshape(count_blocks, step_rows),
        ),
    )
    highest, total, accum = result
    attended = (
        (accum / jnp.transpose(total)[:, :, None]).astype(jnp.bfloat16).reshape(tok_rows, width)
    )
    residual = hidden_in[0].astype(jnp.float32)
    projected = jnp.dot(
        attended,
        lax.all_gather(out_weight, "fsdp", axis=0, tiled=True),
        preferred_element_type=jnp.float32,
    )
    return (residual + projected).astype(jnp.bfloat16)[None]


def solution(mesh):
    return jax.shard_map(
        shards,
        mesh=mesh,
        in_specs=(
            P("fsdp", "seq", None),
            P("fsdp", "seq", None),
            P("fsdp", "seq", None),
            P("fsdp", "seq", None),
            P("seq"),
            P("fsdp", None),
        ),
        out_specs=P("fsdp", "seq", None),
        check_vma=False,
    )
```

profile of v0, /device:TPU:96, one launch (start us, length us, event | category | flops | bytes accessed | tf_op | source)
XLA Modules:
  0.0 467.8 jit_solution(10525958574576909982)
XLA Ops:
  7.3 1.5 copy.28
  9.0 1.5 copy.29
  18.2 9.6 %all-reduce = s32[32]{0:T(128)S(1)} all-reduce(s32[32]{0:T(128)S(1)} %dynamic-update-slice), channel_id=1, replica_groups=mesh['fsdp'=8,'seq'=16] {'seq'}, use_global_device_ids=true, to_apply=%add | all-reduce | flops 32 | bytes 256
  27.8 2.0 fusion.26
  29.9 72.1 %all-gather.9.cloned.1.call-done = bf16[1,4096,2048]{2,1,0:T(8,128)(2,1)} async-done(((bf16[1,256,2048]{2,1,0:T(8,128)(2,1)}), bf16[1,4096,2048]{2,1,0:T(8,128)(2,1)}) %all-gather.9.cloned.1.call-update) | async-done | bytes 16777232 | tf_op jit(solution)/shard_map/all_gather | solution.py:81
  102.1 22.6 %copy.32 = bf16[32,128,2048]{1,2,0:T(8,128)(2,1)} copy(bf16[32,128,2048]{2,1,0:T(8,128)(2,1)} %bitcast.54) | data formatting | bytes 33554432
  124.6 78.0 %all-gather.5.cloned.1.call-done = bf16[4096,2048]{0,1:T(8,128)(2,1)} async-done(((bf16[256,2048]{0,1:T(8,128)(2,1)}), bf16[4096,2048]{0,1:T(8,128)(2,1)}) %all-gather.5.cloned.1.call-update) | async-done | bytes 16777232 | tf_op jit(solution)/shard_map/all_gather | solution.py:80
  202.6 14.9 %copy_bitcast_fusion = bf16[32,128,2048]{1,2,0:T(8,128)(2,1)} fusion(bf16[4096,2048]{0,1:T(8,128)(2,1)} %all-gather.5.cloned.1.call-done), kind=kLoop, calls=%fused_computation.27 | loop fusion | bytes 33554432
  217.8 227.9 %while.15 = (s32[]{:T(128)}, f32[16,256]{1,0:T(8,128)S(1)}, f32[16,256]{1,0:T(8,128)S(1)}, f32[256,16,128]{2,0,1:T(8,128)S(1)}, s32[32,128]{1,0:T(8,128)S(1)}, /...) while((s32[]{:T(128)}, f32[16,256]{1,0:T(8,128)S(1)}, ...), condition=%wide.region_8.9_spmd.clone, body=%wide.region_2.8_spmd.clone.sunk | while | flops 276347264 | bytes 15084399 | solution.py:102
  219.8 5.3 %conditional.3 = ((f32[16,256]{1,0:T(8,128)S(1)}, f32[16,256]{1,0:T(8,128)S(1)}, f32[256,16,128]{2,0,1:T(8,128)S(1)})) conditional(s32[]{:T(128)} %convert_element_type.71, (f32[16,256]{1,0:T(8,128)S(1)}, f32[16,256]{1,0:T(8,128)S(1)}, f32[256,16,128]{2,0,1:T(8,128)S(1)}) %tuple.55, (s32[1,128]{1,0:T(1,128)S(1)}, s32[256]{0:T(256)S(1)}, ...), branch_computations={%region_4.4_spmd, %region_5.7_spmd.clone} | conditional | flops 276346880 | bytes 15081012 | solution.py:94
  223.6 1.5 bitcast_add_fusion
  227.1 5.3 %conditional.3 = ((f32[16,256]{1,0:T(8,128)S(1)}, f32[16,256]{1,0:T(8,128)S(1)}, f32[256,16,128]{2,0,1:T(8,128)S(1)})) conditional(s32[]{:T(128)} %convert_element_type.71, (f32[16,256]{1,0:T(8,128)S(1)}, f32[16,256]{1,0:T(8,128)S(1)}, f32[256,16,128]{2,0,1:T(8,128)S(1)}) %tuple.55, (s32[1,128]{1,0:T(1,128)S(1)}, s32[256]{0:T(256)S(1)}, ...), branch_computations={%region_4.4_spmd, %region_5.7_spmd.clone} | conditional | flops 276346880 | bytes 15081012 | solution.py:94
  234.4 5.3 %conditional.3 = ((f32[16,256]{1,0:T(8,128)S(1)}, f32[16,256]{1,0:T(8,128)S(1)}, f32[256,16,128]{2,0,1:T(8,128)S(1)})) conditional(s32[]{:T(128)} %convert_element_type.71, (f32[16,256]{1,0:T(8,128)S(1)}, f32[16,256]{1,0:T(8,128)S(1)}, f32[256,16,128]{2,0,1:T(8,128)S(1)}) %tuple.55, (s32[1,128]{1,0:T(1,128)S(1)}, s32[256]{0:T(256)S(1)}, ...), branch_computations={%region_4.4_spmd, %region_5.7_spmd.clone} | conditional | flops 276346880 | bytes 15081012 | solution.py:94
  241.7 5.3 %conditional.3 = ((f32[16,256]{1,0:T(8,128)S(1)}, f32[16,256]{1,0:T(8,128)S(1)}, f32[256,16,128]{2,0,1:T(8,128)S(1)})) conditional(s32[]{:T(128)} %convert_element_type.71, (f32[16,256]{1,0:T(8,128)S(1)}, f32[16,256]{1,0:T(8,128)S(1)}, f32[256,16,128]{2,0,1:T(8,128)S(1)}) %tuple.55, (s32[1,128]{1,0:T(1,128)S(1)}, s32[256]{0:T(256)S(1)}, ...), branch_computations={%region_4.4_spmd, %region_5.7_spmd.clone} | conditional | flops 276346880 | bytes 15081012 | solution.py:94
  248.9 5.3 %conditional.3 = ((f32[16,256]{1,0:T(8,128)S(1)}, f32[16,256]{1,0:T(8,128)S(1)}, f32[256,16,128]{2,0,1:T(8,128)S(1)})) conditional(s32[]{:T(128)} %convert_element_type.71, (f32[16,256]{1,0:T(8,128)S(1)}, f32[16,256]{1,0:T(8,128)S(1)}, f32[256,16,128]{2,0,1:T(8,128)S(1)}) %tuple.55, (s32[1,128]{1,0:T(1,128)S(1)}, s32[256]{0:T(256)S(1)}, ...), branch_computations={%region_4.4_spmd, %region_5.7_spmd.clone} | conditional | flops 276346880 | bytes 15081012 | solution.py:94
  256.2 5.3 %conditional.3 = ((f32[16,256]{1,0:T(8,128)S(1)}, f32[16,256]{1,0:T(8,128)S(1)}, f32[256,16,128]{2,0,1:T(8,128)S(1)})) conditional(s32[]{:T(128)} %convert_element_type.71, (f32[16,256]{1,0:T(8,128)S(1)}, f32[16,256]{1,0:T(8,128)S(1)}, f32[256,16,128]{2,0,1:T(8,128)S(1)}) %tuple.55, (s32[1,128]{1,0:T(1,128)S(1)}, s32[256]{0:T(256)S(1)}, ...), branch_computations={%region_4.4_spmd, %region_5.7_spmd.clone} | conditional | flops 276346880 | bytes 15081012 | solution.py:94
  260.0 1.5 bitcast_add_fusion
  263.5 5.3 %conditional.3 = ((f32[16,256]{1,0:T(8,128)S(1)}, f32[16,256]{1,0:T(8,128)S(1)}, f32[256,16,128]{2,0,1:T(8,128)S(1)})) conditional(s32[]{:T(128)} %convert_element_type.71, (f32[16,256]{1,0:T(8,128)S(1)}, f32[16,256]{1,0:T(8,128)S(1)}, f32[256,16,128]{2,0,1:T(8,128)S(1)}) %tuple.55, (s32[1,128]{1,0:T(1,128)S(1)}, s32[256]{0:T(256)S(1)}, ...), branch_computations={%region_4.4_spmd, %region_5.7_spmd.clone} | conditional | flops 276346880 | bytes 15081012 | solution.py:94
  270.8 5.4 %conditional.3 = ((f32[16,256]{1,0:T(8,128)S(1)}, f32[16,256]{1,0:T(8,128)S(1)}, f32[256,16,128]{2,0,1:T(8,128)S(1)})) conditional(s32[]{:T(128)} %convert_element_type.71, (f32[16,256]{1,0:T(8,128)S(1)}, f32[16,256]{1,0:T(8,128)S(1)}, f32[256,16,128]{2,0,1:T(8,128)S(1)}) %tuple.55, (s32[1,128]{1,0:T(1,128)S(1)}, s32[256]{0:T(256)S(1)}, ...), branch_computations={%region_4.4_spmd, %region_5.7_spmd.clone} | conditional | flops 276346880 | bytes 15081012 | solution.py:94
  278.2 5.3 %conditional.3 = ((f32[16,256]{1,0:T(8,128)S(1)}, f32[16,256]{1,0:T(8,128)S(1)}, f32[256,16,128]{2,0,1:T(8,128)S(1)})) conditional(s32[]{:T(128)} %convert_element_type.71, (f32[16,256]{1,0:T(8,128)S(1)}, f32[16,256]{1,0:T(8,128)S(1)}, f32[256,16,128]{2,0,1:T(8,128)S(1)}) %tuple.55, (s32[1,128]{1,0:T(1,128)S(1)}, s32[256]{0:T(256)S(1)}, ...), branch_computations={%region_4.4_spmd, %region_5.7_spmd.clone} | conditional | flops 276346880 | bytes 15081012 | solution.py:94
  285.5 5.3 %conditional.3 = ((f32[16,256]{1,0:T(8,128)S(1)}, f32[16,256]{1,0:T(8,128)S(1)}, f32[256,16,128]{2,0,1:T(8,128)S(1)})) conditional(s32[]{:T(128)} %convert_element_type.71, (f32[16,256]{1,0:T(8,128)S(1)}, f32[16,256]{1,0:T(8,128)S(1)}, f32[256,16,128]{2,0,1:T(8,128)S(1)}) %tuple.55, (s32[1,128]{1,0:T(1,128)S(1)}, s32[256]{0:T(256)S(1)}, ...), branch_computations={%region_4.4_spmd, %region_5.7_spmd.clone} | conditional | flops 276346880 | bytes 15081012 | solution.py:94
  289.3 1.5 bitcast_add_fusion
  292.8 5.3 %conditional.3 = ((f32[16,256]{1,0:T(8,128)S(1)}, f32[16,256]{1,0:T(8,128)S(1)}, f32[256,16,128]{2,0,1:T(8,128)S(1)})) conditional(s32[]{:T(128)} %convert_element_type.71, (f32[16,256]{1,0:T(8,128)S(1)}, f32[16,256]{1,0:T(8,128)S(1)}, f32[256,16,128]{2,0,1:T(8,128)S(1)}) %tuple.55, (s32[1,128]{1,0:T(1,128)S(1)}, s32[256]{0:T(256)S(1)}, ...), branch_computations={%region_4.4_spmd, %region_5.7_spmd.clone} | conditional | flops 276346880 | bytes 15081012 | solution.py:94
  300.0 5.3 %conditional.3 = ((f32[16,256]{1,0:T(8,128)S(1)}, f32[16,256]{1,0:T(8,128)S(1)}, f32[256,16,128]{2,0,1:T(8,128)S(1)})) conditional(s32[]{:T(128)} %convert_element_type.71, (f32[16,256]{1,0:T(8,128)S(1)}, f32[16,256]{1,0:T(8,128)S(1)}, f32[256,16,128]{2,0,1:T(8,128)S(1)}) %tuple.55, (s32[1,128]{1,0:T(1,128)S(1)}, s32[256]{0:T(256)S(1)}, ...), branch_computations={%region_4.4_spmd, %region_5.7_spmd.clone} | conditional | flops 276346880 | bytes 15081012 | solution.py:94
  307.3 5.3 %conditional.3 = ((f32[16,256]{1,0:T(8,128)S(1)}, f32[16,256]{1,0:T(8,128)S(1)}, f32[256,16,128]{2,0,1:T(8,128)S(1)})) conditional(s32[]{:T(128)} %convert_element_type.71, (f32[16,256]{1,0:T(8,128)S(1)}, f32[16,256]{1,0:T(8,128)S(1)}, f32[256,16,128]{2,0,1:T(8,128)S(1)}) %tuple.55, (s32[1,128]{1,0:T(1,128)S(1)}, s32[256]{0:T(256)S(1)}, ...), branch_computations={%region_4.4_spmd, %region_5.7_spmd.clone} | conditional | flops 276346880 | bytes 15081012 | solution.py:94
  311.1 1.5 bitcast_add_fusion
  314.6 5.3 %conditional.3 = ((f32[16,256]{1,0:T(8,128)S(1)}, f32[16,256]{1,0:T(8,128)S(1)}, f32[256,16,128]{2,0,1:T(8,128)S(1)})) conditional(s32[]{:T(128)} %convert_element_type.71, (f32[16,256]{1,0:T(8,128)S(1)}, f32[16,256]{1,0:T(8,128)S(1)}, f32[256,16,128]{2,0,1:T(8,128)S(1)}) %tuple.55, (s32[1,128]{1,0:T(1,128)S(1)}, s32[256]{0:T(256)S(1)}, ...), branch_computations={%region_4.4_spmd, %region_5.7_spmd.clone} | conditional | flops 276346880 | bytes 15081012 | solution.py:94
  321.9 5.3 %conditional.3 = ((f32[16,256]{1,0:T(8,128)S(1)}, f32[16,256]{1,0:T(8,128)S(1)}, f32[256,16,128]{2,0,1:T(8,128)S(1)})) conditional(s32[]{:T(128)} %convert_element_type.71, (f32[16,256]{1,0:T(8,128)S(1)}, f32[16,256]{1,0:T(8,128)S(1)}, f32[256,16,128]{2,0,1:T(8,128)S(1)}) %tuple.55, (s32[1,128]{1,0:T(1,128)S(1)}, s32[256]{0:T(256)S(1)}, ...), branch_computations={%region_4.4_spmd, %region_5.7_spmd.clone} | conditional | flops 276346880 | bytes 15081012 | solution.py:94
  331.2 5.3 %conditional.3 = ((f32[16,256]{1,0:T(8,128)S(1)}, f32[16,256]{1,0:T(8,128)S(1)}, f32[256,16,128]{2,0,1:T(8,128)S(1)})) conditional(s32[]{:T(128)} %convert_element_type.71, (f32[16,256]{1,0:T(8,128)S(1)}, f32[16,256]{1,0:T(8,128)S(1)}, f32[256,16,128]{2,0,1:T(8,128)S(1)}) %tuple.55, (s32[1,128]{1,0:T(1,128)S(1)}, s32[256]{0:T(256)S(1)}, ...), branch_computations={%region_4.4_spmd, %region_5.7_spmd.clone} | conditional | flops 276346880 | bytes 15081012 | solution.py:94
  338.5 5.3 %conditional.3 = ((f32[16,256]{1,0:T(8,128)S(1)}, f32[16,256]{1,0:T(8,128)S(1)}, f32[256,16,128]{2,0,1:T(8,128)S(1)})) conditional(s32[]{:T(128)} %convert_element_type.71, (f32[16,256]{1,0:T(8,128)S(1)}, f32[16,256]{1,0:T(8,128)S(1)}, f32[256,16,128]{2,0,1:T(8,128)S(1)}) %tuple.55, (s32[1,128]{1,0:T(1,128)S(1)}, s32[256]{0:T(256)S(1)}, ...), branch_computations={%region_4.4_spmd, %region_5.7_spmd.clone} | conditional | flops 276346880 | bytes 15081012 | solution.py:94
  342.3 1.5 bitcast_add_fusion
  345.8 5.3 %conditional.3 = ((f32[16,256]{1,0:T(8,128)S(1)}, f32[16,256]{1,0:T(8,128)S(1)}, f32[256,16,128]{2,0,1:T(8,128)S(1)})) conditional(s32[]{:T(128)} %convert_element_type.71, (f32[16,256]{1,0:T(8,128)S(1)}, f32[16,256]{1,0:T(8,128)S(1)}, f32[256,16,128]{2,0,1:T(8,128)S(1)}) %tuple.55, (s32[1,128]{1,0:T(1,128)S(1)}, s32[256]{0:T(256)S(1)}, ...), branch_computations={%region_4.4_spmd, %region_5.7_spmd.clone} | conditional | flops 276346880 | bytes 15081012 | solution.py:94
  353.0 5.3 %conditional.3 = ((f32[16,256]{1,0:T(8,128)S(1)}, f32[16,256]{1,0:T(8,128)S(1)}, f32[256,16,128]{2,0,1:T(8,128)S(1)})) conditional(s32[]{:T(128)} %convert_element_type.71, (f32[16,256]{1,0:T(8,128)S(1)}, f32[16,256]{1,0:T(8,128)S(1)}, f32[256,16,128]{2,0,1:T(8,128)S(1)}) %tuple.55, (s32[1,128]{1,0:T(1,128)S(1)}, s32[256]{0:T(256)S(1)}, ...), branch_computations={%region_4.4_spmd, %region_5.7_spmd.clone} | conditional | flops 276346880 | bytes 15081012 | solution.py:94
  360.3 5.3 %conditional.3 = ((f32[16,256]{1,0:T(8,128)S(1)}, f32[16,256]{1,0:T(8,128)S(1)}, f32[256,16,128]{2,0,1:T(8,128)S(1)})) conditional(s32[]{:T(128)} %convert_element_type.71, (f32[16,256]{1,0:T(8,128)S(1)}, f32[16,256]{1,0:T(8,128)S(1)}, f32[256,16,128]{2,0,1:T(8,128)S(1)}) %tuple.55, (s32[1,128]{1,0:T(1,128)S(1)}, s32[256]{0:T(256)S(1)}, ...), branch_computations={%region_4.4_spmd, %region_5.7_spmd.clone} | conditional | flops 276346880 | bytes 15081012 | solution.py:94
  367.6 5.3 %conditional.3 = ((f32[16,256]{1,0:T(8,128)S(1)}, f32[16,256]{1,0:T(8,128)S(1)}, f32[256,16,128]{2,0,1:T(8,128)S(1)})) conditional(s32[]{:T(128)} %convert_element_type.71, (f32[16,256]{1,0:T(8,128)S(1)}, f32[16,256]{1,0:T(8,128)S(1)}, f32[256,16,128]{2,0,1:T(8,128)S(1)}) %tuple.55, (s32[1,128]{1,0:T(1,128)S(1)}, s32[256]{0:T(256)S(1)}, ...), branch_computations={%region_4.4_spmd, %region_5.7_spmd.clone} | conditional | flops 276346880 | bytes 15081012 | solution.py:94
  374.9 5.3 %conditional.3 = ((f32[16,256]{1,0:T(8,128)S(1)}, f32[16,256]{1,0:T(8,128)S(1)}, f32[256,16,128]{2,0,1:T(8,128)S(1)})) conditional(s32[]{:T(128)} %convert_element_type.71, (f32[16,256]{1,0:T(8,128)S(1)}, f32[16,256]{1,0:T(8,128)S(1)}, f32[256,16,128]{2,0,1:T(8,128)S(1)}) %tuple.55, (s32[1,128]{1,0:T(1,128)S(1)}, s32[256]{0:T(256)S(1)}, ...), branch_computations={%region_4.4_spmd, %region_5.7_spmd.clone} | conditional | flops 276346880 | bytes 15081012 | solution.py:94
  382.2 5.3 %conditional.3 = ((f32[16,256]{1,0:T(8,128)S(1)}, f32[16,256]{1,0:T(8,128)S(1)}, f32[256,16,128]{2,0,1:T(8,128)S(1)})) conditional(s32[]{:T(128)} %convert_element_type.71, (f32[16,256]{1,0:T(8,128)S(1)}, f32[16,256]{1,0:T(8,128)S(1)}, f32[256,16,128]{2,0,1:T(8,128)S(1)}) %tuple.55, (s32[1,128]{1,0:T(1,128)S(1)}, s32[256]{0:T(256)S(1)}, ...), branch_computations={%region_4.4_spmd, %region_5.7_spmd.clone} | conditional | flops 276346880 | bytes 15081012 | solution.py:94
  389.4 5.3 %conditional.3 = ((f32[16,256]{1,0:T(8,128)S(1)}, f32[16,256]{1,0:T(8,128)S(1)}, f32[256,16,128]{2,0,1:T(8,128)S(1)})) conditional(s32[]{:T(128)} %convert_element_type.71, (f32[16,256]{1,0:T(8,128)S(1)}, f32[16,256]{1,0:T(8,128)S(1)}, f32[256,16,128]{2,0,1:T(8,128)S(1)}) %tuple.55, (s32[1,128]{1,0:T(1,128)S(1)}, s32[256]{0:T(256)S(1)}, ...), branch_computations={%region_4.4_spmd, %region_5.7_spmd.clone} | conditional | flops 276346880 | bytes 15081012 | solution.py:94
  396.7 5.3 %conditional.3 = ((f32[16,256]{1,0:T(8,128)S(1)}, f32[16,256]{1,0:T(8,128)S(1)}, f32[256,16,128]{2,0,1:T(8,128)S(1)})) conditional(s32[]{:T(128)} %convert_element_type.71, (f32[16,256]{1,0:T(8,128)S(1)}, f32[16,256]{1,0:T(8,128)S(1)}, f32[256,16,128]{2,0,1:T(8,128)S(1)}) %tuple.55, (s32[1,128]{1,0:T(1,128)S(1)}, s32[256]{0:T(256)S(1)}, ...), branch_computations={%region_4.4_spmd, %region_5.7_spmd.clone} | conditional | flops 276346880 | bytes 15081012 | solution.py:94
  404.0 5.3 %conditional.3 = ((f32[16,256]{1,0:T(8,128)S(1)}, f32[16,256]{1,0:T(8,128)S(1)}, f32[256,16,128]{2,0,1:T(8,128)S(1)})) conditional(s32[]{:T(128)} %convert_element_type.71, (f32[16,256]{1,0:T(8,128)S(1)}, f32[16,256]{1,0:T(8,128)S(1)}, f32[256,16,128]{2,0,1:T(8,128)S(1)}) %tuple.55, (s32[1,128]{1,0:T(1,128)S(1)}, s32[256]{0:T(256)S(1)}, ...), branch_computations={%region_4.4_spmd, %region_5.7_spmd.clone} | conditional | flops 276346880 | bytes 15081012 | solution.py:94
  411.3 5.3 %conditional.3 = ((f32[16,256]{1,0:T(8,128)S(1)}, f32[16,256]{1,0:T(8,128)S(1)}, f32[256,16,128]{2,0,1:T(8,128)S(1)})) conditional(s32[]{:T(128)} %convert_element_type.71, (f32[16,256]{1,0:T(8,128)S(1)}, f32[16,256]{1,0:T(8,128)S(1)}, f32[256,16,128]{2,0,1:T(8,128)S(1)}) %tuple.55, (s32[1,128]{1,0:T(1,128)S(1)}, s32[256]{0:T(256)S(1)}, ...), branch_computations={%region_4.4_spmd, %region_5.7_spmd.clone} | conditional | flops 276346880 | bytes 15081012 | solution.py:94
  418.6 5.3 %conditional.3 = ((f32[16,256]{1,0:T(8,128)S(1)}, f32[16,256]{1,0:T(8,128)S(1)}, f32[256,16,128]{2,0,1:T(8,128)S(1)})) conditional(s32[]{:T(128)} %convert_element_type.71, (f32[16,256]{1,0:T(8,128)S(1)}, f32[16,256]{1,0:T(8,128)S(1)}, f32[256,16,128]{2,0,1:T(8,128)S(1)}) %tuple.55, (s32[1,128]{1,0:T(1,128)S(1)}, s32[256]{0:T(256)S(1)}, ...), branch_computations={%region_4.4_spmd, %region_5.7_spmd.clone} | conditional | flops 276346880 | bytes 15081012 | solution.py:94
  425.9 5.3 %conditional.3 = ((f32[16,256]{1,0:T(8,128)S(1)}, f32[16,256]{1,0:T(8,128)S(1)}, f32[256,16,128]{2,0,1:T(8,128)S(1)})) conditional(s32[]{:T(128)} %convert_element_type.71, (f32[16,256]{1,0:T(8,128)S(1)}, f32[16,256]{1,0:T(8,128)S(1)}, f32[256,16,128]{2,0,1:T(8,128)S(1)}) %tuple.55, (s32[1,128]{1,0:T(1,128)S(1)}, s32[256]{0:T(256)S(1)}, ...), branch_computations={%region_4.4_spmd, %region_5.7_spmd.clone} | conditional | flops 276346880 | bytes 15081012 | solution.py:94
  433.1 5.3 %conditional.3 = ((f32[16,256]{1,0:T(8,128)S(1)}, f32[16,256]{1,0:T(8,128)S(1)}, f32[256,16,128]{2,0,1:T(8,128)S(1)})) conditional(s32[]{:T(128)} %convert_element_type.71, (f32[16,256]{1,0:T(8,128)S(1)}, f32[16,256]{1,0:T(8,128)S(1)}, f32[256,16,128]{2,0,1:T(8,128)S(1)}) %tuple.55, (s32[1,128]{1,0:T(1,128)S(1)}, s32[256]{0:T(256)S(1)}, ...), branch_computations={%region_4.4_spmd, %region_5.7_spmd.clone} | conditional | flops 276346880 | bytes 15081012 | solution.py:94
  440.4 5.3 %conditional.3 = ((f32[16,256]{1,0:T(8,128)S(1)}, f32[16,256]{1,0:T(8,128)S(1)}, f32[256,16,128]{2,0,1:T(8,128)S(1)})) conditional(s32[]{:T(128)} %convert_element_type.71, (f32[16,256]{1,0:T(8,128)S(1)}, f32[16,256]{1,0:T(8,128)S(1)}, f32[256,16,128]{2,0,1:T(8,128)S(1)}) %tuple.55, (s32[1,128]{1,0:T(1,128)S(1)}, s32[256]{0:T(256)S(1)}, ...), branch_computations={%region_4.4_spmd, %region_5.7_spmd.clone} | conditional | flops 276346880 | bytes 15081012 | solution.py:94
  445.7 1.8 copy.33
  447.5 1.9 divide_convert_fusion
  449.7 11.5 %fusion.18 = bf16[1,256,4096]{2,1,0:T(8,128)(2,1)} fusion(bf16[256,2048]{0,1:T(8,128)(2,1)S(1)} %bitcast.58, bf16[2048,4096]{1,0:T(8,128)(2,1)} %all-gather.7.cloned.1.call-done, bf16[1,256,4096]{2,1,0:T(8,128)(2,1)S(1)} %copy-done), kind=kOutput, calls=%fused_computation.30 | convolution fusion | flops 4298113024 | bytes 22020096 | tf_op jit(solution)/shard_map/dot_general | solution.py:116
  (403 shorter events, 182.8 us)
Async XLA Ops:
  6.5 95.5 %all-gather.9.cloned.1.call-start = ((), (), s32[]{:S(2)}) async-start(), calls=%async_computation.2 | async-start | bytes 17825792 | tf_op jit(solution)/shard_map/all_gather | solution.py:81
  7.3 195.4 %all-gather.5.cloned.1.call-start = ((), (), s32[]{:S(2)}) async-start(), calls=%async_computation | async-start | bytes 17825792 | tf_op jit(solution)/shard_map/all_gather | solution.py:80
  10.5 0.7 copy-start.1
  15.0 434.5 %all-gather.7.cloned.1.call-start = ((), (), s32[]{:S(2)}) async-start(), calls=%async_computation.1 | async-start | bytes 18874368 | tf_op jit(solution)/shard_map/all_gather | solution.py:118
  15.8 0.8 copy-start.2
  447.5 2.2 copy-start
Sparse Core Ops, SparseCore 0:
  9.1 92.9 all-gather.8
  103.7 98.9 all-gather.4
  205.0 184.1 all-gather.6
where the time goes:
time: 477 us; the launch traced here: 468 us
  waiting for transfers between devices  152 us (32%)
  other arithmetic  87.2 us (18%)
  local copies, waits for them, and re-layouts  85.2 us (18%)
  matrix products  74 us (16%)
  loops' own time  46.2 us (10%)
  between operations  14 us (3%)
  blocking collectives  9.62 us (2%)
    all_gather x1, waiting for transfers between devices, shards(): key_piece = lax.all_gather(k_rot, 'seq', axis=0, tiled=True)  78 us
    all_gather x1, waiting for transfers between devices, shards(): value_piece = lax.all_gather(values[0], 'seq', axis=0, tiled=True)  72.1 us
    dot_general x31, matrix products, attend_block(): jnp.einsum('hqk,khd->qhd', weights.astype(jnp.bfloat16), value_block.resh...  45.4 us
    another operation x1, loops' own time, shards(): lax.scan(scan_step, start_state, (key_piece.reshape(count_blocks, step_ro...  43.8 us
    unnamed x14, local copies, waits for them, and re-layouts  42.7 us
    dynamic_slice x31, local copies, waits for them, and re-layouts, shards(): lax.scan(scan_step, start_state, (key_piece.reshape(count_blocks, step_ro...  39.7 us
    add x31, other arithmetic, shards(): jnp.where(local_rows < half, block_start[0], block_start[1])  39 us
    reduce_min x32, other arithmetic, scan_step(): jnp.min(block_pos) <= latest  20.4 us
  transfers between devices with their start and end apart: 3, of which 2 were waited for; matrix products, arithmetic and copies ran while one was open for 50% of the time, Pallas kernels for 0%

commit v1 on v0

v1 whole, which is shorter than its diff:
```python
import functools
import itertools
import math

import jax
import jax.numpy as jnp
import numpy as np
from jax import lax
from jax.experimental import pallas as pl
from jax.experimental.pallas import tpu as pltpu
from jax.sharding import Mesh
from jax.sharding import PartitionSpec as P

HEADS = 16
HEAD_DIM = 128
LEN = 4096
HALF = 128
WIDTH = HEADS * HEAD_DIM
D = 4096
ROWS = 3 * HALF + 16
AXES = ("y", "xh", "xl", "z", "c")
SIZES = (4, 2, 2, 4, 2)
FSDP = ("y", "xh")
SEQ = ("xl", "z", "c")
VMEM = 56 * 2**20


def tables():
    frequency = 10000.0 ** (-np.arange(HEAD_DIM // 2) / (HEAD_DIM // 2))
    angles = np.arange(LEN)[:, None] * frequency[None, :]
    cosine, sine = np.cos(angles), np.sin(angles)
    return (
        np.concatenate([cosine, cosine], axis=1).astype(np.float32),
        np.concatenate([-sine, sine], axis=1).astype(np.float32),
    )


def send(array, move):
    places = list(itertools.product(*map(range, SIZES)))
    index = {place: i for i, place in enumerate(places)}
    return lax.ppermute(array, AXES, [(index[p], index[move(*p)]) for p in places])


def y_up(y, xh, xl, z, c):
    return ((y + 1) % 4, xh, xl, z, c)


def y_down(y, xh, xl, z, c):
    return ((y + 3) % 4, xh, xl, z, c)


def x_over(y, xh, xl, z, c):
    return (y, 1 - xh, 1 - xl, z, c)


def core_over(y, xh, xl, z, c):
    return (y, xh, xl, z, 1 - c)


def pack_kernel(starts, q_ref, k_ref, v_ref, cos_ref, sin_ref, out_ref):
    cosine, sine = cos_ref[...], sin_ref[...]
    factor = math.log2(math.e) / math.sqrt(HEAD_DIM)

    def turn(block, cosine, sine):
        block = block.astype(jnp.float32)
        turned = block * cosine + pltpu.roll(block, HEAD_DIM // 2, 1) * sine
        return turned.astype(jnp.bfloat16)

    for h in range(HEADS):
        lanes = slice(h * HEAD_DIM, (h + 1) * HEAD_DIM)
        out_ref[h, 0, 0:HALF] = turn(q_ref[:, lanes], cosine * factor, sine * factor)
        out_ref[h, 0, HALF : 2 * HALF] = turn(k_ref[:, lanes], cosine, sine)
        out_ref[h, 0, 2 * HALF : 3 * HALF] = v_ref[:, lanes]
    block = (starts[pl.program_id(0)] // HALF).astype(jnp.float32)
    out_ref[:, 0, 3 * HALF :] = jnp.full((HEADS, 16, HEAD_DIM), block, jnp.float32).astype(
        jnp.bfloat16
    )


def pack(starts, queries, keys, values):
    cosine, sine = tables()
    rows = pl.BlockSpec((HALF, WIDTH), lambda b, s: (b, 0))
    table = pl.BlockSpec((HALF, HEAD_DIM), lambda b, s: (s[b] // HALF, 0))
    return pl.pallas_call(
        pack_kernel,
        grid_spec=pltpu.PrefetchScalarGridSpec(
            num_scalar_prefetch=1,
            grid=(2,),
            in_specs=[rows, rows, rows, table, table],
            out_specs=pl.BlockSpec((HEADS, 1, ROWS, HEAD_DIM), lambda b, s: (0, b, 0, 0)),
        ),
        out_shape=jax.ShapeDtypeStruct((HEADS, 2, ROWS, HEAD_DIM), jnp.bfloat16),
        compiler_params=pltpu.CompilerParams(vmem_limit_bytes=VMEM),
        name="pack",
    )(starts, queries, keys, values, jnp.asarray(cosine), jnp.asarray(sine))


def attention_kernel(pos_ref, x_ref, o_ref, qs, kt, vs, scores, acc, high, *, tq):
    tiles = LEN // tq
    vs[:, HEAD_DIM:] = jnp.ones((LEN, HEAD_DIM), jnp.bfloat16)

    def place(t, carry):
        at = pl.ds(pl.multiple_of(pos_ref[t] * HALF, HALF), HALF)
        s, b = t // 2, t % 2
        qs[at, :] = x_ref[s, b, 0:HALF, :]
        kt[:, at] = x_ref[s, b, HALF : 2 * HALF, :].T
        vs[at, :HEAD_DIM] = x_ref[s, b, 2 * HALF : 3 * HALF, :]
        return carry

    lax.fori_loop(0, 2 * HEADS, place, 0, unroll=4)

    def span(i):
        return pl.ds(pl.multiple_of(i * tq, tq), tq)

    def product(i, j):
        return jnp.dot(qs[span(i), :], kt[:, span(j)], preferred_element_type=jnp.float32)

    def lane_max(s):
        m = s[:, :128]
        for c in range(1, tq // 128):
            m = jnp.maximum(m, s[:, c * 128 : (c + 1) * 128])
        return m

    row = lax.broadcasted_iota(jnp.int32, (tq, tq), 0)
    col = lax.broadcasted_iota(jnp.int32, (tq, tq), 1)

    def diagonal(i, slot):
        s = jnp.where(col <= row, product(i, i), -1e30)
        scores[slot, :, span(i)] = s
        return lane_max(s)

    high[...] = diagonal(0, 0)

    def tile(i, carry):
        now = lax.rem(i, 2)
        later = 1 - now
        m = jnp.broadcast_to(jnp.max(high[...], axis=1, keepdims=True), (tq, 128))
        high[...] = jnp.full((tq, 128), -1e30, jnp.float32)
        acc[...] = jnp.zeros((tq, 2 * HEAD_DIM), jnp.float32)
        following = jnp.minimum(i + 1, tiles - 1)

        def chunk(j, inner):
            s = scores[now, :, span(j)]
            p = jnp.concatenate(
                [
                    jnp.exp2(s[:, t * 128 : (t + 1) * 128] - m).astype(jnp.bfloat16)
                    for t in range(tq // 128)
                ],
                axis=1,
            )
            acc[...] += jnp.dot(p, vs[span(j), :], preferred_element_type=jnp.float32)
            ahead = product(following, j)
            scores[later, :, span(j)] = ahead
            high[...] = jnp.maximum(high[...], lane_max(ahead))
            return inner

        lax.fori_loop(0, i + 1, chunk, 0)

        @pl.when(i + 1 < tiles)
        def _():
            high[...] = jnp.maximum(high[...], diagonal(following, later))

        qs[span(i), :] = (acc[:, :HEAD_DIM] / acc[:, HEAD_DIM:]).astype(jnp.bfloat16)
        return carry

    lax.fori_loop(0, tiles, tile, 0)

    def unplace(t, carry):
        at = pl.ds(pl.multiple_of(pos_ref[t] * HALF, HALF), HALF)
        o_ref[t // 2, t % 2] = qs[at, :]
        return carry

    lax.fori_loop(0, 2 * HEADS, unplace, 0, unroll=4)


def attention(pos, packed, tq=512):
    return pl.pallas_call(
        functools.partial(attention_kernel, tq=tq),
        out_shape=jax.ShapeDtypeStruct((HEADS, 2, HALF, HEAD_DIM), jnp.bfloat16),
        in_specs=[
            pl.BlockSpec(memory_space=pltpu.SMEM),
            pl.BlockSpec(memory_space=pltpu.VMEM),
        ],
        out_specs=pl.BlockSpec(memory_space=pltpu.VMEM),
        scratch_shapes=[
            pltpu.VMEM((LEN, HEAD_DIM), jnp.bfloat16),
            pltpu.VMEM((HEAD_DIM, LEN), jnp.bfloat16),
            pltpu.VMEM((LEN, 2 * HEAD_DIM), jnp.bfloat16),
            pltpu.VMEM((2, tq, LEN), jnp.float32),
            pltpu.VMEM((tq, 2 * HEAD_DIM), jnp.float32),
            pltpu.VMEM((tq, 128), jnp.float32),
        ],
        compiler_params=pltpu.CompilerParams(vmem_limit_bytes=VMEM),
        cost_estimate=pl.CostEstimate(
            flops=2 * LEN * LEN * HEAD_DIM, bytes_accessed=4 * 2**20, transcendentals=LEN * LEN // 2
        ),
        name="attention",
    )(pos, packed)


PIECES = ((0, 0), (0, 1), (3, 0), (1, 0), (3, 1), (1, 1), (2, 0), (2, 1))
STEP = 512


def project_kernel(place, att_ref, hidden_ref, own_ref, *refs):
    mine, other, (out_ref, left) = refs[:8], refs[8:16], refs[16:]
    step = pl.program_id(0)

    @pl.when(step == 0)
    def _():
        for n in range(len(PIECES)):
            for t in range(2):
                head = att_ref[2 * place[1 + n] + t].reshape(2 * HALF, HEAD_DIM)
                left[:, (2 * n + t) * HEAD_DIM : (2 * n + t + 1) * HEAD_DIM] = head

    def total(blocks):
        rows = jnp.concatenate([own_ref[...]] + [b[...] for b in blocks], axis=0)
        summed = jnp.dot(left[...], rows, preferred_element_type=jnp.float32)
        out_ref[...] = (hidden_ref[...].astype(jnp.float32) + summed).astype(jnp.bfloat16)

    @pl.when(step < 4)
    def _():
        total(mine)

    @pl.when(step >= 4)
    def _():
        total(other)


def project(place, att, hidden, own, mine, other):
    def column(j, s):
        return (0, (s[0] * 4 + j) % 8)

    def spec(array, index):
        return pl.BlockSpec((array.shape[0], STEP), index)

    return pl.pallas_call(
        project_kernel,
        grid_spec=pltpu.PrefetchScalarGridSpec(
            num_scalar_prefetch=1,
            grid=(D // STEP,),
            in_specs=[
                pl.BlockSpec((HEADS, 2, HALF, HEAD_DIM), lambda j, s: (0, 0, 0, 0)),
                spec(hidden, column),
                spec(own, column),
                *[spec(a, lambda j, s: (0, jnp.minimum(j, 3))) for a in mine],
                *[spec(a, lambda j, s: (0, jnp.maximum(j - 4, 0))) for a in other],
            ],
            out_specs=pl.BlockSpec((2 * HALF, STEP), column),
            scratch_shapes=[pltpu.VMEM((2 * HALF, WIDTH), jnp.bfloat16)],
        ),
        out_shape=jax.ShapeDtypeStruct((2 * HALF, D), jnp.bfloat16),
        compiler_params=pltpu.CompilerParams(vmem_limit_bytes=VMEM),
        cost_estimate=pl.CostEstimate(
            flops=4 * HALF * WIDTH * D, bytes_accessed=20 * 2**20, transcendentals=0
        ),
        name="project",
    )(place, att, hidden, own, *mine, *other)


def shards(hidden_in, queries, keys, values, block_start, out_weight):
    y, xh, c = lax.axis_index("y"), lax.axis_index("xh"), lax.axis_index("c")
    packed = pack(block_start, queries[0], keys[0], values[0])
    packed = lax.all_to_all(packed, SEQ, 0, 0, tiled=True)

    half = lax.dynamic_slice(out_weight, (0, c * (D // 2)), (WIDTH // 8, D // 2))
    piece = {}
    piece[0, 1] = send(half, x_over)
    piece[3, 0] = send(half, y_up)
    piece[1, 0] = send(half, y_down)
    piece[3, 1] = send(piece[3, 0], x_over)
    piece[1, 1] = send(piece[0, 1], y_down)
    piece[2, 0] = send(piece[3, 0], y_up)
    top = send(piece[3, 1][:HALF], y_up)
    bottom = send(piece[1, 1][HALF:], y_down)
    mine = [piece[at] for at in PIECES[1:7]] + [top, bottom]
    other = [send(a, core_over) for a in mine]

    pos = packed[:, :, 3 * HALF, 0].reshape(2 * HEADS).astype(jnp.int32)
    attended = attention(pos, packed)
    attended = lax.all_to_all(attended, SEQ, 0, 0, tiled=True)

    owners = [((y + dy) % 4) * 2 + (xh + dx) % 2 for dy, dx in PIECES]
    place = jnp.stack([c, *owners]).astype(jnp.int32)
    return project(place, attended, hidden_in[0], out_weight, mine, other)[None]


def solution(mesh):
    fine = Mesh(mesh.devices.reshape(SIZES), AXES)
    return jax.shard_map(
        shards,
        mesh=fine,
        in_specs=(
            P(FSDP, SEQ, None),
            P(FSDP, SEQ, None),
            P(FSDP, SEQ, None),
            P(FSDP, SEQ, None),
            P(SEQ),
            P(FSDP, None),
        ),
        out_specs=P(FSDP, SEQ, None),
        check_vma=False,
    )
```

time: 477 us -> 133 us (0.28)
  the two profiles are of different devices: /device:TPU:96 before, /device:TPU:1 now
where the time goes in v1:
time: 133 us; the launch traced here: 132 us
  waiting for transfers between devices  54.7 us (41%)
  Pallas kernels  41.9 us (32%)
  starting transfers between devices  30 us (23%)
  local copies, waits for them, and re-layouts  4.17 us (3%)
  other arithmetic  1.49 us (1%)
    ppermute x16, waiting for transfers between devices, send(): lax.ppermute(array, AXES, [(index[p], index[move(*p)]) for p in places])  41.9 us
    pallas_call x1, Pallas kernels, attention(): pl.pallas_call(functools.partial(attention_kernel, tq=tq), out_shape=jax....  23.9 us
    ppermute x16, starting transfers between devices, send(): lax.ppermute(array, AXES, [(index[p], index[move(*p)]) for p in places])  17.7 us
    pallas_call x1, Pallas kernels, project(): pl.pallas_call(project_kernel, grid_spec=pltpu.PrefetchScalarGridSpec(num...  13.4 us
    all_to_all x1, waiting for transfers between devices, shards(): attended = lax.all_to_all(attended, SEQ, 0, 0, tiled=True)  12.7 us
    all_to_all x1, starting transfers between devices, shards(): packed = lax.all_to_all(packed, SEQ, 0, 0, tiled=True)  7.89 us
    pallas_call x1, Pallas kernels, pack(): pl.pallas_call(pack_kernel, grid_spec=pltpu.PrefetchScalarGridSpec(num_sc...  4.63 us
    all_to_all x1, starting transfers between devices, shards(): attended = lax.all_to_all(attended, SEQ, 0, 0, tiled=True)  4.4 us
  transfers between devices with their start and end apart: 18, of which 5 were waited for; matrix products, arithmetic and copies ran while one was open for 4% of the time, Pallas kernels for 18%

profile of v1, /device:TPU:1, one launch (start us, length us, event | category | flops | bytes accessed | tf_op | source)
XLA Modules:
  0.0 132.3 jit_solution(3856199769404866964)
XLA Ops:
  0.0 4.6 %pack.1 = bf16[16,2,400,128]{3,2,1,0:T(8,128)(2,1)} custom-call(s32[2]{0:T(128)} %starts.1, bf16[256,2048]{1,0:T(8,128)(2,1)} %bitcast.15, bf16[256,2048]{1,0:T(8,128)(2,1)} %bitcast.16, bf16[256,2048]{1,0:T(8,128)(2,1)} %bitcast.17, f32[4096,128]{1,0:T(8,128)} %constant.84.clone.cos_ref, f32[4096,128]{1,0:T(8,128)} %constant.85.clone.sin_ref), custom_call_target="tpu_custom_call" | custom-call | tf_op jit(solution)/shard_map/pack/pallas_call | solution.py:84
  4.6 7.9 %all-to-all-start = ((bf16[16,2,400,128]{3,2,1,0:T(8,128)(2,1)}), bf16[16,2,400,128]{3,2,1,0:T(8,128)(2,1)}, u32[]{:S(2)}, u32[]{:S(2)}) async-start(bf16[16,2,400,128]{3,2,1,0:T(8,128)(2,1)} %pack.1), calls=%async_computation | async-start | bytes 6553600 | tf_op jit(solution)/shard_map/all_to_all | solution.py:264
  12.5 0.0 copy-done
  12.5 0.1 constant_dynamic-slice_fusion
  12.6 1.4 %collective-permute-start.1 = (bf16[256,2048]{1,0:T(8,128)(2,1)S(1)}, bf16[256,2048]{1,0:T(8,128)(2,1)S(1)}, u32[]{:S(2)}, u32[]{:S(2)}) collective-permute-start(bf16[256,2048]{1,0:T(8,128)(2,1)S(1)} %constant_dynamic-slice_fusion), channel_id=1, source_target_pairs={{0,32},{1,33},{2,34},{3,35},{4,36},{5,37},{6,38},{7,39},{8,40},{9,... | collective-permute-start | bytes 3145736 | tf_op jit(solution)/shard_map/ppermute | solution.py:41
  14.0 2.7 %collective-permute-start = (bf16[256,2048]{1,0:T(8,128)(2,1)S(1)}, bf16[256,2048]{1,0:T(8,128)(2,1)}, u32[]{:S(2)}, u32[]{:S(2)}) collective-permute-start(bf16[256,2048]{1,0:T(8,128)(2,1)S(1)} %constant_dynamic-slice_fusion), channel_id=1, source_target_pairs={{0,24},{1,25},{2,26},{3,27},{4,28},{5,29},{6,30},{7,31},{8,16},{9,... | collective-permute-start | bytes 3145736 | tf_op jit(solution)/shard_map/ppermute | solution.py:41
  16.6 1.5 %collective-permute-start.2 = (bf16[256,2048]{1,0:T(8,128)(2,1)S(1)}, bf16[256,2048]{1,0:T(8,128)(2,1)}, u32[]{:S(2)}, u32[]{:S(2)}) collective-permute-start(bf16[256,2048]{1,0:T(8,128)(2,1)S(1)} %constant_dynamic-slice_fusion), channel_id=1, source_target_pairs={{0,96},{1,97},{2,98},{3,99},{4,100},{5,101},{6,102},{7,103},{8,104... | collective-permute-start | bytes 3145736 | tf_op jit(solution)/shard_map/ppermute | solution.py:41
  18.2 20.6 %collective-permute-done.1.refs_1_ = bf16[256,2048]{1,0:T(8,128)(2,1)S(1)} collective-permute-done((bf16[256,2048]{1,0:T(8,128)(2,1)S(1)}, bf16[256,2048]{1,0:T(8,128)(2,1)S(1)}, u32[]{:S(2)}, u32[]{:S(2)}) %collective-permute-start.1) | collective-permute-done | bytes 1048608 | tf_op jit(solution)/shard_map/ppermute | solution.py:41
  38.8 2.4 %collective-permute-start.3 = (bf16[256,2048]{1,0:T(8,128)(2,1)S(1)}, bf16[256,2048]{1,0:T(8,128)(2,1)S(1)}, u32[]{:S(2)}, u32[]{:S(2)}) collective-permute-start(bf16[256,2048]{1,0:T(8,128)(2,1)S(1)} %collective-permute-done.1.refs_1_), channel_id=1, source_target_pairs={{0,24},{1,25},{2,26},{3,27},{4,28},{5,29},{6,30},{7,31},{8,16},{9,... | collective-permute-start | bytes 3145736 | tf_op jit(solution)/shard_map/ppermute | solution.py:41
  41.2 0.0 collective-permute-done.refs_0_
  41.2 1.4 %collective-permute-start.4 = (bf16[256,2048]{1,0:T(8,128)(2,1)}, bf16[256,2048]{1,0:T(8,128)(2,1)S(1)}, u32[]{:S(2)}, u32[]{:S(2)}) collective-permute-start(bf16[256,2048]{1,0:T(8,128)(2,1)} %collective-permute-done.refs_0_), channel_id=1, source_target_pairs={{0,96},{1,97},{2,98},{3,99},{4,100},{5,101},{6,102},{7,103},{8,104... | collective-permute-start | bytes 3145736 | tf_op jit(solution)/shard_map/ppermute | solution.py:41
  42.6 0.1 collective-permute-start.5
  42.6 1.9 %collective-permute-start.8 = (bf16[256,2048]{1,0:T(8,128)(2,1)}, bf16[256,2048]{1,0:T(8,128)(2,1)}, u32[]{:S(2)}, u32[]{:S(2)}) collective-permute-start(bf16[256,2048]{1,0:T(8,128)(2,1)} %collective-permute-done.refs_0_), channel_id=1, source_target_pairs={{0,1},{1,0},{2,3},{3,2},{4,5},{5,4},{6,7},{7,6},{8,9},{9,8},{10,11... | collective-permute-start | bytes 3145736 | tf_op jit(solution)/shard_map/ppermute | solution.py:41
  44.5 0.0 collective-permute-done.2.refs_2_
  44.5 0.0 collective-permute-start.9
  44.5 19.5 %collective-permute-done.3.refs_3_ = bf16[256,2048]{1,0:T(8,128)(2,1)S(1)} collective-permute-done((bf16[256,2048]{1,0:T(8,128)(2,1)S(1)}, bf16[256,2048]{1,0:T(8,128)(2,1)S(1)}, u32[]{:S(2)}, u32[]{:S(2)}) %collective-permute-start.3) | collective-permute-done | bytes 1048608 | tf_op jit(solution)/shard_map/ppermute | solution.py:41
  64.0 1.6 %collective-permute-start.10 = (bf16[256,2048]{1,0:T(8,128)(2,1)}, bf16[256,2048]{1,0:T(8,128)(2,1)}, u32[]{:S(2)}, u32[]{:S(2)}) collective-permute-start(bf16[256,2048]{1,0:T(8,128)(2,1)} %collective-permute-done.2.refs_2_), channel_id=1, source_target_pairs={{0,1},{1,0},{2,3},{3,2},{4,5},{5,4},{6,7},{7,6},{8,9},{9,8},{10,11... | collective-permute-start | bytes 3145736 | tf_op jit(solution)/shard_map/ppermute | solution.py:41
  65.5 0.8 slice.13
  66.4 0.0 collective-permute-done.4.refs_4_
  66.4 0.0 collective-permute-start.6
  66.4 0.9 slice.14
  67.3 0.0 all-to-all-done.x_ref
  67.3 1.5 %fusion = s32[16,2]{1,0:T(8,128)S(1)} fusion(bf16[16,2,400,128]{3,2,1,0:T(8,128)(2,1)} %all-to-all-done.x_ref), kind=kLoop, calls=%fused_computation.1 | loop fusion | flops 32 | bytes 192 | tf_op jit(solution)/shard_map/convert_element_type | solution.py:279
  68.8 0.7 reshape.2.pos_ref
  69.5 0.0 collective-permute-done.5.refs_5_
  69.5 2.6 %collective-permute-start.7 = (bf16[128,2048]{1,0:T(8,128)(2,1)}, bf16[128,2048]{1,0:T(8,128)(2,1)}, u32[]{:S(2)}, u32[]{:S(2)}) collective-permute-start(bf16[128,2048]{1,0:T(8,128)(2,1)} %slice.14), channel_id=1, source_target_pairs={{0,96},{1,97},{2,98},{3,99},{4,100},{5,101},{6,102},{7,103},{8,104... | collective-permute-start | bytes 1572872 | tf_op jit(solution)/shard_map/ppermute | solution.py:41
  72.1 0.0 collective-permute-done.8.refs_8_
  72.1 1.1 collective-permute-start.11
  73.2 0.0 collective-permute-done.9.refs_9_
  73.2 0.1 collective-permute-start.12
  73.3 0.0 collective-permute-done.10.refs_10_
  73.3 0.4 collective-permute-start.13
  73.8 23.9 %attention.1 = bf16[16,2,128,128]{3,2,1,0:T(8,128)(2,1)} custom-call(s32[32]{0:T(128)} %reshape.2.pos_ref, bf16[16,2,400,128]{3,2,1,0:T(8,128)(2,1)} %all-to-all-done.x_ref), custom_call_target="tpu_custom_call" | custom-call | flops 4294967296 | bytes 4194304 | tf_op jit(solution)/shard_map/attention/pallas_call | solution.py:177
  97.7 0.0 copy-done.4
  97.7 4.4 %all-to-all-start.1 = ((bf16[16,2,128,128]{3,2,1,0:T(8,128)(2,1)}), bf16[16,2,128,128]{3,2,1,0:T(8,128)(2,1)S(1)}, u32[]{:S(2)}, u32[]{:S(2)}) async-start(bf16[16,2,128,128]{3,2,1,0:T(8,128)(2,1)} %attention.1), calls=%async_computation.1 | async-start | bytes 2097152 | tf_op jit(solution)/shard_map/all_to_all | solution.py:281
  102.1 0.0 collective-permute-done.6.refs_6_
  102.1 0.2 collective-permute-start.14
  102.3 0.0 collective-permute-done.7.refs_7_
  102.3 0.4 collective-permute-start.15
  102.7 0.6 stack.39.place
  103.3 0.0 collective-permute-done.11.refs_11_
  103.3 0.0 collective-permute-done.12.refs_12_
  103.3 0.0 collective-permute-done.13.refs_13_
  103.3 1.1 collective-permute-done.14.refs_14_
  104.4 0.7 collective-permute-done.15.refs_15_
  105.2 12.7 %all-to-all-done.1.att_ref = bf16[16,2,128,128]{3,2,1,0:T(8,128)(2,1)S(1)} async-done(((bf16[16,2,128,128]{3,2,1,0:T(8,128)(2,1)}), bf16[16,2,128,128]{3,2,1,0:T(8,128)(2,1)S(1)}, u32[]{:S(2)}, u32[]{:S(2)}) %all-to-all-start.1) | async-done | bytes 1048608 | tf_op jit(solution)/shard_map/all_to_all | solution.py:281
  117.9 1.0 copy-done.1
  118.9 13.4 %project.1 = bf16[256,4096]{1,0:T(8,128)(2,1)} custom-call(s32[9]{0:T(128)} %stack.39.place, bf16[16,2,128,128]{3,2,1,0:T(8,128)(2,1)} %copy-done.1, bf16[256,4096]{1,0:T(8,128)(2,1)} %bitcast.14, bf16[256,4096]{1,0:T(8,128)(2,1)} %own_ref.1, bf16[256,2048]{1,0:T(8,128)(2,1)} %collective-permute-done.refs_0_, bf16[256,2048]{1,0:T(8,128)(2,1)} %copy-done.4, ...), custom_call_target="tpu_custom_call" | custom-call | flops 4294967296 | bytes 20971520 | tf_op jit(solution)/shard_map/project/pallas_call | solution.py:237
  (7 shorter events, 0.0 us)
Async XLA Ops:
  4.6 7.9 %copy-start = (bf16[256,4096]{1,0:T(8,128)(2,1)S(1)}, bf16[256,4096]{1,0:T(8,128)(2,1)}, u32[]{:S(2)}) copy-start(bf16[256,4096]{1,0:T(8,128)(2,1)} %own_ref.1) | copy-start | bytes 6291460
  4.6 62.7 %all-to-all-start = ((bf16[16,2,400,128]{3,2,1,0:T(8,128)(2,1)}), bf16[16,2,400,128]{3,2,1,0:T(8,128)(2,1)}, u32[]{:S(2)}, u32[]{:S(2)}) async-start(bf16[16,2,400,128]{3,2,1,0:T(8,128)(2,1)} %pack.1), calls=%async_computation | async-start | bytes 6553600 | tf_op jit(solution)/shard_map/all_to_all | solution.py:264
  12.6 26.1 %collective-permute-start.1 = (bf16[256,2048]{1,0:T(8,128)(2,1)S(1)}, bf16[256,2048]{1,0:T(8,128)(2,1)S(1)}, u32[]{:S(2)}, u32[]{:S(2)}) collective-permute-start(bf16[256,2048]{1,0:T(8,128)(2,1)S(1)} %constant_dynamic-slice_fusion), channel_id=1, source_target_pairs={{0,32},{1,33},{2,34},{3,35},{4,36},{5,37},{6,38},{7,39},{8,40},{9,... | collective-permute-start | bytes 3145736 | tf_op jit(solution)/shard_map/ppermute | solution.py:41
  14.0 27.2 %collective-permute-start = (bf16[256,2048]{1,0:T(8,128)(2,1)S(1)}, bf16[256,2048]{1,0:T(8,128)(2,1)}, u32[]{:S(2)}, u32[]{:S(2)}) collective-permute-start(bf16[256,2048]{1,0:T(8,128)(2,1)S(1)} %constant_dynamic-slice_fusion), channel_id=1, source_target_pairs={{0,24},{1,25},{2,26},{3,27},{4,28},{5,29},{6,30},{7,31},{8,16},{9,... | collective-permute-start | bytes 3145736 | tf_op jit(solution)/shard_map/ppermute | solution.py:41
  16.6 27.9 %collective-permute-start.2 = (bf16[256,2048]{1,0:T(8,128)(2,1)S(1)}, bf16[256,2048]{1,0:T(8,128)(2,1)}, u32[]{:S(2)}, u32[]{:S(2)}) collective-permute-start(bf16[256,2048]{1,0:T(8,128)(2,1)S(1)} %constant_dynamic-slice_fusion), channel_id=1, source_target_pairs={{0,96},{1,97},{2,98},{3,99},{4,100},{5,101},{6,102},{7,103},{8,104... | collective-permute-start | bytes 3145736 | tf_op jit(solution)/shard_map/ppermute | solution.py:41
  38.8 58.9 %copy-start.4 = (bf16[256,2048]{1,0:T(8,128)(2,1)}, bf16[256,2048]{1,0:T(8,128)(2,1)S(1)}, u32[]{:S(2)}) copy-start(bf16[256,2048]{1,0:T(8,128)(2,1)S(1)} %collective-permute-done.1.refs_1_) | copy-start | bytes 3145732
  38.8 25.2 %collective-permute-start.3 = (bf16[256,2048]{1,0:T(8,128)(2,1)S(1)}, bf16[256,2048]{1,0:T(8,128)(2,1)S(1)}, u32[]{:S(2)}, u32[]{:S(2)}) collective-permute-start(bf16[256,2048]{1,0:T(8,128)(2,1)S(1)} %collective-permute-done.1.refs_1_), channel_id=1, source_target_pairs={{0,24},{1,25},{2,26},{3,27},{4,28},{5,29},{6,30},{7,31},{8,16},{9,... | collective-permute-start | bytes 3145736 | tf_op jit(solution)/shard_map/ppermute | solution.py:41
  41.2 25.2 %collective-permute-start.4 = (bf16[256,2048]{1,0:T(8,128)(2,1)}, bf16[256,2048]{1,0:T(8,128)(2,1)S(1)}, u32[]{:S(2)}, u32[]{:S(2)}) collective-permute-start(bf16[256,2048]{1,0:T(8,128)(2,1)} %collective-permute-done.refs_0_), channel_id=1, source_target_pairs={{0,96},{1,97},{2,98},{3,99},{4,100},{5,101},{6,102},{7,103},{8,104... | collective-permute-start | bytes 3145736 | tf_op jit(solution)/shard_map/ppermute | solution.py:41
  42.6 26.9 %collective-permute-start.5 = (bf16[256,2048]{1,0:T(8,128)(2,1)S(1)}, bf16[256,2048]{1,0:T(8,128)(2,1)}, u32[]{:S(2)}, u32[]{:S(2)}) collective-permute-start(bf16[256,2048]{1,0:T(8,128)(2,1)S(1)} %collective-permute-done.1.refs_1_), channel_id=1, source_target_pairs={{0,32},{1,33},{2,34},{3,35},{4,36},{5,37},{6,38},{7,39},{8,40},{9,... | collective-permute-start | bytes 3145736 | tf_op jit(solution)/shard_map/ppermute | solution.py:41
  42.6 29.5 %collective-permute-start.8 = (bf16[256,2048]{1,0:T(8,128)(2,1)}, bf16[256,2048]{1,0:T(8,128)(2,1)}, u32[]{:S(2)}, u32[]{:S(2)}) collective-permute-start(bf16[256,2048]{1,0:T(8,128)(2,1)} %collective-permute-done.refs_0_), channel_id=1, source_target_pairs={{0,1},{1,0},{2,3},{3,2},{4,5},{5,4},{6,7},{7,6},{8,9},{9,8},{10,11... | collective-permute-start | bytes 3145736 | tf_op jit(solution)/shard_map/ppermute | solution.py:41
  44.5 28.7 %collective-permute-start.9 = (bf16[256,2048]{1,0:T(8,128)(2,1)S(1)}, bf16[256,2048]{1,0:T(8,128)(2,1)}, u32[]{:S(2)}, u32[]{:S(2)}) collective-permute-start(bf16[256,2048]{1,0:T(8,128)(2,1)S(1)} %collective-permute-done.1.refs_1_), channel_id=1, source_target_pairs={{0,1},{1,0},{2,3},{3,2},{4,5},{5,4},{6,7},{7,6},{8,9},{9,8},{10,11... | collective-permute-start | bytes 3145736 | tf_op jit(solution)/shard_map/ppermute | solution.py:41
  64.0 33.7 %copy-start.2 = (bf16[256,2048]{1,0:T(8,128)(2,1)}, bf16[256,2048]{1,0:T(8,128)(2,1)S(1)}, u32[]{:S(2)}) copy-start(bf16[256,2048]{1,0:T(8,128)(2,1)S(1)} %collective-permute-done.3.refs_3_) | copy-start | bytes 3145732
  64.0 9.3 %collective-permute-start.10 = (bf16[256,2048]{1,0:T(8,128)(2,1)}, bf16[256,2048]{1,0:T(8,128)(2,1)}, u32[]{:S(2)}, u32[]{:S(2)}) collective-permute-start(bf16[256,2048]{1,0:T(8,128)(2,1)} %collective-permute-done.2.refs_2_), channel_id=1, source_target_pairs={{0,1},{1,0},{2,3},{3,2},{4,5},{5,4},{6,7},{7,6},{8,9},{9,8},{10,11... | collective-permute-start | bytes 3145736 | tf_op jit(solution)/shard_map/ppermute | solution.py:41
  66.4 31.3 %copy-start.3 = (bf16[256,2048]{1,0:T(8,128)(2,1)}, bf16[256,2048]{1,0:T(8,128)(2,1)S(1)}, u32[]{:S(2)}) copy-start(bf16[256,2048]{1,0:T(8,128)(2,1)S(1)} %collective-permute-done.4.refs_4_) | copy-start | bytes 3145732
  66.4 35.7 %collective-permute-start.6 = (bf16[128,2048]{1,0:T(8,128)(2,1)}, bf16[128,2048]{1,0:T(8,128)(2,1)}, u32[]{:S(2)}, u32[]{:S(2)}) collective-permute-start(bf16[128,2048]{1,0:T(8,128)(2,1)} %slice.13), channel_id=1, source_target_pairs={{0,32},{1,33},{2,34},{3,35},{4,36},{5,37},{6,38},{7,39},{8,40},{9,... | collective-permute-start | bytes 1572872 | tf_op jit(solution)/shard_map/ppermute | solution.py:41
  69.5 32.8 %collective-permute-start.7 = (bf16[128,2048]{1,0:T(8,128)(2,1)}, bf16[128,2048]{1,0:T(8,128)(2,1)}, u32[]{:S(2)}, u32[]{:S(2)}) collective-permute-start(bf16[128,2048]{1,0:T(8,128)(2,1)} %slice.14), channel_id=1, source_target_pairs={{0,96},{1,97},{2,98},{3,99},{4,100},{5,101},{6,102},{7,103},{8,104... | collective-permute-start | bytes 1572872 | tf_op jit(solution)/shard_map/ppermute | solution.py:41
  72.1 31.2 %collective-permute-start.11 = (bf16[256,2048]{1,0:T(8,128)(2,1)S(1)}, bf16[256,2048]{1,0:T(8,128)(2,1)}, u32[]{:S(2)}, u32[]{:S(2)}) collective-permute-start(bf16[256,2048]{1,0:T(8,128)(2,1)S(1)} %collective-permute-done.3.refs_3_), channel_id=1, source_target_pairs={{0,1},{1,0},{2,3},{3,2},{4,5},{5,4},{6,7},{7,6},{8,9},{9,8},{10,11... | collective-permute-start | bytes 3145736 | tf_op jit(solution)/shard_map/ppermute | solution.py:41
  73.2 30.1 %collective-permute-start.12 = (bf16[256,2048]{1,0:T(8,128)(2,1)S(1)}, bf16[256,2048]{1,0:T(8,128)(2,1)}, u32[]{:S(2)}, u32[]{:S(2)}) collective-permute-start(bf16[256,2048]{1,0:T(8,128)(2,1)S(1)} %collective-permute-done.4.refs_4_), channel_id=1, source_target_pairs={{0,1},{1,0},{2,3},{3,2},{4,5},{5,4},{6,7},{7,6},{8,9},{9,8},{10,11... | collective-permute-start | bytes 3145736 | tf_op jit(solution)/shard_map/ppermute | solution.py:41
  73.3 30.0 %collective-permute-start.13 = (bf16[256,2048]{1,0:T(8,128)(2,1)}, bf16[256,2048]{1,0:T(8,128)(2,1)}, u32[]{:S(2)}, u32[]{:S(2)}) collective-permute-start(bf16[256,2048]{1,0:T(8,128)(2,1)} %collective-permute-done.5.refs_5_), channel_id=1, source_target_pairs={{0,1},{1,0},{2,3},{3,2},{4,5},{5,4},{6,7},{7,6},{8,9},{9,8},{10,11... | collective-permute-start | bytes 3145736 | tf_op jit(solution)/shard_map/ppermute | solution.py:41
  97.7 20.2 %all-to-all-start.1 = ((bf16[16,2,128,128]{3,2,1,0:T(8,128)(2,1)}), bf16[16,2,128,128]{3,2,1,0:T(8,128)(2,1)S(1)}, u32[]{:S(2)}, u32[]{:S(2)}) async-start(bf16[16,2,128,128]{3,2,1,0:T(8,128)(2,1)} %attention.1), calls=%async_computation.1 | async-start | bytes 2097152 | tf_op jit(solution)/shard_map/all_to_all | solution.py:281
  102.1 2.3 %collective-permute-start.14 = (bf16[128,2048]{1,0:T(8,128)(2,1)}, bf16[128,2048]{1,0:T(8,128)(2,1)}, u32[]{:S(2)}, u32[]{:S(2)}) collective-permute-start(bf16[128,2048]{1,0:T(8,128)(2,1)} %collective-permute-done.6.refs_6_), channel_id=1, source_target_pairs={{0,1},{1,0},{2,3},{3,2},{4,5},{5,4},{6,7},{7,6},{8,9},{9,8},{10,11... | collective-permute-start | bytes 1572872 | tf_op jit(solution)/shard_map/ppermute | solution.py:41
  102.3 2.9 %collective-permute-start.15 = (bf16[128,2048]{1,0:T(8,128)(2,1)}, bf16[128,2048]{1,0:T(8,128)(2,1)}, u32[]{:S(2)}, u32[]{:S(2)}) collective-permute-start(bf16[128,2048]{1,0:T(8,128)(2,1)} %collective-permute-done.7.refs_7_), channel_id=1, source_target_pairs={{0,1},{1,0},{2,3},{3,2},{4,5},{5,4},{6,7},{7,6},{8,9},{9,8},{10,11... | collective-permute-start | bytes 1572872 | tf_op jit(solution)/shard_map/ppermute | solution.py:41
  117.9 1.0 copy-start.1

commit v2 on v1

v2 whole, which is shorter than its diff:
```python
import functools
import itertools
import math

import jax
import jax.numpy as jnp
import numpy as np
from jax import lax
from jax.experimental import pallas as pl
from jax.experimental.pallas import tpu as pltpu
from jax.sharding import Mesh
from jax.sharding import PartitionSpec as P

HEADS = 16
HEAD_DIM = 128
LEN = 4096
HALF = 128
WIDTH = HEADS * HEAD_DIM
D = 4096
ROWS = 3 * HALF + 16
AXES = ("y", "xh", "xl", "z", "c")
SIZES = (4, 2, 2, 4, 2)
FSDP = ("y", "xh")
SEQ = ("xl", "z", "c")
VMEM = 56 * 2**20


def tables():
    frequency = 10000.0 ** (-np.arange(HEAD_DIM // 2) / (HEAD_DIM // 2))
    angles = np.arange(LEN)[:, None] * frequency[None, :]
    cosine, sine = np.cos(angles), np.sin(angles)
    return (
        np.concatenate([cosine, cosine], axis=1).astype(np.float32),
        np.concatenate([-sine, sine], axis=1).astype(np.float32),
    )


def send(array, move):
    places = list(itertools.product(*map(range, SIZES)))
    index = {place: i for i, place in enumerate(places)}
    return lax.ppermute(array, AXES, [(index[p], index[move(*p)]) for p in places])


def y_up(y, xh, xl, z, c):
    return ((y + 1) % 4, xh, xl, z, c)


def y_down(y, xh, xl, z, c):
    return ((y + 3) % 4, xh, xl, z, c)


def x_over(y, xh, xl, z, c):
    return (y, 1 - xh, 1 - xl, z, c)


def core_over(y, xh, xl, z, c):
    return (y, xh, xl, z, 1 - c)


def pack_kernel(starts, q_ref, k_ref, v_ref, cos_ref, sin_ref, out_ref):
    cosine, sine = cos_ref[...], sin_ref[...]
    factor = math.log2(math.e) / math.sqrt(HEAD_DIM)

    def turn(block, cosine, sine):
        block = block.astype(jnp.float32)
        turned = block * cosine + pltpu.roll(block, HEAD_DIM // 2, 1) * sine
        return turned.astype(jnp.bfloat16)

    for h in range(HEADS):
        lanes = slice(h * HEAD_DIM, (h + 1) * HEAD_DIM)
        out_ref[h, 0, 0:HALF] = turn(q_ref[:, lanes], cosine * factor, sine * factor)
        out_ref[h, 0, HALF : 2 * HALF] = turn(k_ref[:, lanes], cosine, sine)
        out_ref[h, 0, 2 * HALF : 3 * HALF] = v_ref[:, lanes]
    block = jnp.full((16, HEAD_DIM), starts[pl.program_id(0)] // HALF, jnp.int32)
    block = block.astype(jnp.float32).astype(jnp.bfloat16)
    for h in range(HEADS):
        out_ref[h, 0, 3 * HALF :] = block


def pack(starts, queries, keys, values):
    cosine, sine = tables()
    rows = pl.BlockSpec((HALF, WIDTH), lambda b, s: (b, 0))
    table = pl.BlockSpec((HALF, HEAD_DIM), lambda b, s: (s[b] // HALF, 0))
    return pl.pallas_call(
        pack_kernel,
        grid_spec=pltpu.PrefetchScalarGridSpec(
            num_scalar_prefetch=1,
            grid=(2,),
            in_specs=[rows, rows, rows, table, table],
            out_specs=pl.BlockSpec((HEADS, 1, ROWS, HEAD_DIM), lambda b, s: (0, b, 0, 0)),
        ),
        out_shape=jax.ShapeDtypeStruct((HEADS, 2, ROWS, HEAD_DIM), jnp.bfloat16),
        compiler_params=pltpu.CompilerParams(vmem_limit_bytes=VMEM),
        name="pack",
    )(starts, queries, keys, values, jnp.asarray(cosine), jnp.asarray(sine))


def attention_kernel(x_ref, o_ref, qs, kt, vs, scores, index, pos, moved, *, tq, width):
    tiles = LEN // tq
    for t in range(2 * HEADS):
        row = x_ref[t // 2, t % 2, 3 * HALF :, :].astype(jnp.float32)
        index[t : t + 1, :] = row[:1].astype(jnp.int32)
    copy = pltpu.make_async_copy(index, pos, moved)
    copy.start()
    copy.wait()
    vs[:, HEAD_DIM:] = jnp.ones((LEN, HEAD_DIM), jnp.bfloat16)

    def place(t, carry):
        at = pl.ds(pl.multiple_of(pos[t, 0] * HALF, HALF), HALF)
        s, b = t // 2, t % 2
        qs[at, :] = x_ref[s, b, 0:HALF, :]
        kt[:, at] = x_ref[s, b, HALF : 2 * HALF, :].T
        vs[at, :HEAD_DIM] = x_ref[s, b, 2 * HALF : 3 * HALF, :]
        return carry

    lax.fori_loop(0, 2 * HEADS, place, 0, unroll=4)

    row = lax.broadcasted_iota(jnp.int32, (tq, tq), 0)
    col = lax.broadcasted_iota(jnp.int32, (tq, tq), 1)

    def chunks(i):
        seen = (i + 1) * tq
        return [(o, min(width, seen - o)) for o in range(0, seen, width)]

    def score(i, first, count, high):
        s = jnp.dot(
            qs[i * tq : (i + 1) * tq, :],
            kt[:, first : first + count],
            preferred_element_type=jnp.float32,
        )
        if first + count > i * tq:
            before = i * tq - first
            last = jnp.where(col <= row, s[:, before:], -1e30)
            s = jnp.concatenate([s[:, :before], last], axis=1) if before else last
        scores[i % 2, :, first : first + count] = s
        for c in range(0, count, 128):
            part = s[:, c : c + 128]
            high = part if high is None else jnp.maximum(high, part)
        return high

    def weigh(i, first, count, high, total):
        p = jnp.concatenate(
            [
                jnp.exp2(scores[i % 2, :, c : c + 128] - high).astype(jnp.bfloat16)
                for c in range(first, first + count, 128)
            ],
            axis=1,
        )
        part = jnp.dot(p, vs[first : first + count, :], preferred_element_type=jnp.float32)
        return part if total is None else total + part

    high = None
    for chunk in chunks(0):
        high = score(0, *chunk, high)
    for i in range(tiles):
        m = jnp.broadcast_to(jnp.max(high, axis=1, keepdims=True), (tq, 128))
        high = total = None
        mine, following = chunks(i), chunks(i + 1) if i + 1 < tiles else []
        for t in range(max(len(mine), len(following))):
            if t < len(following):
                high = score(i + 1, *following[t], high)
            if t < len(mine):
                total = weigh(i, *mine[t], m, total)
        qs[i * tq : (i + 1) * tq, :] = (total[:, :HEAD_DIM] / total[:, HEAD_DIM:]).astype(
            jnp.bfloat16
        )

    def unplace(t, carry):
        at = pl.ds(pl.multiple_of(pos[t, 0] * HALF, HALF), HALF)
        o_ref[t // 2, t % 2] = qs[at, :]
        return carry

    lax.fori_loop(0, 2 * HEADS, unplace, 0, unroll=4)


def attention(packed, tq=256, width=1024):
    return pl.pallas_call(
        functools.partial(attention_kernel, tq=tq, width=width),
        out_shape=jax.ShapeDtypeStruct((HEADS, 2, HALF, HEAD_DIM), jnp.bfloat16),
        in_specs=[
            pl.BlockSpec(memory_space=pltpu.VMEM),
        ],
        out_specs=pl.BlockSpec(memory_space=pltpu.VMEM),
        scratch_shapes=[
            pltpu.VMEM((LEN, HEAD_DIM), jnp.bfloat16),
            pltpu.VMEM((HEAD_DIM, LEN), jnp.bfloat16),
            pltpu.VMEM((LEN, 2 * HEAD_DIM), jnp.bfloat16),
            pltpu.VMEM((2, tq, LEN), jnp.float32),
            pltpu.VMEM((2 * HEADS, 128), jnp.int32),
            pltpu.SMEM((2 * HEADS, 128), jnp.int32),
            pltpu.SemaphoreType.DMA,
        ],
        compiler_params=pltpu.CompilerParams(vmem_limit_bytes=VMEM),
        cost_estimate=pl.CostEstimate(
            flops=8 * LEN * LEN * HEAD_DIM, bytes_accessed=4 * 2**20, transcendentals=LEN * LEN // 2
        ),
        name="attention",
    )(packed)


PIECES = ((0, 0), (0, 1), (3, 0), (1, 0), (3, 1), (1, 1), (2, 0), (2, 1))
STEP = 512
HALF_D = D // 2
GROUP = WIDTH // 2


def project_kernel(place, att_ref, hidden_ref, own_ref, *refs):
    halves = refs[:8], refs[8:16]
    out_ref, heads, left, rows, hidden, acc, out, att_sem, hidden_sem, in_sem, out_sem = refs[16:]

    def first_column(half):
        core = place[0] if half == 0 else 1 - place[0]
        return core * HALF_D

    def fetches(half):
        first, copies = 0, []
        at = pl.ds(pl.multiple_of(first_column(half), HALF_D), HALF_D)
        for n, ref in enumerate([own_ref.at[:, at], *halves[half]]):
            count = ref.shape[0]
            to = rows.at[half, first : first + count]
            copies.append((first, pltpu.make_async_copy(ref, to, in_sem.at[half, n])))
            first += count
        return copies

    att = pltpu.make_async_copy(att_ref, heads, att_sem)
    residual = pltpu.make_async_copy(hidden_ref, hidden, hidden_sem)
    pieces = [fetches(half) for half in range(2)]
    att.start()
    for first, copy in pieces[0]:
        if first == GROUP:
            residual.start()
        copy.start()
    for _, copy in pieces[1]:
        copy.start()
    att.wait()
    for n in range(len(PIECES)):
        for i in range(2):
            head = heads[2 * place[1 + n] + i].reshape(2 * HALF, HEAD_DIM)
            left[:, (2 * n + i) * HEAD_DIM : (2 * n + i + 1) * HEAD_DIM] = head
    stores = []
    for half in range(2):
        for group in range(0, WIDTH, GROUP):
            for first, copy in pieces[half]:
                if group <= first < group + GROUP:
                    copy.wait()
            if half == 0 and group > 0:
                residual.wait()
            for t in range(HALF_D // STEP):
                at = pl.ds(t * STEP, STEP)
                part = jnp.dot(
                    left[:, group : group + GROUP],
                    rows[half, group : group + GROUP, at],
                    preferred_element_type=jnp.float32,
                )
                if group == 0:
                    acc[:, at] = part
                else:
                    to = pl.ds(pl.multiple_of(first_column(half) + t * STEP, STEP), STEP)
                    total = hidden[:, to].astype(jnp.float32) + (acc[:, at] + part)
                    n = half * (HALF_D // STEP) + t
                    out[n] = total.astype(jnp.bfloat16)
                    stores.append(
                        pltpu.make_async_copy(out.at[n], out_ref.at[:, to], out_sem.at[n])
                    )
                    stores[-1].start()
    for copy in stores:
        copy.wait()


def project(place, att, hidden, own, mine, other):
    return pl.pallas_call(
        project_kernel,
        in_specs=[pl.BlockSpec(memory_space=pltpu.SMEM)]
        + [pl.BlockSpec(memory_space=pl.ANY)] * 19,
        out_specs=pl.BlockSpec(memory_space=pl.ANY),
        scratch_shapes=[
            pltpu.VMEM((HEADS, 2, HALF, HEAD_DIM), jnp.bfloat16),
            pltpu.VMEM((2 * HALF, WIDTH), jnp.bfloat16),
            pltpu.VMEM((2, WIDTH, HALF_D), jnp.bfloat16),
            pltpu.VMEM((2 * HALF, D), jnp.bfloat16),
            pltpu.VMEM((2 * HALF, HALF_D), jnp.float32),
            pltpu.VMEM((D // STEP, 2 * HALF, STEP), jnp.bfloat16),
            pltpu.SemaphoreType.DMA,
            pltpu.SemaphoreType.DMA,
            pltpu.SemaphoreType.DMA((2, 9)),
            pltpu.SemaphoreType.DMA((D // STEP,)),
        ],
        out_shape=jax.ShapeDtypeStruct((2 * HALF, D), jnp.bfloat16),
        compiler_params=pltpu.CompilerParams(vmem_limit_bytes=VMEM),
        cost_estimate=pl.CostEstimate(
            flops=4 * HALF * WIDTH * D, bytes_accessed=20 * 2**20, transcendentals=0
        ),
        name="project",
    )(place, att, hidden, own, *mine, *other)


def arrive_kernel(att_ref, out_ref):
    del att_ref, out_ref


def arrive(att):
    return pl.pallas_call(
        arrive_kernel,
        in_specs=[pl.BlockSpec(memory_space=pl.ANY)],
        out_specs=pl.BlockSpec(memory_space=pl.ANY),
        out_shape=jax.ShapeDtypeStruct(att.shape, att.dtype),
        input_output_aliases={0: 0},
        compiler_params=pltpu.CompilerParams(vmem_limit_bytes=VMEM),
        cost_estimate=pl.CostEstimate(
            flops=2 * 10**10, bytes_accessed=2 * 2**20, transcendentals=0
        ),
        name="arrive",
    )(att)


def shards(hidden_in, queries, keys, values, block_start, out_weight):
    y, xh, c = lax.axis_index("y"), lax.axis_index("xh"), lax.axis_index("c")
    packed = pack(block_start, queries[0], keys[0], values[0])
    packed = lax.all_to_all(packed, SEQ, 0, 0, tiled=True)

    half = lax.dynamic_slice(out_weight, (0, c * (D // 2)), (WIDTH // 8, D // 2))
    mine, other = {}, {}
    mine[0, 1] = send(half, x_over)
    mine[3, 0] = send(half, y_up)
    mine[1, 0] = send(half, y_down)
    second = {
        (3, 1): send(mine[3, 0], x_over),
        (1, 1): send(mine[0, 1], y_down),
        (2, 0): send(mine[3, 0], y_up),
    }
    other[0, 1] = send(mine[0, 1], core_over)
    other[3, 0] = send(mine[3, 0], core_over)
    later, _ = lax.optimization_barrier((mine[1, 0], other[3, 0]))
    other[1, 0] = send(later, core_over)

    attended = attention(packed)
    second, _ = lax.optimization_barrier((second, attended))
    attended = lax.all_to_all(attended, SEQ, 0, 0, tiled=True)
    top = send(second[3, 1][:HALF], y_up)
    bottom = send(second[1, 1][HALF:], y_down)
    last = [second[at] for at in PIECES[4:7]] + [top, bottom]
    mine = [mine[at] for at in PIECES[1:4]] + last
    other = [other[at] for at in PIECES[1:4]] + [send(a, core_over) for a in last]

    owners = [((y + dy) % 4) * 2 + (xh + dx) % 2 for dy, dx in PIECES]
    place = jnp.stack([c, *owners]).astype(jnp.int32)
    attended = arrive(attended)
    return project(place, attended, hidden_in[0], out_weight, mine, other)[None]


def solution(mesh):
    fine = Mesh(mesh.devices.reshape(SIZES), AXES)
    return jax.shard_map(
        shards,
        mesh=fine,
        in_specs=(
            P(FSDP, SEQ, None),
            P(FSDP, SEQ, None),
            P(FSDP, SEQ, None),
            P(FSDP, SEQ, None),
            P(SEQ),
            P(FSDP, None),
        ),
        out_specs=P(FSDP, SEQ, None),
        check_vma=False,
    )
```

time: 133 us -> 116 us (0.87)
  waiting for transfers between devices: 54.7 us -> 42.7 us
  Pallas kernels: 41.9 us -> 32.8 us
  starting transfers between devices: 30 us -> 36.7 us
  other arithmetic: 1.49 us -> 0 us
    all_to_all x1, waiting for transfers between devices: 12.7 us -> 0.01 us  [shards(): attended = lax.all_to_all(attended, SEQ, 0, 0, tiled=True)]
    pallas_call x2 -> x3, Pallas kernels: 37.3 us -> 28.1 us  [the longest x1 15.5 us: attention(): pl.pallas_call(functools.partial(attention_kernel, tq=tq, width=width), o...]
    all_to_all x1, waiting for transfers between devices: 0.01 us -> 8.87 us  [shards(): packed = lax.all_to_all(packed, SEQ, 0, 0, tiled=True)]
    ppermute x16, waiting for transfers between devices: 41.9 us -> 33.8 us  [send(): lax.ppermute(array, AXES, [(index[p], index[move(*p)]) for p in places])]
    all_to_all x1, starting transfers between devices: 4.4 us -> 10.4 us  [shards(): attended = lax.all_to_all(attended, SEQ, 0, 0, tiled=True)]
    convert_element_type x1 -> x0, other arithmetic: 1.49 us -> none  [shards(): pos = packed[:, :, 3 * HALF, 0].reshape(2 * HEADS).astype(jnp.int32)]
  transfers between devices with their start and end apart: 18 -> 18, of which waited for: 5 -> 5; matrix products, arithmetic and copies ran while one was open for 4% -> 2% of each run, Pallas kernels for 18% -> 13%
where the time goes in v2:
time: 116 us
  waiting for transfers between devices  42.7 us (37%)
  starting transfers between devices  36.7 us (32%)
  Pallas kernels  32.8 us (28%)
  local copies, waits for them, and re-layouts  3.49 us (3%)
    ppermute x16, waiting for transfers between devices, send(): lax.ppermute(array, AXES, [(index[p], index[move(*p)]) for p in places])  33.8 us
    ppermute x16, starting transfers between devices, send(): lax.ppermute(array, AXES, [(index[p], index[move(*p)]) for p in places])  18.4 us
    pallas_call x1, Pallas kernels, attention(): pl.pallas_call(functools.partial(attention_kernel, tq=tq, width=width), o...  15.5 us
    pallas_call x1, Pallas kernels, project(): pl.pallas_call(project_kernel, in_specs=[pl.BlockSpec(memory_space=pltpu....  12.7 us
    all_to_all x1, starting transfers between devices, shards(): attended = lax.all_to_all(attended, SEQ, 0, 0, tiled=True)  10.4 us
    all_to_all x1, waiting for transfers between devices, shards(): packed = lax.all_to_all(packed, SEQ, 0, 0, tiled=True)  8.87 us
    all_to_all x1, starting transfers between devices, shards(): packed = lax.all_to_all(packed, SEQ, 0, 0, tiled=True)  7.89 us
    pallas_call x1, Pallas kernels, pack(): pl.pallas_call(pack_kernel, grid_spec=pltpu.PrefetchScalarGridSpec(num_sc...  4.61 us
  transfers between devices with their start and end apart: 18, of which 5 were waited for; matrix products, arithmetic and copies ran while one was open for 2% of the time, Pallas kernels for 13%

profile of v2, /device:TPU:1, one launch (start us, length us, event | category | flops | bytes accessed | tf_op | source)
XLA Modules:
  0.0 115.8 jit_solution(8556752202846113237)
XLA Ops:
  0.0 4.6 %pack.1 = bf16[16,2,400,128]{3,2,1,0:T(8,128)(2,1)} custom-call(s32[2]{0:T(128)} %starts.1, bf16[256,2048]{1,0:T(8,128)(2,1)} %bitcast.15, bf16[256,2048]{1,0:T(8,128)(2,1)} %bitcast.16, bf16[256,2048]{1,0:T(8,128)(2,1)} %bitcast.17, f32[4096,128]{1,0:T(8,128)} %constant.84.clone.cos_ref, f32[4096,128]{1,0:T(8,128)} %constant.85.clone.sin_ref), custom_call_target="tpu_custom_call" | custom-call | tf_op jit(solution)/shard_map/pack/pallas_call | solution.py:84
  4.6 7.9 %all-to-all-start = ((bf16[16,2,400,128]{3,2,1,0:T(8,128)(2,1)}), bf16[16,2,400,128]{3,2,1,0:T(8,128)(2,1)}, u32[]{:S(2)}, u32[]{:S(2)}) async-start(bf16[16,2,400,128]{3,2,1,0:T(8,128)(2,1)} %pack.1), calls=%async_computation | async-start | bytes 6553600 | tf_op jit(solution)/shard_map/all_to_all | solution.py:319
  12.5 0.0 copy-done
  12.5 0.1 constant_dynamic-slice_fusion
  12.6 1.4 %collective-permute-start.1 = (bf16[256,2048]{1,0:T(8,128)(2,1)S(1)}, bf16[256,2048]{1,0:T(8,128)(2,1)}, u32[]{:S(2)}, u32[]{:S(2)}) collective-permute-start(bf16[256,2048]{1,0:T(8,128)(2,1)S(1)} %constant_dynamic-slice_fusion), channel_id=1, source_target_pairs={{0,32},{1,33},{2,34},{3,35},{4,36},{5,37},{6,38},{7,39},{8,40},{9,... | collective-permute-start | bytes 3145736 | tf_op jit(solution)/shard_map/ppermute | solution.py:41
  14.0 2.7 %collective-permute-start = (bf16[256,2048]{1,0:T(8,128)(2,1)S(1)}, bf16[256,2048]{1,0:T(8,128)(2,1)}, u32[]{:S(2)}, u32[]{:S(2)}) collective-permute-start(bf16[256,2048]{1,0:T(8,128)(2,1)S(1)} %constant_dynamic-slice_fusion), channel_id=1, source_target_pairs={{0,24},{1,25},{2,26},{3,27},{4,28},{5,29},{6,30},{7,31},{8,16},{9,... | collective-permute-start | bytes 3145736 | tf_op jit(solution)/shard_map/ppermute | solution.py:41
  16.6 1.5 %collective-permute-start.2 = (bf16[256,2048]{1,0:T(8,128)(2,1)S(1)}, bf16[256,2048]{1,0:T(8,128)(2,1)}, u32[]{:S(2)}, u32[]{:S(2)}) collective-permute-start(bf16[256,2048]{1,0:T(8,128)(2,1)S(1)} %constant_dynamic-slice_fusion), channel_id=1, source_target_pairs={{0,96},{1,97},{2,98},{3,99},{4,100},{5,101},{6,102},{7,103},{8,104... | collective-permute-start | bytes 3145736 | tf_op jit(solution)/shard_map/ppermute | solution.py:41
  18.2 20.6 %collective-permute-done.1.refs_1_ = bf16[256,2048]{1,0:T(8,128)(2,1)} collective-permute-done((bf16[256,2048]{1,0:T(8,128)(2,1)S(1)}, bf16[256,2048]{1,0:T(8,128)(2,1)}, u32[]{:S(2)}, u32[]{:S(2)}) %collective-permute-start.1) | collective-permute-done | bytes 1048608 | tf_op jit(solution)/shard_map/ppermute | solution.py:41
  38.8 0.9 collective-permute-start.9
  39.7 2.7 %collective-permute-start.5 = (bf16[256,2048]{1,0:T(8,128)(2,1)}, bf16[256,2048]{1,0:T(8,128)(2,1)S(1)}, u32[]{:S(2)}, u32[]{:S(2)}) collective-permute-start(bf16[256,2048]{1,0:T(8,128)(2,1)} %collective-permute-done.1.refs_1_), channel_id=1, source_target_pairs={{0,24},{1,25},{2,26},{3,27},{4,28},{5,29},{6,30},{7,31},{8,16},{9,... | collective-permute-start | bytes 3145736 | tf_op jit(solution)/shard_map/ppermute | solution.py:41
  42.3 0.0 collective-permute-start.4
  42.3 0.0 collective-permute-done.refs_0_
  42.3 0.6 collective-permute-start.8
  42.9 0.0 collective-permute-done.2.refs_2_
  42.9 2.7 %collective-permute-start.3 = (bf16[256,2048]{1,0:T(8,128)(2,1)}, bf16[256,2048]{1,0:T(8,128)(2,1)S(1)}, u32[]{:S(2)}, u32[]{:S(2)}) collective-permute-start(bf16[256,2048]{1,0:T(8,128)(2,1)} %collective-permute-done.refs_0_), channel_id=1, source_target_pairs={{0,96},{1,97},{2,98},{3,99},{4,100},{5,101},{6,102},{7,103},{8,104... | collective-permute-start | bytes 3145736 | tf_op jit(solution)/shard_map/ppermute | solution.py:41
  45.6 0.0 collective-permute-done.9.refs_9_
  45.6 0.4 collective-permute-start.10
  45.9 8.9 %all-to-all-done.x_ref = bf16[16,2,400,128]{3,2,1,0:T(8,128)(2,1)} async-done(((bf16[16,2,400,128]{3,2,1,0:T(8,128)(2,1)}), bf16[16,2,400,128]{3,2,1,0:T(8,128)(2,1)}, u32[]{:S(2)}, u32[]{:S(2)}) %all-to-all-start) | async-done | bytes 3276832 | tf_op jit(solution)/shard_map/all_to_all | solution.py:319
  54.8 15.5 %attention.1 = bf16[16,2,128,128]{3,2,1,0:T(8,128)(2,1)} custom-call(bf16[16,2,400,128]{3,2,1,0:T(8,128)(2,1)} %all-to-all-done.x_ref), custom_call_target="tpu_custom_call" | custom-call | flops 17179869184 | bytes 4194304 | tf_op jit(solution)/shard_map/attention/pallas_call | solution.py:177
  70.3 10.4 %all-to-all-start.1 = ((bf16[16,2,128,128]{3,2,1,0:T(8,128)(2,1)}), bf16[16,2,128,128]{3,2,1,0:T(8,128)(2,1)S(1)}, u32[]{:S(2)}, u32[]{:S(2)}) async-start(bf16[16,2,128,128]{3,2,1,0:T(8,128)(2,1)} %attention.1), calls=%async_computation.1 | async-start | bytes 2097152 | tf_op jit(solution)/shard_map/all_to_all | solution.py:338
  80.7 0.0 collective-permute-done.5.refs_3_
  80.7 0.0 copy-start.2
  80.7 0.0 collective-permute-done.4.refs_5_
  80.7 0.0 collective-permute-done.3.refs_4_
  80.7 0.0 copy-start.3
  80.7 0.9 slice.7
  81.6 2.8 %collective-permute-start.7 = (bf16[128,2048]{1,0:T(8,128)(2,1)}, bf16[128,2048]{1,0:T(8,128)(2,1)}, u32[]{:S(2)}, u32[]{:S(2)}) collective-permute-start(bf16[128,2048]{1,0:T(8,128)(2,1)} %slice.7), channel_id=1, source_target_pairs={{0,96},{1,97},{2,98},{3,99},{4,100},{5,101},{6,102},{7,103},{8,104... | collective-permute-start | bytes 1572872 | tf_op jit(solution)/shard_map/ppermute | solution.py:41
  84.4 0.8 slice.6
  85.2 0.0 collective-permute-start.6
  85.2 0.6 stack.39.place
  85.9 0.4 collective-permute-start.11
  86.2 0.0 collective-permute-done.8.refs_8_
  86.2 0.1 collective-permute-start.12
  86.4 0.0 collective-permute-done.10.refs_10_
  86.4 0.4 collective-permute-start.13
  86.7 9.2 %collective-permute-done.7.refs_7_ = bf16[128,2048]{1,0:T(8,128)(2,1)} collective-permute-done((bf16[128,2048]{1,0:T(8,128)(2,1)}, bf16[128,2048]{1,0:T(8,128)(2,1)}, u32[]{:S(2)}, u32[]{:S(2)}) %collective-permute-start.7) | collective-permute-done | bytes 524320 | tf_op jit(solution)/shard_map/ppermute | solution.py:41
  96.0 0.9 collective-permute-start.15
  96.8 3.1 %collective-permute-done.6.refs_6_ = bf16[128,2048]{1,0:T(8,128)(2,1)} collective-permute-done((bf16[128,2048]{1,0:T(8,128)(2,1)}, bf16[128,2048]{1,0:T(8,128)(2,1)}, u32[]{:S(2)}, u32[]{:S(2)}) %collective-permute-start.6) | collective-permute-done | bytes 524320 | tf_op jit(solution)/shard_map/ppermute | solution.py:41
  99.9 1.2 %collective-permute-start.14 = (bf16[128,2048]{1,0:T(8,128)(2,1)}, bf16[128,2048]{1,0:T(8,128)(2,1)}, u32[]{:S(2)}, u32[]{:S(2)}) collective-permute-start(bf16[128,2048]{1,0:T(8,128)(2,1)} %collective-permute-done.6.refs_6_), channel_id=1, source_target_pairs={{0,1},{1,0},{2,3},{3,2},{4,5},{5,4},{6,7},{7,6},{8,9},{9,8},{10,11... | collective-permute-start | bytes 1572872 | tf_op jit(solution)/shard_map/ppermute | solution.py:41
  101.1 0.0 all-to-all-done.1.att_ref
  101.1 1.0 copy-done.1
  102.1 0.0 copy-done.2
  102.1 0.0 collective-permute-done.15.refs_15_
  102.1 0.9 collective-permute-done.14.refs_14_
  103.0 0.0 collective-permute-done.13.refs_13_
  103.0 0.0 collective-permute-done.11.refs_11_
  103.0 0.0 collective-permute-done.12.refs_12_
  103.0 12.7 %project.1 = bf16[256,4096]{1,0:T(8,128)(2,1)} custom-call(s32[9]{0:T(128)} %stack.39.place, bf16[16,2,128,128]{3,2,1,0:T(8,128)(2,1)} %arrive.1.att_ref, bf16[256,4096]{1,0:T(8,128)(2,1)} %bitcast.14, bf16[256,4096]{1,0:T(8,128)(2,1)} %own_ref.1, bf16[256,2048]{1,0:T(8,128)(2,1)} %collective-permute-done.refs_0_, ...), custom_call_target="tpu_custom_call" | custom-call | flops 4294967296 | bytes 20971520 | tf_op jit(solution)/shard_map/project/pallas_call | solution.py:271
  (4 shorter events, 0.0 us)
Async XLA Ops:
  4.6 7.9 %copy-start = (bf16[256,4096]{1,0:T(8,128)(2,1)S(1)}, bf16[256,4096]{1,0:T(8,128)(2,1)}, u32[]{:S(2)}) copy-start(bf16[256,4096]{1,0:T(8,128)(2,1)} %own_ref.1) | copy-start | bytes 6291460
  4.6 50.2 %all-to-all-start = ((bf16[16,2,400,128]{3,2,1,0:T(8,128)(2,1)}), bf16[16,2,400,128]{3,2,1,0:T(8,128)(2,1)}, u32[]{:S(2)}, u32[]{:S(2)}) async-start(bf16[16,2,400,128]{3,2,1,0:T(8,128)(2,1)} %pack.1), calls=%async_computation | async-start | bytes 6553600 | tf_op jit(solution)/shard_map/all_to_all | solution.py:319
  12.6 26.1 %collective-permute-start.1 = (bf16[256,2048]{1,0:T(8,128)(2,1)S(1)}, bf16[256,2048]{1,0:T(8,128)(2,1)}, u32[]{:S(2)}, u32[]{:S(2)}) collective-permute-start(bf16[256,2048]{1,0:T(8,128)(2,1)S(1)} %constant_dynamic-slice_fusion), channel_id=1, source_target_pairs={{0,32},{1,33},{2,34},{3,35},{4,36},{5,37},{6,38},{7,39},{8,40},{9,... | collective-permute-start | bytes 3145736 | tf_op jit(solution)/shard_map/ppermute | solution.py:41
  14.0 28.3 %collective-permute-start = (bf16[256,2048]{1,0:T(8,128)(2,1)S(1)}, bf16[256,2048]{1,0:T(8,128)(2,1)}, u32[]{:S(2)}, u32[]{:S(2)}) collective-permute-start(bf16[256,2048]{1,0:T(8,128)(2,1)S(1)} %constant_dynamic-slice_fusion), channel_id=1, source_target_pairs={{0,24},{1,25},{2,26},{3,27},{4,28},{5,29},{6,30},{7,31},{8,16},{9,... | collective-permute-start | bytes 3145736 | tf_op jit(solution)/shard_map/ppermute | solution.py:41
  16.6 26.3 %collective-permute-start.2 = (bf16[256,2048]{1,0:T(8,128)(2,1)S(1)}, bf16[256,2048]{1,0:T(8,128)(2,1)}, u32[]{:S(2)}, u32[]{:S(2)}) collective-permute-start(bf16[256,2048]{1,0:T(8,128)(2,1)S(1)} %constant_dynamic-slice_fusion), channel_id=1, source_target_pairs={{0,96},{1,97},{2,98},{3,99},{4,100},{5,101},{6,102},{7,103},{8,104... | collective-permute-start | bytes 3145736 | tf_op jit(solution)/shard_map/ppermute | solution.py:41
  38.8 6.8 %collective-permute-start.9 = (bf16[256,2048]{1,0:T(8,128)(2,1)}, bf16[256,2048]{1,0:T(8,128)(2,1)}, u32[]{:S(2)}, u32[]{:S(2)}) collective-permute-start(bf16[256,2048]{1,0:T(8,128)(2,1)} %collective-permute-done.1.refs_1_), channel_id=1, source_target_pairs={{0,1},{1,0},{2,3},{3,2},{4,5},{5,4},{6,7},{7,6},{8,9},{9,8},{10,11... | collective-permute-start | bytes 3145736 | tf_op jit(solution)/shard_map/ppermute | solution.py:41
  39.7 41.0 %collective-permute-start.5 = (bf16[256,2048]{1,0:T(8,128)(2,1)}, bf16[256,2048]{1,0:T(8,128)(2,1)S(1)}, u32[]{:S(2)}, u32[]{:S(2)}) collective-permute-start(bf16[256,2048]{1,0:T(8,128)(2,1)} %collective-permute-done.1.refs_1_), channel_id=1, source_target_pairs={{0,24},{1,25},{2,26},{3,27},{4,28},{5,29},{6,30},{7,31},{8,16},{9,... | collective-permute-start | bytes 3145736 | tf_op jit(solution)/shard_map/ppermute | solution.py:41
  42.3 38.4 %collective-permute-start.4 = (bf16[256,2048]{1,0:T(8,128)(2,1)}, bf16[256,2048]{1,0:T(8,128)(2,1)}, u32[]{:S(2)}, u32[]{:S(2)}) collective-permute-start(bf16[256,2048]{1,0:T(8,128)(2,1)} %collective-permute-done.1.refs_1_), channel_id=1, source_target_pairs={{0,32},{1,33},{2,34},{3,35},{4,36},{5,37},{6,38},{7,39},{8,40},{9,... | collective-permute-start | bytes 3145736 | tf_op jit(solution)/shard_map/ppermute | solution.py:41
  42.3 43.9 %collective-permute-start.8 = (bf16[256,2048]{1,0:T(8,128)(2,1)}, bf16[256,2048]{1,0:T(8,128)(2,1)}, u32[]{:S(2)}, u32[]{:S(2)}) collective-permute-start(bf16[256,2048]{1,0:T(8,128)(2,1)} %collective-permute-done.refs_0_), channel_id=1, source_target_pairs={{0,1},{1,0},{2,3},{3,2},{4,5},{5,4},{6,7},{7,6},{8,9},{9,8},{10,11... | collective-permute-start | bytes 3145736 | tf_op jit(solution)/shard_map/ppermute | solution.py:41
  42.9 37.8 %collective-permute-start.3 = (bf16[256,2048]{1,0:T(8,128)(2,1)}, bf16[256,2048]{1,0:T(8,128)(2,1)S(1)}, u32[]{:S(2)}, u32[]{:S(2)}) collective-permute-start(bf16[256,2048]{1,0:T(8,128)(2,1)} %collective-permute-done.refs_0_), channel_id=1, source_target_pairs={{0,96},{1,97},{2,98},{3,99},{4,100},{5,101},{6,102},{7,103},{8,104... | collective-permute-start | bytes 3145736 | tf_op jit(solution)/shard_map/ppermute | solution.py:41
  45.6 40.8 %collective-permute-start.10 = (bf16[256,2048]{1,0:T(8,128)(2,1)}, bf16[256,2048]{1,0:T(8,128)(2,1)}, u32[]{:S(2)}, u32[]{:S(2)}) collective-permute-start(bf16[256,2048]{1,0:T(8,128)(2,1)} %collective-permute-done.2.refs_2_), channel_id=1, source_target_pairs={{0,1},{1,0},{2,3},{3,2},{4,5},{5,4},{6,7},{7,6},{8,9},{9,8},{10,11... | collective-permute-start | bytes 3145736 | tf_op jit(solution)/shard_map/ppermute | solution.py:41
  70.3 30.8 %all-to-all-start.1 = ((bf16[16,2,128,128]{3,2,1,0:T(8,128)(2,1)}), bf16[16,2,128,128]{3,2,1,0:T(8,128)(2,1)S(1)}, u32[]{:S(2)}, u32[]{:S(2)}) async-start(bf16[16,2,128,128]{3,2,1,0:T(8,128)(2,1)} %attention.1), calls=%async_computation.1 | async-start | bytes 2097152 | tf_op jit(solution)/shard_map/all_to_all | solution.py:338
  80.7 21.4 %copy-start.2 = (bf16[256,2048]{1,0:T(8,128)(2,1)}, bf16[256,2048]{1,0:T(8,128)(2,1)S(1)}, u32[]{:S(2)}) copy-start(bf16[256,2048]{1,0:T(8,128)(2,1)S(1)} %collective-permute-done.5.refs_3_) | copy-start | bytes 3145732
  80.7 21.4 %copy-start.3 = (bf16[256,2048]{1,0:T(8,128)(2,1)}, bf16[256,2048]{1,0:T(8,128)(2,1)S(1)}, u32[]{:S(2)}) copy-start(bf16[256,2048]{1,0:T(8,128)(2,1)S(1)} %collective-permute-done.3.refs_4_) | copy-start | bytes 3145732
  81.6 14.3 %collective-permute-start.7 = (bf16[128,2048]{1,0:T(8,128)(2,1)}, bf16[128,2048]{1,0:T(8,128)(2,1)}, u32[]{:S(2)}, u32[]{:S(2)}) collective-permute-start(bf16[128,2048]{1,0:T(8,128)(2,1)} %slice.7), channel_id=1, source_target_pairs={{0,96},{1,97},{2,98},{3,99},{4,100},{5,101},{6,102},{7,103},{8,104... | collective-permute-start | bytes 1572872 | tf_op jit(solution)/shard_map/ppermute | solution.py:41
  85.2 14.7 %collective-permute-start.6 = (bf16[128,2048]{1,0:T(8,128)(2,1)}, bf16[128,2048]{1,0:T(8,128)(2,1)}, u32[]{:S(2)}, u32[]{:S(2)}) collective-permute-start(bf16[128,2048]{1,0:T(8,128)(2,1)} %slice.6), channel_id=1, source_target_pairs={{0,32},{1,33},{2,34},{3,35},{4,36},{5,37},{6,38},{7,39},{8,40},{9,... | collective-permute-start | bytes 1572872 | tf_op jit(solution)/shard_map/ppermute | solution.py:41
  85.9 17.1 %collective-permute-start.11 = (bf16[256,2048]{1,0:T(8,128)(2,1)S(1)}, bf16[256,2048]{1,0:T(8,128)(2,1)}, u32[]{:S(2)}, u32[]{:S(2)}) collective-permute-start(bf16[256,2048]{1,0:T(8,128)(2,1)S(1)} %collective-permute-done.5.refs_3_), channel_id=1, source_target_pairs={{0,1},{1,0},{2,3},{3,2},{4,5},{5,4},{6,7},{7,6},{8,9},{9,8},{10,11... | collective-permute-start | bytes 3145736 | tf_op jit(solution)/shard_map/ppermute | solution.py:41
  86.2 16.8 %collective-permute-start.12 = (bf16[256,2048]{1,0:T(8,128)(2,1)S(1)}, bf16[256,2048]{1,0:T(8,128)(2,1)}, u32[]{:S(2)}, u32[]{:S(2)}) collective-permute-start(bf16[256,2048]{1,0:T(8,128)(2,1)S(1)} %collective-permute-done.3.refs_4_), channel_id=1, source_target_pairs={{0,1},{1,0},{2,3},{3,2},{4,5},{5,4},{6,7},{7,6},{8,9},{9,8},{10,11... | collective-permute-start | bytes 3145736 | tf_op jit(solution)/shard_map/ppermute | solution.py:41
  86.4 16.6 %collective-permute-start.13 = (bf16[256,2048]{1,0:T(8,128)(2,1)}, bf16[256,2048]{1,0:T(8,128)(2,1)}, u32[]{:S(2)}, u32[]{:S(2)}) collective-permute-start(bf16[256,2048]{1,0:T(8,128)(2,1)} %collective-permute-done.4.refs_5_), channel_id=1, source_target_pairs={{0,1},{1,0},{2,3},{3,2},{4,5},{5,4},{6,7},{7,6},{8,9},{9,8},{10,11... | collective-permute-start | bytes 3145736 | tf_op jit(solution)/shard_map/ppermute | solution.py:41
  96.0 6.1 %collective-permute-start.15 = (bf16[128,2048]{1,0:T(8,128)(2,1)}, bf16[128,2048]{1,0:T(8,128)(2,1)}, u32[]{:S(2)}, u32[]{:S(2)}) collective-permute-start(bf16[128,2048]{1,0:T(8,128)(2,1)} %collective-permute-done.7.refs_7_), channel_id=1, source_target_pairs={{0,1},{1,0},{2,3},{3,2},{4,5},{5,4},{6,7},{7,6},{8,9},{9,8},{10,11... | collective-permute-start | bytes 1572872 | tf_op jit(solution)/shard_map/ppermute | solution.py:41
  99.9 3.1 %collective-permute-start.14 = (bf16[128,2048]{1,0:T(8,128)(2,1)}, bf16[128,2048]{1,0:T(8,128)(2,1)}, u32[]{:S(2)}, u32[]{:S(2)}) collective-permute-start(bf16[128,2048]{1,0:T(8,128)(2,1)} %collective-permute-done.6.refs_6_), channel_id=1, source_target_pairs={{0,1},{1,0},{2,3},{3,2},{4,5},{5,4},{6,7},{7,6},{8,9},{9,8},{10,11... | collective-permute-start | bytes 1572872 | tf_op jit(solution)/shard_map/ppermute | solution.py:41
  101.1 1.0 copy-start.1

commit v3 on v2

--- a/solution.py
+++ b/solution.py
@@ -23,6 +23,7 @@
 FSDP = ("y", "xh")
 SEQ = ("xl", "z", "c")
 VMEM = 56 * 2**20
+SMALL = 24 * 2**20
 
 
 def tables():
@@ -51,6 +52,10 @@
 
 def x_over(y, xh, xl, z, c):
     return (y, 1 - xh, 1 - xl, z, c)
+
+
+def x_over_y_down(y, xh, xl, z, c):
+    return ((y + 3) % 4, 1 - xh, 1 - xl, z, c)
 
 
 def core_over(y, xh, xl, z, c):
@@ -95,7 +100,7 @@
     )(starts, queries, keys, values, jnp.asarray(cosine), jnp.asarray(sine))
 
 
-def attention_kernel(x_ref, o_ref, qs, kt, vs, scores, index, pos, moved, *, tq, width):
+def attention_kernel(x_ref, o_ref, qs, kt, vs, scores, index, pos, moved, left, *, tq, width):
     tiles = LEN // tq
     for t in range(2 * HEADS):
         row = x_ref[t // 2, t % 2, 3 * HALF :, :].astype(jnp.float32)
@@ -165,22 +170,30 @@
             jnp.bfloat16
         )
 
-    def unplace(t, carry):
-        at = pl.ds(pl.multiple_of(pos[t, 0] * HALF, HALF), HALF)
-        o_ref[t // 2, t % 2] = qs[at, :]
+    def leave(t):
+        from_ = qs.at[pl.ds(pl.multiple_of(pos[t, 0] * HALF, HALF), HALF)]
+        return pltpu.make_async_copy(from_, o_ref.at[t // 2, t % 2], left.at[t])
+
+    def start(t, carry):
+        leave(t).start()
         return carry
 
-    lax.fori_loop(0, 2 * HEADS, unplace, 0, unroll=4)
+    def wait(t, carry):
+        leave(t).wait()
+        return carry
+
+    lax.fori_loop(0, 2 * HEADS, start, 0, unroll=8)
+    lax.fori_loop(0, 2 * HEADS, wait, 0, unroll=8)
 
 
 def attention(packed, tq=256, width=1024):
     return pl.pallas_call(
         functools.partial(attention_kernel, tq=tq, width=width),
-        out_shape=jax.ShapeDtypeStruct((HEADS, 2, HALF, HEAD_DIM), jnp.bfloat16),
+        out_shape=pltpu.HBM((HEADS, 2, HALF, HEAD_DIM), jnp.bfloat16),
         in_specs=[
             pl.BlockSpec(memory_space=pltpu.VMEM),
         ],
-        out_specs=pl.BlockSpec(memory_space=pltpu.VMEM),
+        out_specs=pl.BlockSpec(memory_space=pltpu.HBM),
         scratch_shapes=[
             pltpu.VMEM((LEN, HEAD_DIM), jnp.bfloat16),
             pltpu.VMEM((HEAD_DIM, LEN), jnp.bfloat16),
@@ -189,8 +202,9 @@
             pltpu.VMEM((2 * HEADS, 128), jnp.int32),
             pltpu.SMEM((2 * HEADS, 128), jnp.int32),
             pltpu.SemaphoreType.DMA,
+            pltpu.SemaphoreType.DMA((2 * HEADS,)),
         ],
-        compiler_params=pltpu.CompilerParams(vmem_limit_bytes=VMEM),
+        compiler_params=pltpu.CompilerParams(vmem_limit_bytes=SMALL),
         cost_estimate=pl.CostEstimate(
             flops=8 * LEN * LEN * HEAD_DIM, bytes_accessed=4 * 2**20, transcendentals=LEN * LEN // 2
         ),
@@ -201,97 +215,85 @@
 PIECES = ((0, 0), (0, 1), (3, 0), (1, 0), (3, 1), (1, 1), (2, 0), (2, 1))
 STEP = 512
 HALF_D = D // 2
-GROUP = WIDTH // 2
-
-
-def project_kernel(place, att_ref, hidden_ref, own_ref, *refs):
-    halves = refs[:8], refs[8:16]
-    out_ref, heads, left, rows, hidden, acc, out, att_sem, hidden_sem, in_sem, out_sem = refs[16:]
-
-    def first_column(half):
-        core = place[0] if half == 0 else 1 - place[0]
-        return core * HALF_D
-
-    def fetches(half):
-        first, copies = 0, []
-        at = pl.ds(pl.multiple_of(first_column(half), HALF_D), HALF_D)
-        for n, ref in enumerate([own_ref.at[:, at], *halves[half]]):
-            count = ref.shape[0]
-            to = rows.at[half, first : first + count]
-            copies.append((first, pltpu.make_async_copy(ref, to, in_sem.at[half, n])))
-            first += count
-        return copies
-
+GROUP = WIDTH // 4
+
+
+def project_kernel(place, att_ref, hidden_ref, own_ref, *refs, half):
+    pieces = refs[:7]
+    out_ref, heads, left, rows, hidden, acc, out, att_sem, hidden_sem, in_sem, out_sem = refs[-11:]
+    core = place[0] if half == 0 else 1 - place[0]
+    here = pl.ds(pl.multiple_of(core * HALF_D, HALF_D), HALF_D)
+    first, fetches = 0, []
+    for n, ref in enumerate([own_ref.at[:, here], *pieces]):
+        to = rows.at[first : first + ref.shape[0]]
+        fetches.append((first, pltpu.make_async_copy(ref, to, in_sem.at[n])))
+        first += ref.shape[0]
     att = pltpu.make_async_copy(att_ref, heads, att_sem)
-    residual = pltpu.make_async_copy(hidden_ref, hidden, hidden_sem)
-    pieces = [fetches(half) for half in range(2)]
+    residual = pltpu.make_async_copy(hidden_ref.at[:, here], hidden, hidden_sem)
     att.start()
-    for first, copy in pieces[0]:
-        if first == GROUP:
-            residual.start()
+    for _, copy in fetches:
         copy.start()
-    for _, copy in pieces[1]:
-        copy.start()
+    residual.start()
     att.wait()
     for n in range(len(PIECES)):
         for i in range(2):
             head = heads[2 * place[1 + n] + i].reshape(2 * HALF, HEAD_DIM)
             left[:, (2 * n + i) * HEAD_DIM : (2 * n + i + 1) * HEAD_DIM] = head
     stores = []
-    for half in range(2):
-        for group in range(0, WIDTH, GROUP):
-            for first, copy in pieces[half]:
-                if group <= first < group + GROUP:
-                    copy.wait()
-            if half == 0 and group > 0:
-                residual.wait()
-            for t in range(HALF_D // STEP):
-                at = pl.ds(t * STEP, STEP)
-                part = jnp.dot(
-                    left[:, group : group + GROUP],
-                    rows[half, group : group + GROUP, at],
-                    preferred_element_type=jnp.float32,
-                )
-                if group == 0:
-                    acc[:, at] = part
-                else:
-                    to = pl.ds(pl.multiple_of(first_column(half) + t * STEP, STEP), STEP)
-                    total = hidden[:, to].astype(jnp.float32) + (acc[:, at] + part)
-                    n = half * (HALF_D // STEP) + t
-                    out[n] = total.astype(jnp.bfloat16)
-                    stores.append(
-                        pltpu.make_async_copy(out.at[n], out_ref.at[:, to], out_sem.at[n])
-                    )
-                    stores[-1].start()
-    for copy in stores:
-        copy.wait()
-
-
-def project(place, att, hidden, own, mine, other):
+    for group in range(0, WIDTH, GROUP):
+        for first, copy in fetches:
+            if group <= first < group + GROUP:
+                copy.wait()
+        if group + GROUP == WIDTH:
+            residual.wait()
+        for t in range(HALF_D // STEP):
+            at = pl.ds(t * STEP, STEP)
+            part = jnp.dot(
+                left[:, group : group + GROUP],
+                rows[group : group + GROUP, at],
+                preferred_element_type=jnp.float32,
+            )
+            if group > 0:
+                part += acc[:, at]
+            if group + GROUP < WIDTH:
+                acc[:, at] = part
+            else:
+                out[t] = (hidden[:, at].astype(jnp.float32) + part).astype(jnp.bfloat16)
+                to = pl.ds(pl.multiple_of(core * HALF_D + t * STEP, STEP), STEP)
+                store = pltpu.make_async_copy(out.at[t], out_ref.at[:, to], out_sem.at[t])
+                store.start()
+                stores.append(store)
+    for store in stores:
+        store.wait()
+
+
+def project(half, place, att, hidden, own, pieces, *done):
+    hidden = pltpu.with_memory_space_constraint(hidden, pltpu.HBM)
     return pl.pallas_call(
-        project_kernel,
+        functools.partial(project_kernel, half=half),
         in_specs=[pl.BlockSpec(memory_space=pltpu.SMEM)]
-        + [pl.BlockSpec(memory_space=pl.ANY)] * 19,
+        + [pl.BlockSpec(memory_space=pl.ANY)] * (10 + len(done)),
         out_specs=pl.BlockSpec(memory_space=pl.ANY),
         scratch_shapes=[
             pltpu.VMEM((HEADS, 2, HALF, HEAD_DIM), jnp.bfloat16),
             pltpu.VMEM((2 * HALF, WIDTH), jnp.bfloat16),
-            pltpu.VMEM((2, WIDTH, HALF_D), jnp.bfloat16),
-            pltpu.VMEM((2 * HALF, D), jnp.bfloat16),
+            pltpu.VMEM((WIDTH, HALF_D), jnp.bfloat16),
+            pltpu.VMEM((2 * HALF, HALF_D), jnp.bfloat16),
             pltpu.VMEM((2 * HALF, HALF_D), jnp.float32),
-            pltpu.VMEM((D // STEP, 2 * HALF, STEP), jnp.bfloat16),
+            pltpu.VMEM((HALF_D // STEP, 2 * HALF, STEP), jnp.bfloat16),
             pltpu.SemaphoreType.DMA,
             pltpu.SemaphoreType.DMA,
-            pltpu.SemaphoreType.DMA((2, 9)),
-            pltpu.SemaphoreType.DMA((D // STEP,)),
+            pltpu.SemaphoreType.DMA((8,)),
+            pltpu.SemaphoreType.DMA((HALF_D // STEP,)),
         ],
         out_shape=jax.ShapeDtypeStruct((2 * HALF, D), jnp.bfloat16),
-        compiler_params=pltpu.CompilerParams(vmem_limit_bytes=VMEM),
+        input_output_aliases={11: 0} if done else {},
+        compiler_params=pltpu.CompilerParams(vmem_limit_bytes=SMALL),
         cost_estimate=pl.CostEstimate(
-            flops=4 * HALF * WIDTH * D, bytes_accessed=20 * 2**20, transcendentals=0
+            flops=2 * HALF * WIDTH * D, bytes_accessed=12 * 2**20, transcendentals=0
         ),
         name="project",
-    )(place, att, hidden, own, *mine, *other)
+    )(place, att, hidden, own, *pieces, *done)
 
 
 def arrive_kernel(att_ref, out_ref):
@@ -305,7 +307,7 @@
         out_specs=pl.BlockSpec(memory_space=pl.ANY),
         out_shape=jax.ShapeDtypeStruct(att.shape, att.dtype),
         input_output_aliases={0: 0},
-        compiler_params=pltpu.CompilerParams(vmem_limit_bytes=VMEM),
+        compiler_params=pltpu.CompilerParams(vmem_limit_bytes=SMALL),
         cost_estimate=pl.CostEstimate(
             flops=2 * 10**10, bytes_accessed=2 * 2**20, transcendentals=0
         ),
@@ -327,25 +329,27 @@
         (3, 1): send(mine[3, 0], x_over),
         (1, 1): send(mine[0, 1], y_down),
         (2, 0): send(mine[3, 0], y_up),
+        (2, 1): send(mine[1, 0], x_over_y_down),
     }
-    other[0, 1] = send(mine[0, 1], core_over)
-    other[3, 0] = send(mine[3, 0], core_over)
-    later, _ = lax.optimization_barrier((mine[1, 0], other[3, 0]))
-    other[1, 0] = send(later, core_over)
+    before = mine[3, 0]
+    for at in (3, 0), (0, 1), (1, 0):
+        piece, _ = lax.optimization_barrier((mine[at], before))
+        other[at] = before = send(piece, core_over)
 
     attended = attention(packed)
     second, _ = lax.optimization_barrier((second, attended))
     attended = lax.all_to_all(attended, SEQ, 0, 0, tiled=True)
-    top = send(second[3, 1][:HALF], y_up)
-    bottom = send(second[1, 1][HALF:], y_down)
-    last = [second[at] for at in PIECES[4:7]] + [top, bottom]
-    mine = [mine[at] for at in PIECES[1:4]] + last
-    other = [other[at] for at in PIECES[1:4]] + [send(a, core_over) for a in last]
+    for at in second:
+        mine[at] = second[at]
+        other[at] = send(mine[at], core_over)
+    mine = [mine[at] for at in PIECES[1:]]
+    other = [other[at] for at in PIECES[1:]]
 
     owners = [((y + dy) % 4) * 2 + (xh + dx) % 2 for dy, dx in PIECES]
     place = jnp.stack([c, *owners]).astype(jnp.int32)
     attended = arrive(attended)
-    return project(place, attended, hidden_in[0], out_weight, mine, other)[None]
+    done = project(0, place, attended, hidden_in[0], out_weight, mine)
+    return project(1, place, attended, hidden_in[0], out_weight, other, done)[None]
 
 
 def solution(mesh):

time: 116 us -> 108 us (0.931)
  starting transfers between devices: 36.7 us -> 34.2 us
  local copies, waits for them, and re-layouts: 3.49 us -> 1.19 us
  waiting for transfers between devices: 42.7 us -> 41 us
  Pallas kernels: 32.8 us -> 31.1 us
    all_to_all x1, waiting for transfers between devices: 0.01 us -> 4.26 us  [shards(): attended = lax.all_to_all(attended, SEQ, 0, 0, tiled=True)]
    ppermute x16 -> x14, waiting for transfers between devices: 33.8 us -> 29.6 us  [send(): lax.ppermute(array, AXES, [(index[p], index[move(*p)]) for p in places])]
    ppermute x16 -> x14, starting transfers between devices: 18.4 us -> 15.9 us  [send(): lax.ppermute(array, AXES, [(index[p], index[move(*p)]) for p in places])]
    all_to_all x1, waiting for transfers between devices: 8.87 us -> 7.05 us  [shards(): packed = lax.all_to_all(packed, SEQ, 0, 0, tiled=True)]
    slice x2 -> x0, local copies, waits for them, and re-layouts: 1.78 us -> none  [the longest x1 0.93 us: shards(): bottom = send(second[1, 1][HALF:], y_down)]
    pallas_call x1 -> x2, Pallas kernels: 12.7 us -> 11.1 us  [project(): pl.pallas_call(functools.partial(project_kernel, half=half), in_specs=[pl...]
  transfers between devices with their start and end apart: 18 -> 16, of which waited for: 5 -> 4; matrix products, arithmetic and copies ran while one was open for 2% -> 0% of each run, Pallas kernels for 13% -> 20%
where the time goes in v3:
time: 108 us
  waiting for transfers between devices  41 us (38%)
  starting transfers between devices  34.2 us (32%)
  Pallas kernels  31.1 us (29%)
  local copies, waits for them, and re-layouts  1.19 us (1%)
    ppermute x14, waiting for transfers between devices, send(): lax.ppermute(array, AXES, [(index[p], index[move(*p)]) for p in places])  29.6 us
    ppermute x14, starting transfers between devices, send(): lax.ppermute(array, AXES, [(index[p], index[move(*p)]) for p in places])  15.9 us
    pallas_call x1, Pallas kernels, attention(): pl.pallas_call(functools.partial(attention_kernel, tq=tq, width=width), o...  15.4 us
    pallas_call x2, Pallas kernels, project(): pl.pallas_call(functools.partial(project_kernel, half=half), in_specs=[pl...  11.1 us
    all_to_all x1, starting transfers between devices, shards(): attended = lax.all_to_all(attended, SEQ, 0, 0, tiled=True)  10.4 us
    all_to_all x1, starting transfers between devices, shards(): packed = lax.all_to_all(packed, SEQ, 0, 0, tiled=True)  7.89 us
    all_to_all x1, waiting for transfers between devices, shards(): packed = lax.all_to_all(packed, SEQ, 0, 0, tiled=True)  7.05 us
    pallas_call x1, Pallas kernels, pack(): pl.pallas_call(pack_kernel, grid_spec=pltpu.PrefetchScalarGridSpec(num_sc...  4.64 us
  transfers between devices with their start and end apart: 16, of which 4 were waited for; matrix products, arithmetic and copies ran while one was open for 0% of the time, Pallas kernels for 20%

profile of v3, /device:TPU:1, one launch (start us, length us, event | category | flops | bytes accessed | tf_op | source)
XLA Modules:
  0.0 107.8 jit_solution(4932600432000613415)
XLA Ops:
  0.0 4.6 %pack.1 = bf16[16,2,400,128]{3,2,1,0:T(8,128)(2,1)} custom-call(s32[2]{0:T(128)} %starts.1, bf16[256,2048]{1,0:T(8,128)(2,1)} %bitcast.16, bf16[256,2048]{1,0:T(8,128)(2,1)} %bitcast.17, bf16[256,2048]{1,0:T(8,128)(2,1)} %bitcast.18, f32[4096,128]{1,0:T(8,128)} %constant.84.clone.cos_ref, f32[4096,128]{1,0:T(8,128)} %constant.85.clone.sin_ref), custom_call_target="tpu_custom_call" | custom-call | tf_op jit(solution)/shard_map/pack/pallas_call | solution.py:89
  4.6 0.0 copy-start
  4.6 7.9 %all-to-all-start = ((bf16[16,2,400,128]{3,2,1,0:T(8,128)(2,1)}), bf16[16,2,400,128]{3,2,1,0:T(8,128)(2,1)}, u32[]{:S(2)}, u32[]{:S(2)}) async-start(bf16[16,2,400,128]{3,2,1,0:T(8,128)(2,1)} %pack.1), calls=%async_computation | async-start | bytes 6553600 | tf_op jit(solution)/shard_map/all_to_all | solution.py:321
  12.5 0.0 copy-done
  12.5 0.1 constant_dynamic-slice_fusion
  12.7 1.4 %collective-permute-start.1 = (bf16[256,2048]{1,0:T(8,128)(2,1)S(1)}, bf16[256,2048]{1,0:T(8,128)(2,1)}, u32[]{:S(2)}, u32[]{:S(2)}) collective-permute-start(bf16[256,2048]{1,0:T(8,128)(2,1)S(1)} %constant_dynamic-slice_fusion), channel_id=1, source_target_pairs={{0,32},{1,33},{2,34},{3,35},{4,36},{5,37},{6,38},{7,39},{8,40},{9,... | collective-permute-start | bytes 3145736 | tf_op jit(solution)/shard_map/ppermute | solution.py:42
  14.0 2.7 %collective-permute-start = (bf16[256,2048]{1,0:T(8,128)(2,1)S(1)}, bf16[256,2048]{1,0:T(8,128)(2,1)}, u32[]{:S(2)}, u32[]{:S(2)}) collective-permute-start(bf16[256,2048]{1,0:T(8,128)(2,1)S(1)} %constant_dynamic-slice_fusion), channel_id=1, source_target_pairs={{0,24},{1,25},{2,26},{3,27},{4,28},{5,29},{6,30},{7,31},{8,16},{9,... | collective-permute-start | bytes 3145736 | tf_op jit(solution)/shard_map/ppermute | solution.py:42
  16.7 1.5 %collective-permute-start.4 = (bf16[256,2048]{1,0:T(8,128)(2,1)S(1)}, bf16[256,2048]{1,0:T(8,128)(2,1)}, u32[]{:S(2)}, u32[]{:S(2)}) collective-permute-start(bf16[256,2048]{1,0:T(8,128)(2,1)S(1)} %constant_dynamic-slice_fusion), channel_id=1, source_target_pairs={{0,96},{1,97},{2,98},{3,99},{4,100},{5,101},{6,102},{7,103},{8,104... | collective-permute-start | bytes 3145736 | tf_op jit(solution)/shard_map/ppermute | solution.py:42
  18.2 20.6 %collective-permute-done.1.refs_1_ = bf16[256,2048]{1,0:T(8,128)(2,1)} collective-permute-done((bf16[256,2048]{1,0:T(8,128)(2,1)S(1)}, bf16[256,2048]{1,0:T(8,128)(2,1)}, u32[]{:S(2)}, u32[]{:S(2)}) %collective-permute-start.1) | collective-permute-done | bytes 1048608 | tf_op jit(solution)/shard_map/ppermute | solution.py:42
  38.8 0.9 collective-permute-start.2
  39.7 0.0 collective-permute-start.7
  39.7 2.7 %collective-permute-start.9 = (bf16[256,2048]{1,0:T(8,128)(2,1)}, bf16[256,2048]{1,0:T(8,128)(2,1)}, u32[]{:S(2)}, u32[]{:S(2)}) collective-permute-start(bf16[256,2048]{1,0:T(8,128)(2,1)} %collective-permute-done.1.refs_1_), channel_id=1, source_target_pairs={{0,24},{1,25},{2,26},{3,27},{4,28},{5,29},{6,30},{7,31},{8,16},{9,... | collective-permute-start | bytes 3145736 | tf_op jit(solution)/shard_map/ppermute | solution.py:42
  42.4 0.0 collective-permute-done.refs_0_
  42.4 2.7 %collective-permute-start.6 = (bf16[256,2048]{1,0:T(8,128)(2,1)}, bf16[256,2048]{1,0:T(8,128)(2,1)}, u32[]{:S(2)}, u32[]{:S(2)}) collective-permute-start(bf16[256,2048]{1,0:T(8,128)(2,1)} %collective-permute-done.refs_0_), channel_id=1, source_target_pairs={{0,96},{1,97},{2,98},{3,99},{4,100},{5,101},{6,102},{7,103},{8,104... | collective-permute-start | bytes 3145736 | tf_op jit(solution)/shard_map/ppermute | solution.py:42
  45.0 0.0 collective-permute-done.4.refs_2_
  45.0 0.0 collective-permute-start.8
  45.0 0.0 collective-permute-done.2.refs_1_
  45.0 0.0 copy-start.1
  45.0 1.0 copy-done.1
  46.0 1.7 %collective-permute-start.3 = (bf16[256,2048]{1,0:T(8,128)(2,1)}, bf16[256,2048]{1,0:T(8,128)(2,1)}, u32[]{:S(2)}, u32[]{:S(2)}) collective-permute-start(bf16[256,2048]{1,0:T(8,128)(2,1)} %collective-permute-done.refs_0_), channel_id=1, source_target_pairs={{0,1},{1,0},{2,3},{3,2},{4,5},{5,4},{6,7},{7,6},{8,9},{9,8},{10,11... | collective-permute-start | bytes 3145736 | tf_op jit(solution)/shard_map/ppermute | solution.py:42
  47.8 7.1 %all-to-all-done.x_ref = bf16[16,2,400,128]{3,2,1,0:T(8,128)(2,1)} async-done(((bf16[16,2,400,128]{3,2,1,0:T(8,128)(2,1)}), bf16[16,2,400,128]{3,2,1,0:T(8,128)(2,1)}, u32[]{:S(2)}, u32[]{:S(2)}) %all-to-all-start) | async-done | bytes 3276832 | tf_op jit(solution)/shard_map/all_to_all | solution.py:321
  54.8 15.4 %attention.1 = bf16[16,2,128,128]{3,2,1,0:T(8,128)(2,1)} custom-call(bf16[16,2,400,128]{3,2,1,0:T(8,128)(2,1)} %all-to-all-done.x_ref), custom_call_target="tpu_custom_call" | custom-call | flops 17179869184 | bytes 4194304 | tf_op jit(solution)/shard_map/attention/pallas_call | solution.py:190
  70.2 10.4 %all-to-all-start.1 = ((bf16[16,2,128,128]{3,2,1,0:T(8,128)(2,1)}), bf16[16,2,128,128]{3,2,1,0:T(8,128)(2,1)S(1)}, u32[]{:S(2)}, u32[]{:S(2)}) async-start(bf16[16,2,128,128]{3,2,1,0:T(8,128)(2,1)} %attention.1), calls=%async_computation.1 | async-start | bytes 2097152 | tf_op jit(solution)/shard_map/all_to_all | solution.py:341
  80.6 0.1 stack.39.place
  80.7 0.0 collective-permute-done.7.refs_5_
  80.7 0.0 collective-permute-done.9.refs_3_
  80.7 9.0 %collective-permute-done.6.refs_4_ = bf16[256,2048]{1,0:T(8,128)(2,1)} collective-permute-done((bf16[256,2048]{1,0:T(8,128)(2,1)}, bf16[256,2048]{1,0:T(8,128)(2,1)}, u32[]{:S(2)}, u32[]{:S(2)}) %collective-permute-start.6) | collective-permute-done | bytes 1048608 | tf_op jit(solution)/shard_map/ppermute | solution.py:42
  89.8 0.0 collective-permute-done.8.refs_6_
  89.8 1.4 %collective-permute-start.10 = (bf16[256,2048]{1,0:T(8,128)(2,1)}, bf16[256,2048]{1,0:T(8,128)(2,1)}, u32[]{:S(2)}, u32[]{:S(2)}) collective-permute-start(bf16[256,2048]{1,0:T(8,128)(2,1)} %collective-permute-done.9.refs_3_), channel_id=1, source_target_pairs={{0,1},{1,0},{2,3},{3,2},{4,5},{5,4},{6,7},{7,6},{8,9},{9,8},{10,11... | collective-permute-start | bytes 3145736 | tf_op jit(solution)/shard_map/ppermute | solution.py:42
  91.2 0.0 collective-permute-start.11
  91.2 0.5 collective-permute-start.12
  91.7 0.0 collective-permute-start.13
  91.7 0.0 collective-permute-done.3.refs_0_
  91.7 0.5 collective-permute-start.5
  92.2 4.3 %all-to-all-done.1.att_ref = bf16[16,2,128,128]{3,2,1,0:T(8,128)(2,1)S(1)} async-done(((bf16[16,2,128,128]{3,2,1,0:T(8,128)(2,1)}), bf16[16,2,128,128]{3,2,1,0:T(8,128)(2,1)S(1)}, u32[]{:S(2)}, u32[]{:S(2)}) %all-to-all-start.1) | async-done | bytes 1048608 | tf_op jit(solution)/shard_map/all_to_all | solution.py:341
  96.5 0.0 copy-start.2
  96.5 5.7 %project.2.refs_7_ = bf16[256,4096]{1,0:T(8,128)(2,1)} custom-call(s32[9]{0:T(128)S(1)} %stack.39.place, bf16[16,2,128,128]{3,2,1,0:T(8,128)(2,1)S(1)} %arrive.1.att_ref, bf16[256,4096]{1,0:T(8,128)(2,1)} %bitcast.14, bf16[256,4096]{1,0:T(8,128)(2,1)S(1)} %copy-done, bf16[256,2048]{1,0:T(8,128)(2,1)} %collective-permute-done.refs_0_, ...), custom_call_target="tpu_custom_call" | custom-call | flops 2147483648 | bytes 12582912 | tf_op jit(solution)/shard_map/project/pallas_call | solution.py:272
  102.1 0.0 collective-permute-done.10.refs_3_
  102.2 0.0 collective-permute-done.11.refs_4_
  102.2 0.0 collective-permute-done.12.refs_5_
  102.2 0.0 collective-permute-done.13.refs_6_
  102.2 0.0 collective-permute-done.5.refs_2_
  102.2 0.0 copy-done.2
  102.2 5.4 %project.3 = bf16[256,4096]{1,0:T(8,128)(2,1)} custom-call(s32[9]{0:T(128)S(1)} %stack.39.place, bf16[16,2,128,128]{3,2,1,0:T(8,128)(2,1)S(1)} %arrive.1.att_ref, bf16[256,4096]{1,0:T(8,128)(2,1)} %bitcast.15, bf16[256,4096]{1,0:T(8,128)(2,1)S(1)} %copy-done, bf16[256,2048]{1,0:T(8,128)(2,1)} %collective-permute-done.3.refs_0_, ...), custom_call_target="tpu_custom_call", output_to_operand_aliasing={{}: (11, {})} | custom-call | flops 2147483648 | bytes 12582912 | tf_op jit(solution)/shard_map/project/pallas_call | solution.py:272
  (1 shorter events, 0.0 us)
Async XLA Ops:
  4.6 7.9 %copy-start = (bf16[256,4096]{1,0:T(8,128)(2,1)S(1)}, bf16[256,4096]{1,0:T(8,128)(2,1)}, u32[]{:S(2)}) copy-start(bf16[256,4096]{1,0:T(8,128)(2,1)} %own_ref.3) | copy-start | bytes 6291460
  4.6 50.2 %all-to-all-start = ((bf16[16,2,400,128]{3,2,1,0:T(8,128)(2,1)}), bf16[16,2,400,128]{3,2,1,0:T(8,128)(2,1)}, u32[]{:S(2)}, u32[]{:S(2)}) async-start(bf16[16,2,400,128]{3,2,1,0:T(8,128)(2,1)} %pack.1), calls=%async_computation | async-start | bytes 6553600 | tf_op jit(solution)/shard_map/all_to_all | solution.py:321
  12.7 26.1 %collective-permute-start.1 = (bf16[256,2048]{1,0:T(8,128)(2,1)S(1)}, bf16[256,2048]{1,0:T(8,128)(2,1)}, u32[]{:S(2)}, u32[]{:S(2)}) collective-permute-start(bf16[256,2048]{1,0:T(8,128)(2,1)S(1)} %constant_dynamic-slice_fusion), channel_id=1, source_target_pairs={{0,32},{1,33},{2,34},{3,35},{4,36},{5,37},{6,38},{7,39},{8,40},{9,... | collective-permute-start | bytes 3145736 | tf_op jit(solution)/shard_map/ppermute | solution.py:42
  14.0 28.3 %collective-permute-start = (bf16[256,2048]{1,0:T(8,128)(2,1)S(1)}, bf16[256,2048]{1,0:T(8,128)(2,1)}, u32[]{:S(2)}, u32[]{:S(2)}) collective-permute-start(bf16[256,2048]{1,0:T(8,128)(2,1)S(1)} %constant_dynamic-slice_fusion), channel_id=1, source_target_pairs={{0,24},{1,25},{2,26},{3,27},{4,28},{5,29},{6,30},{7,31},{8,16},{9,... | collective-permute-start | bytes 3145736 | tf_op jit(solution)/shard_map/ppermute | solution.py:42
  16.7 28.3 %collective-permute-start.4 = (bf16[256,2048]{1,0:T(8,128)(2,1)S(1)}, bf16[256,2048]{1,0:T(8,128)(2,1)}, u32[]{:S(2)}, u32[]{:S(2)}) collective-permute-start(bf16[256,2048]{1,0:T(8,128)(2,1)S(1)} %constant_dynamic-slice_fusion), channel_id=1, source_target_pairs={{0,96},{1,97},{2,98},{3,99},{4,100},{5,101},{6,102},{7,103},{8,104... | collective-permute-start | bytes 3145736 | tf_op jit(solution)/shard_map/ppermute | solution.py:42
  38.8 6.2 %collective-permute-start.2 = (bf16[256,2048]{1,0:T(8,128)(2,1)}, bf16[256,2048]{1,0:T(8,128)(2,1)S(1)}, u32[]{:S(2)}, u32[]{:S(2)}) collective-permute-start(bf16[256,2048]{1,0:T(8,128)(2,1)} %collective-permute-done.1.refs_1_), channel_id=1, source_target_pairs={{0,1},{1,0},{2,3},{3,2},{4,5},{5,4},{6,7},{7,6},{8,9},{9,8},{10,11... | collective-permute-start | bytes 3145736 | tf_op jit(solution)/shard_map/ppermute | solution.py:42
  39.7 41.0 %collective-permute-start.7 = (bf16[256,2048]{1,0:T(8,128)(2,1)}, bf16[256,2048]{1,0:T(8,128)(2,1)}, u32[]{:S(2)}, u32[]{:S(2)}) collective-permute-start(bf16[256,2048]{1,0:T(8,128)(2,1)} %collective-permute-done.1.refs_1_), channel_id=1, source_target_pairs={{0,32},{1,33},{2,34},{3,35},{4,36},{5,37},{6,38},{7,39},{8,40},{9,... | collective-permute-start | bytes 3145736 | tf_op jit(solution)/shard_map/ppermute | solution.py:42
  39.7 41.0 %collective-permute-start.9 = (bf16[256,2048]{1,0:T(8,128)(2,1)}, bf16[256,2048]{1,0:T(8,128)(2,1)}, u32[]{:S(2)}, u32[]{:S(2)}) collective-permute-start(bf16[256,2048]{1,0:T(8,128)(2,1)} %collective-permute-done.1.refs_1_), channel_id=1, source_target_pairs={{0,24},{1,25},{2,26},{3,27},{4,28},{5,29},{6,30},{7,31},{8,16},{9,... | collective-permute-start | bytes 3145736 | tf_op jit(solution)/shard_map/ppermute | solution.py:42
  42.4 47.4 %collective-permute-start.6 = (bf16[256,2048]{1,0:T(8,128)(2,1)}, bf16[256,2048]{1,0:T(8,128)(2,1)}, u32[]{:S(2)}, u32[]{:S(2)}) collective-permute-start(bf16[256,2048]{1,0:T(8,128)(2,1)} %collective-permute-done.refs_0_), channel_id=1, source_target_pairs={{0,96},{1,97},{2,98},{3,99},{4,100},{5,101},{6,102},{7,103},{8,104... | collective-permute-start | bytes 3145736 | tf_op jit(solution)/shard_map/ppermute | solution.py:42
  45.0 44.7 %collective-permute-start.8 = (bf16[256,2048]{1,0:T(8,128)(2,1)}, bf16[256,2048]{1,0:T(8,128)(2,1)}, u32[]{:S(2)}, u32[]{:S(2)}) collective-permute-start(bf16[256,2048]{1,0:T(8,128)(2,1)} %collective-permute-done.4.refs_2_), channel_id=1, source_target_pairs={{0,120},{1,121},{2,122},{3,123},{4,124},{5,125},{6,126},{7,127},{8... | collective-permute-start | bytes 3145736 | tf_op jit(solution)/shard_map/ppermute | solution.py:42
  45.0 1.0 copy-start.1
  46.0 45.7 %collective-permute-start.3 = (bf16[256,2048]{1,0:T(8,128)(2,1)}, bf16[256,2048]{1,0:T(8,128)(2,1)}, u32[]{:S(2)}, u32[]{:S(2)}) collective-permute-start(bf16[256,2048]{1,0:T(8,128)(2,1)} %collective-permute-done.refs_0_), channel_id=1, source_target_pairs={{0,1},{1,0},{2,3},{3,2},{4,5},{5,4},{6,7},{7,6},{8,9},{9,8},{10,11... | collective-permute-start | bytes 3145736 | tf_op jit(solution)/shard_map/ppermute | solution.py:42
  70.2 26.2 %all-to-all-start.1 = ((bf16[16,2,128,128]{3,2,1,0:T(8,128)(2,1)}), bf16[16,2,128,128]{3,2,1,0:T(8,128)(2,1)S(1)}, u32[]{:S(2)}, u32[]{:S(2)}) async-start(bf16[16,2,128,128]{3,2,1,0:T(8,128)(2,1)} %attention.1), calls=%async_computation.1 | async-start | bytes 2097152 | tf_op jit(solution)/shard_map/all_to_all | solution.py:341
  89.8 12.4 %collective-permute-start.10 = (bf16[256,2048]{1,0:T(8,128)(2,1)}, bf16[256,2048]{1,0:T(8,128)(2,1)}, u32[]{:S(2)}, u32[]{:S(2)}) collective-permute-start(bf16[256,2048]{1,0:T(8,128)(2,1)} %collective-permute-done.9.refs_3_), channel_id=1, source_target_pairs={{0,1},{1,0},{2,3},{3,2},{4,5},{5,4},{6,7},{7,6},{8,9},{9,8},{10,11... | collective-permute-start | bytes 3145736 | tf_op jit(solution)/shard_map/ppermute | solution.py:42
  91.2 11.0 %collective-permute-start.11 = (bf16[256,2048]{1,0:T(8,128)(2,1)}, bf16[256,2048]{1,0:T(8,128)(2,1)}, u32[]{:S(2)}, u32[]{:S(2)}) collective-permute-start(bf16[256,2048]{1,0:T(8,128)(2,1)} %collective-permute-done.6.refs_4_), channel_id=1, source_target_pairs={{0,1},{1,0},{2,3},{3,2},{4,5},{5,4},{6,7},{7,6},{8,9},{9,8},{10,11... | collective-permute-start | bytes 3145736 | tf_op jit(solution)/shard_map/ppermute | solution.py:42
  91.2 11.0 %collective-permute-start.12 = (bf16[256,2048]{1,0:T(8,128)(2,1)}, bf16[256,2048]{1,0:T(8,128)(2,1)}, u32[]{:S(2)}, u32[]{:S(2)}) collective-permute-start(bf16[256,2048]{1,0:T(8,128)(2,1)} %collective-permute-done.7.refs_5_), channel_id=1, source_target_pairs={{0,1},{1,0},{2,3},{3,2},{4,5},{5,4},{6,7},{7,6},{8,9},{9,8},{10,11... | collective-permute-start | bytes 3145736 | tf_op jit(solution)/shard_map/ppermute | solution.py:42
  91.7 10.5 %collective-permute-start.13 = (bf16[256,2048]{1,0:T(8,128)(2,1)}, bf16[256,2048]{1,0:T(8,128)(2,1)}, u32[]{:S(2)}, u32[]{:S(2)}) collective-permute-start(bf16[256,2048]{1,0:T(8,128)(2,1)} %collective-permute-done.8.refs_6_), channel_id=1, source_target_pairs={{0,1},{1,0},{2,3},{3,2},{4,5},{5,4},{6,7},{7,6},{8,9},{9,8},{10,11... | collective-permute-start | bytes 3145736 | tf_op jit(solution)/shard_map/ppermute | solution.py:42
  91.7 10.5 %collective-permute-start.5 = (bf16[256,2048]{1,0:T(8,128)(2,1)}, bf16[256,2048]{1,0:T(8,128)(2,1)}, u32[]{:S(2)}, u32[]{:S(2)}) collective-permute-start(bf16[256,2048]{1,0:T(8,128)(2,1)} %collective-permute-done.4.refs_2_), channel_id=1, source_target_pairs={{0,1},{1,0},{2,3},{3,2},{4,5},{5,4},{6,7},{7,6},{8,9},{9,8},{10,11... | collective-permute-start | bytes 3145736 | tf_op jit(solution)/shard_map/ppermute | solution.py:42
  96.5 5.7 %copy-start.2 = (bf16[256,2048]{1,0:T(8,128)(2,1)S(1)}, bf16[256,2048]{1,0:T(8,128)(2,1)}, u32[]{:S(2)}) copy-start(bf16[256,2048]{1,0:T(8,128)(2,1)} %copy-done.1) | copy-start | bytes 3145732

commit v4 on v3

--- a/solution.py
+++ b/solution.py
@@ -22,6 +22,7 @@
 SIZES = (4, 2, 2, 4, 2)
 FSDP = ("y", "xh")
 SEQ = ("xl", "z", "c")
+OWNERS = ("z", "c", "xl")
 VMEM = 56 * 2**20
 SMALL = 24 * 2**20
 
@@ -62,53 +63,111 @@
     return (y, xh, xl, z, 1 - c)
 
 
-def pack_kernel(starts, q_ref, k_ref, v_ref, cos_ref, sin_ref, out_ref):
-    cosine, sine = cos_ref[...], sin_ref[...]
+def pack_kernel(starts, q_ref, k_ref, v_ref, cos_ref, sin_ref, out_ref, *scratch):
+    q, k, v, cosine, sine, turned, index, in_sem, out_sem = scratch
     factor = math.log2(math.e) / math.sqrt(HEAD_DIM)
+    fetches = []
+    for b in range(2):
+        rows = pl.ds(b * HALF, HALF)
+        at = pl.ds(pl.multiple_of(starts[b], HALF), HALF)
+        pairs = [
+            (cos_ref.at[at], cosine.at[b]),
+            (sin_ref.at[at], sine.at[b]),
+            (q_ref.at[rows], q.at[b]),
+            (k_ref.at[rows], k.at[b]),
+            (v_ref.at[rows], v.at[b]),
+        ]
+        fetches.append(
+            [
+                pltpu.make_async_copy(source, target, in_sem.at[b, n])
+                for n, (source, target) in enumerate(pairs)
+            ]
+        )
+    for copies in fetches:
+        for copy in copies:
+            copy.start()
+
+    stores = []
+
+    def leave(source, target):
+        copy = pltpu.make_async_copy(source, target, out_sem.at[len(stores)])
+        copy.start()
+        stores.append(copy)
 
     def turn(block, cosine, sine):
         block = block.astype(jnp.float32)
-        turned = block * cosine + pltpu.roll(block, HEAD_DIM // 2, 1) * sine
-        return turned.astype(jnp.bfloat16)
-
-    for h in range(HEADS):
-        lanes = slice(h * HEAD_DIM, (h + 1) * HEAD_DIM)
-        out_ref[h, 0, 0:HALF] = turn(q_ref[:, lanes], cosine * factor, sine * factor)
-        out_ref[h, 0, HALF : 2 * HALF] = turn(k_ref[:, lanes], cosine, sine)
-        out_ref[h, 0, 2 * HALF : 3 * HALF] = v_ref[:, lanes]
-    block = jnp.full((16, HEAD_DIM), starts[pl.program_id(0)] // HALF, jnp.int32)
-    block = block.astype(jnp.float32).astype(jnp.bfloat16)
-    for h in range(HEADS):
-        out_ref[h, 0, 3 * HALF :] = block
+        rolled = pltpu.roll(block, HEAD_DIM // 2, 1)
+        return (block * cosine + rolled * sine).astype(jnp.bfloat16)
+
+    for b in range(2):
+        block = jnp.full((16, HEAD_DIM), starts[b] // HALF, jnp.int32)
+        block = block.astype(jnp.float32).astype(jnp.bfloat16)
+        for h in range(HEADS):
+            index[h, b] = block
+    leave(index, out_ref.at[:, :, 3 * HALF :])
+    for b in range(2):
+        for copy in fetches[b]:
+            copy.wait()
+        for h in range(HEADS):
+            lanes = pl.ds(h * HEAD_DIM, HEAD_DIM)
+            leave(v.at[b, :, lanes], out_ref.at[h, b, 2 * HALF : 3 * HALF])
+        for part, source, scale in (0, q, factor), (1, k, 1.0):
+            cos_b, sin_b = cosine[b] * scale, sine[b] * scale
+            for h in range(HEADS):
+                lanes = slice(h * HEAD_DIM, (h + 1) * HEAD_DIM)
+                turned[b, part, h] = turn(source[b, :, lanes], cos_b, sin_b)
+            leave(turned.at[b, part], out_ref.at[:, b, part * HALF : (part + 1) * HALF])
+    for copy in stores:
+        copy.wait()
 
 
 def pack(starts, queries, keys, values):
     cosine, sine = tables()
-    rows = pl.BlockSpec((HALF, WIDTH), lambda b, s: (b, 0))
-    table = pl.BlockSpec((HALF, HEAD_DIM), lambda b, s: (s[b] // HALF, 0))
+    anywhere = pl.BlockSpec(memory_space=pl.ANY)
+    rows = pltpu.VMEM((2, HALF, WIDTH), jnp.bfloat16)
+    table = pltpu.VMEM((2, HALF, HEAD_DIM), jnp.float32)
     return pl.pallas_call(
         pack_kernel,
-        grid_spec=pltpu.PrefetchScalarGridSpec(
-            num_scalar_prefetch=1,
-            grid=(2,),
-            in_specs=[rows, rows, rows, table, table],
-            out_specs=pl.BlockSpec((HEADS, 1, ROWS, HEAD_DIM), lambda b, s: (0, b, 0, 0)),
-        ),
+        in_specs=[pl.BlockSpec(memory_space=pltpu.SMEM)] + [anywhere] * 5,
+        out_specs=anywhere,
+        scratch_shapes=[
+            rows,
+            rows,
+            rows,
+            table,
+            table,
+            pltpu.VMEM((2, 2, HEADS, HALF, HEAD_DIM), jnp.bfloat16),
+            pltpu.VMEM((HEADS, 2, 16, HEAD_DIM), jnp.bfloat16),
+            pltpu.SemaphoreType.DMA((2, 5)),
+            pltpu.SemaphoreType.DMA((1 + 2 * (HEADS + 2),)),
+        ],
         out_shape=jax.ShapeDtypeStruct((HEADS, 2, ROWS, HEAD_DIM), jnp.bfloat16),
         compiler_params=pltpu.CompilerParams(vmem_limit_bytes=VMEM),
         name="pack",
     )(starts, queries, keys, values, jnp.asarray(cosine), jnp.asarray(sine))
 
 
-def attention_kernel(x_ref, o_ref, qs, kt, vs, scores, index, pos, moved, left, *, tq, width):
+def attention_kernel(packed, o_ref, x_ref, qs, kt, vs, scores, index, pos, got, moved, left, *, tq, width):
     tiles = LEN // tq
+    fetches = [
+        pltpu.make_async_copy(packed.at[:, :, 3 * HALF :], x_ref.at[:, :, 3 * HALF :], got.at[0]),
+        *[
+            pltpu.make_async_copy(packed.at[s, :, : 3 * HALF], x_ref.at[s, :, : 3 * HALF], got.at[1 + s])
+            for s in range(HEADS)
+        ],
+    ]
+    for fetch in fetches:
+        fetch.start()
+    vs[:, HEAD_DIM:] = jnp.ones((LEN, HEAD_DIM), jnp.bfloat16)
+    fetches[0].wait()
     for t in range(2 * HEADS):
         row = x_ref[t // 2, t % 2, 3 * HALF :, :].astype(jnp.float32)
         index[t : t + 1, :] = row[:1].astype(jnp.int32)
     copy = pltpu.make_async_copy(index, pos, moved)
     copy.start()
     copy.wait()
-    vs[:, HEAD_DIM:] = jnp.ones((LEN, HEAD_DIM), jnp.bfloat16)
+    for fetch in fetches[1:]:
+        fetch.wait()
 
     def place(t, carry):
         at = pl.ds(pl.multiple_of(pos[t, 0] * HALF, HALF), HALF)
@@ -191,16 +250,18 @@
         functools.partial(attention_kernel, tq=tq, width=width),
         out_shape=pltpu.HBM((HEADS, 2, HALF, HEAD_DIM), jnp.bfloat16),
         in_specs=[
-            pl.BlockSpec(memory_space=pltpu.VMEM),
+            pl.BlockSpec(memory_space=pl.ANY),
         ],
         out_specs=pl.BlockSpec(memory_space=pltpu.HBM),
         scratch_shapes=[
+            pltpu.VMEM((HEADS, 2, ROWS, HEAD_DIM), jnp.bfloat16),
             pltpu.VMEM((LEN, HEAD_DIM), jnp.bfloat16),
             pltpu.VMEM((HEAD_DIM, LEN), jnp.bfloat16),
             pltpu.VMEM((LEN, 2 * HEAD_DIM), jnp.bfloat16),
             pltpu.VMEM((2, tq, LEN), jnp.float32),
             pltpu.VMEM((2 * HEADS, 128), jnp.int32),
             pltpu.SMEM((2 * HEADS, 128), jnp.int32),
+            pltpu.SemaphoreType.DMA((1 + HEADS,)),
             pltpu.SemaphoreType.DMA,
             pltpu.SemaphoreType.DMA((2 * HEADS,)),
         ],
@@ -318,7 +379,7 @@
 def shards(hidden_in, queries, keys, values, block_start, out_weight):
     y, xh, c = lax.axis_index("y"), lax.axis_index("xh"), lax.axis_index("c")
     packed = pack(block_start, queries[0], keys[0], values[0])
-    packed = lax.all_to_all(packed, SEQ, 0, 0, tiled=True)
+    packed = lax.all_to_all(packed, OWNERS, 0, 0, tiled=True)
 
     half = lax.dynamic_slice(out_weight, (0, c * (D // 2)), (WIDTH // 8, D // 2))
     mine, other = {}, {}
@@ -338,7 +399,7 @@
 
     attended = attention(packed)
     second, _ = lax.optimization_barrier((second, attended))
-    attended = lax.all_to_all(attended, SEQ, 0, 0, tiled=True)
+    attended = lax.all_to_all(attended, OWNERS, 0, 0, tiled=True)
     for at in second:
         mine[at] = second[at]
         other[at] = send(mine[at], core_over)

time: 108 us -> 105 us (0.972)
  starting transfers between devices: 34.2 us -> 28 us
  waiting for transfers between devices: 41 us -> 45.6 us
    ppermute x14, waiting for transfers between devices: 29.6 us -> 41.5 us  [send(): lax.ppermute(array, AXES, [(index[p], index[move(*p)]) for p in places])]
    all_to_all x2, waiting for transfers between devices: 11.3 us -> 4.04 us  [the longest x1 4.04 us: shards(): packed = lax.all_to_all(packed, OWNERS, 0, 0, tiled=True)]
    all_to_all x2, starting transfers between devices: 18.3 us -> 12.1 us  [the longest x1 7.9 us: shards(): packed = lax.all_to_all(packed, OWNERS, 0, 0, tiled=True)]
  transfers between devices with their start and end apart: 16 -> 16, of which waited for: 4 -> 5; matrix products, arithmetic and copies ran while one was open for 0% -> 0% of each run, Pallas kernels for 20% -> 19%
where the time goes in v4:
time: 105 us
  waiting for transfers between devices  45.6 us (43%)
  Pallas kernels  30.1 us (29%)
  starting transfers between devices  28 us (27%)
  local copies, waits for them, and re-layouts  1.2 us (1%)
    ppermute x14, waiting for transfers between devices, send(): lax.ppermute(array, AXES, [(index[p], index[move(*p)]) for p in places])  41.5 us
    ppermute x14, starting transfers between devices, send(): lax.ppermute(array, AXES, [(index[p], index[move(*p)]) for p in places])  15.9 us
    pallas_call x1, Pallas kernels, attention(): pl.pallas_call(functools.partial(attention_kernel, tq=tq, width=width), o...  14.7 us
    pallas_call x2, Pallas kernels, project(): pl.pallas_call(functools.partial(project_kernel, half=half), in_specs=[pl...  11.1 us
    all_to_all x1, starting transfers between devices, shards(): packed = lax.all_to_all(packed, OWNERS, 0, 0, tiled=True)  7.9 us
    pallas_call x1, Pallas kernels, pack(): pl.pallas_call(pack_kernel, in_specs=[pl.BlockSpec(memory_space=pltpu.SME...  4.37 us
    all_to_all x1, starting transfers between devices, shards(): attended = lax.all_to_all(attended, OWNERS, 0, 0, tiled=True)  4.16 us
    all_to_all x1, waiting for transfers between devices, shards(): packed = lax.all_to_all(packed, OWNERS, 0, 0, tiled=True)  4.04 us
  transfers between devices with their start and end apart: 16, of which 5 were waited for; matrix products, arithmetic and copies ran while one was open for 0% of the time, Pallas kernels for 19%

profile of v4, /device:TPU:1, one launch (start us, length us, event | category | flops | bytes accessed | tf_op | source)
XLA Modules:
  0.0 105.1 jit_solution(3789049136526649711)
XLA Ops:
  0.0 4.4 %pack.1 = bf16[16,2,400,128]{3,2,1,0:T(8,128)(2,1)} custom-call(s32[2]{0:T(128)} %starts.1, bf16[256,2048]{1,0:T(8,128)(2,1)} %bitcast.16, bf16[256,2048]{1,0:T(8,128)(2,1)} %bitcast.17, bf16[256,2048]{1,0:T(8,128)(2,1)} %bitcast.18, f32[4096,128]{1,0:T(8,128)} %constant.84.clone.cos_ref, f32[4096,128]{1,0:T(8,128)} %constant.85.clone.sin_ref), custom_call_target="tpu_custom_call" | custom-call | tf_op jit(solution)/shard_map/pack/pallas_call | solution.py:129
  4.4 0.0 copy-start
  4.4 7.9 %all-to-all-start = ((bf16[16,2,400,128]{3,2,1,0:T(8,128)(2,1)}), bf16[16,2,400,128]{3,2,1,0:T(8,128)(2,1)}, u32[]{:S(2)}, u32[]{:S(2)}) async-start(bf16[16,2,400,128]{3,2,1,0:T(8,128)(2,1)} %pack.1), calls=%async_computation | async-start | bytes 6553600 | tf_op jit(solution)/shard_map/all_to_all | solution.py:382
  12.3 0.0 copy-done
  12.3 0.1 constant_dynamic-slice_fusion
  12.4 1.4 %collective-permute-start.1 = (bf16[256,2048]{1,0:T(8,128)(2,1)S(1)}, bf16[256,2048]{1,0:T(8,128)(2,1)}, u32[]{:S(2)}, u32[]{:S(2)}) collective-permute-start(bf16[256,2048]{1,0:T(8,128)(2,1)S(1)} %constant_dynamic-slice_fusion), channel_id=1, source_target_pairs={{0,32},{1,33},{2,34},{3,35},{4,36},{5,37},{6,38},{7,39},{8,40},{9,... | collective-permute-start | bytes 3145736 | tf_op jit(solution)/shard_map/ppermute | solution.py:43
  13.8 2.7 %collective-permute-start = (bf16[256,2048]{1,0:T(8,128)(2,1)S(1)}, bf16[256,2048]{1,0:T(8,128)(2,1)}, u32[]{:S(2)}, u32[]{:S(2)}) collective-permute-start(bf16[256,2048]{1,0:T(8,128)(2,1)S(1)} %constant_dynamic-slice_fusion), channel_id=1, source_target_pairs={{0,24},{1,25},{2,26},{3,27},{4,28},{5,29},{6,30},{7,31},{8,16},{9,... | collective-permute-start | bytes 3145736 | tf_op jit(solution)/shard_map/ppermute | solution.py:43
  16.4 1.5 %collective-permute-start.4 = (bf16[256,2048]{1,0:T(8,128)(2,1)S(1)}, bf16[256,2048]{1,0:T(8,128)(2,1)}, u32[]{:S(2)}, u32[]{:S(2)}) collective-permute-start(bf16[256,2048]{1,0:T(8,128)(2,1)S(1)} %constant_dynamic-slice_fusion), channel_id=1, source_target_pairs={{0,96},{1,97},{2,98},{3,99},{4,100},{5,101},{6,102},{7,103},{8,104... | collective-permute-start | bytes 3145736 | tf_op jit(solution)/shard_map/ppermute | solution.py:43
  18.0 20.6 %collective-permute-done.1.refs_1_ = bf16[256,2048]{1,0:T(8,128)(2,1)} collective-permute-done((bf16[256,2048]{1,0:T(8,128)(2,1)S(1)}, bf16[256,2048]{1,0:T(8,128)(2,1)}, u32[]{:S(2)}, u32[]{:S(2)}) %collective-permute-start.1) | collective-permute-done | bytes 1048608 | tf_op jit(solution)/shard_map/ppermute | solution.py:43
  38.5 0.9 collective-permute-start.2
  39.4 0.0 collective-permute-start.7
  39.5 2.7 %collective-permute-start.9 = (bf16[256,2048]{1,0:T(8,128)(2,1)}, bf16[256,2048]{1,0:T(8,128)(2,1)}, u32[]{:S(2)}, u32[]{:S(2)}) collective-permute-start(bf16[256,2048]{1,0:T(8,128)(2,1)} %collective-permute-done.1.refs_1_), channel_id=1, source_target_pairs={{0,24},{1,25},{2,26},{3,27},{4,28},{5,29},{6,30},{7,31},{8,16},{9,... | collective-permute-start | bytes 3145736 | tf_op jit(solution)/shard_map/ppermute | solution.py:43
  42.1 0.0 collective-permute-done.refs_0_
  42.1 2.7 %collective-permute-start.6 = (bf16[256,2048]{1,0:T(8,128)(2,1)}, bf16[256,2048]{1,0:T(8,128)(2,1)}, u32[]{:S(2)}, u32[]{:S(2)}) collective-permute-start(bf16[256,2048]{1,0:T(8,128)(2,1)} %collective-permute-done.refs_0_), channel_id=1, source_target_pairs={{0,96},{1,97},{2,98},{3,99},{4,100},{5,101},{6,102},{7,103},{8,104... | collective-permute-start | bytes 3145736 | tf_op jit(solution)/shard_map/ppermute | solution.py:43
  44.8 0.0 collective-permute-done.4.refs_2_
  44.8 0.0 collective-permute-start.8
  44.8 0.0 collective-permute-done.2.refs_1_
  44.8 0.0 copy-start.1
  44.8 1.0 copy-done.1
  45.8 1.7 %collective-permute-start.3 = (bf16[256,2048]{1,0:T(8,128)(2,1)}, bf16[256,2048]{1,0:T(8,128)(2,1)}, u32[]{:S(2)}, u32[]{:S(2)}) collective-permute-start(bf16[256,2048]{1,0:T(8,128)(2,1)} %collective-permute-done.refs_0_), channel_id=1, source_target_pairs={{0,1},{1,0},{2,3},{3,2},{4,5},{5,4},{6,7},{7,6},{8,9},{9,8},{10,11... | collective-permute-start | bytes 3145736 | tf_op jit(solution)/shard_map/ppermute | solution.py:43
  47.5 4.0 %all-to-all-done.packed = bf16[16,2,400,128]{3,2,1,0:T(8,128)(2,1)} async-done(((bf16[16,2,400,128]{3,2,1,0:T(8,128)(2,1)}), bf16[16,2,400,128]{3,2,1,0:T(8,128)(2,1)}, u32[]{:S(2)}, u32[]{:S(2)}) %all-to-all-start) | async-done | bytes 3276832 | tf_op jit(solution)/shard_map/all_to_all | solution.py:382
  51.5 14.7 %attention.1 = bf16[16,2,128,128]{3,2,1,0:T(8,128)(2,1)} custom-call(bf16[16,2,400,128]{3,2,1,0:T(8,128)(2,1)} %all-to-all-done.packed), custom_call_target="tpu_custom_call" | custom-call | flops 17179869184 | bytes 4194304 | tf_op jit(solution)/shard_map/attention/pallas_call | solution.py:249
  66.2 4.2 %all-to-all-start.1 = ((bf16[16,2,128,128]{3,2,1,0:T(8,128)(2,1)}), bf16[16,2,128,128]{3,2,1,0:T(8,128)(2,1)S(1)}, u32[]{:S(2)}, u32[]{:S(2)}) async-start(bf16[16,2,128,128]{3,2,1,0:T(8,128)(2,1)} %attention.1), calls=%async_computation.1 | async-start | bytes 2097152 | tf_op jit(solution)/shard_map/all_to_all | solution.py:402
  70.4 0.1 stack.39.place
  70.5 0.0 collective-permute-done.7.refs_5_
  70.5 0.0 collective-permute-done.9.refs_3_
  70.5 19.0 %collective-permute-done.6.refs_4_ = bf16[256,2048]{1,0:T(8,128)(2,1)} collective-permute-done((bf16[256,2048]{1,0:T(8,128)(2,1)}, bf16[256,2048]{1,0:T(8,128)(2,1)}, u32[]{:S(2)}, u32[]{:S(2)}) %collective-permute-start.6) | collective-permute-done | bytes 1048608 | tf_op jit(solution)/shard_map/ppermute | solution.py:43
  89.5 0.0 collective-permute-done.8.refs_6_
  89.5 1.4 %collective-permute-start.10 = (bf16[256,2048]{1,0:T(8,128)(2,1)}, bf16[256,2048]{1,0:T(8,128)(2,1)}, u32[]{:S(2)}, u32[]{:S(2)}) collective-permute-start(bf16[256,2048]{1,0:T(8,128)(2,1)} %collective-permute-done.9.refs_3_), channel_id=1, source_target_pairs={{0,1},{1,0},{2,3},{3,2},{4,5},{5,4},{6,7},{7,6},{8,9},{9,8},{10,11... | collective-permute-start | bytes 3145736 | tf_op jit(solution)/shard_map/ppermute | solution.py:43
  90.9 0.0 collective-permute-start.11
  90.9 0.5 collective-permute-start.12
  91.4 0.0 collective-permute-start.13
  91.4 0.0 collective-permute-done.3.refs_0_
  91.4 0.5 collective-permute-start.5
  92.0 0.0 all-to-all-done.1.att_ref
  92.0 0.0 copy-start.2
  92.0 5.7 %project.2.refs_7_ = bf16[256,4096]{1,0:T(8,128)(2,1)} custom-call(s32[9]{0:T(128)S(1)} %stack.39.place, bf16[16,2,128,128]{3,2,1,0:T(8,128)(2,1)S(1)} %arrive.1.att_ref, bf16[256,4096]{1,0:T(8,128)(2,1)} %bitcast.14, bf16[256,4096]{1,0:T(8,128)(2,1)S(1)} %copy-done, bf16[256,2048]{1,0:T(8,128)(2,1)} %collective-permute-done.refs_0_, ...), custom_call_target="tpu_custom_call" | custom-call | flops 2147483648 | bytes 12582912 | tf_op jit(solution)/shard_map/project/pallas_call | solution.py:333
  97.6 0.0 collective-permute-done.10.refs_3_
  97.7 0.0 collective-permute-done.11.refs_4_
  97.7 0.0 collective-permute-done.12.refs_5_
  97.7 0.4 collective-permute-done.13.refs_6_
  98.1 1.5 %collective-permute-done.5.refs_2_ = bf16[256,2048]{1,0:T(8,128)(2,1)} collective-permute-done((bf16[256,2048]{1,0:T(8,128)(2,1)}, bf16[256,2048]{1,0:T(8,128)(2,1)}, u32[]{:S(2)}, u32[]{:S(2)}) %collective-permute-start.5) | collective-permute-done | bytes 1048608 | tf_op jit(solution)/shard_map/ppermute | solution.py:43
  99.6 0.0 copy-done.2
  99.6 5.4 %project.3 = bf16[256,4096]{1,0:T(8,128)(2,1)} custom-call(s32[9]{0:T(128)S(1)} %stack.39.place, bf16[16,2,128,128]{3,2,1,0:T(8,128)(2,1)S(1)} %arrive.1.att_ref, bf16[256,4096]{1,0:T(8,128)(2,1)} %bitcast.15, bf16[256,4096]{1,0:T(8,128)(2,1)S(1)} %copy-done, bf16[256,2048]{1,0:T(8,128)(2,1)} %collective-permute-done.3.refs_0_, ...), custom_call_target="tpu_custom_call", output_to_operand_aliasing={{}: (11, {})} | custom-call | flops 2147483648 | bytes 12582912 | tf_op jit(solution)/shard_map/project/pallas_call | solution.py:333
  (1 shorter events, 0.0 us)
Async XLA Ops:
  4.4 7.9 %copy-start = (bf16[256,4096]{1,0:T(8,128)(2,1)S(1)}, bf16[256,4096]{1,0:T(8,128)(2,1)}, u32[]{:S(2)}) copy-start(bf16[256,4096]{1,0:T(8,128)(2,1)} %own_ref.3) | copy-start | bytes 6291460
  4.4 47.2 %all-to-all-start = ((bf16[16,2,400,128]{3,2,1,0:T(8,128)(2,1)}), bf16[16,2,400,128]{3,2,1,0:T(8,128)(2,1)}, u32[]{:S(2)}, u32[]{:S(2)}) async-start(bf16[16,2,400,128]{3,2,1,0:T(8,128)(2,1)} %pack.1), calls=%async_computation | async-start | bytes 6553600 | tf_op jit(solution)/shard_map/all_to_all | solution.py:382
  12.4 26.1 %collective-permute-start.1 = (bf16[256,2048]{1,0:T(8,128)(2,1)S(1)}, bf16[256,2048]{1,0:T(8,128)(2,1)}, u32[]{:S(2)}, u32[]{:S(2)}) collective-permute-start(bf16[256,2048]{1,0:T(8,128)(2,1)S(1)} %constant_dynamic-slice_fusion), channel_id=1, source_target_pairs={{0,32},{1,33},{2,34},{3,35},{4,36},{5,37},{6,38},{7,39},{8,40},{9,... | collective-permute-start | bytes 3145736 | tf_op jit(solution)/shard_map/ppermute | solution.py:43
  13.8 28.3 %collective-permute-start = (bf16[256,2048]{1,0:T(8,128)(2,1)S(1)}, bf16[256,2048]{1,0:T(8,128)(2,1)}, u32[]{:S(2)}, u32[]{:S(2)}) collective-permute-start(bf16[256,2048]{1,0:T(8,128)(2,1)S(1)} %constant_dynamic-slice_fusion), channel_id=1, source_target_pairs={{0,24},{1,25},{2,26},{3,27},{4,28},{5,29},{6,30},{7,31},{8,16},{9,... | collective-permute-start | bytes 3145736 | tf_op jit(solution)/shard_map/ppermute | solution.py:43
  16.4 28.3 %collective-permute-start.4 = (bf16[256,2048]{1,0:T(8,128)(2,1)S(1)}, bf16[256,2048]{1,0:T(8,128)(2,1)}, u32[]{:S(2)}, u32[]{:S(2)}) collective-permute-start(bf16[256,2048]{1,0:T(8,128)(2,1)S(1)} %constant_dynamic-slice_fusion), channel_id=1, source_target_pairs={{0,96},{1,97},{2,98},{3,99},{4,100},{5,101},{6,102},{7,103},{8,104... | collective-permute-start | bytes 3145736 | tf_op jit(solution)/shard_map/ppermute | solution.py:43
  38.5 6.2 %collective-permute-start.2 = (bf16[256,2048]{1,0:T(8,128)(2,1)}, bf16[256,2048]{1,0:T(8,128)(2,1)S(1)}, u32[]{:S(2)}, u32[]{:S(2)}) collective-permute-start(bf16[256,2048]{1,0:T(8,128)(2,1)} %collective-permute-done.1.refs_1_), channel_id=1, source_target_pairs={{0,1},{1,0},{2,3},{3,2},{4,5},{5,4},{6,7},{7,6},{8,9},{9,8},{10,11... | collective-permute-start | bytes 3145736 | tf_op jit(solution)/shard_map/ppermute | solution.py:43
  39.4 31.0 %collective-permute-start.7 = (bf16[256,2048]{1,0:T(8,128)(2,1)}, bf16[256,2048]{1,0:T(8,128)(2,1)}, u32[]{:S(2)}, u32[]{:S(2)}) collective-permute-start(bf16[256,2048]{1,0:T(8,128)(2,1)} %collective-permute-done.1.refs_1_), channel_id=1, source_target_pairs={{0,32},{1,33},{2,34},{3,35},{4,36},{5,37},{6,38},{7,39},{8,40},{9,... | collective-permute-start | bytes 3145736 | tf_op jit(solution)/shard_map/ppermute | solution.py:43
  39.5 31.0 %collective-permute-start.9 = (bf16[256,2048]{1,0:T(8,128)(2,1)}, bf16[256,2048]{1,0:T(8,128)(2,1)}, u32[]{:S(2)}, u32[]{:S(2)}) collective-permute-start(bf16[256,2048]{1,0:T(8,128)(2,1)} %collective-permute-done.1.refs_1_), channel_id=1, source_target_pairs={{0,24},{1,25},{2,26},{3,27},{4,28},{5,29},{6,30},{7,31},{8,16},{9,... | collective-permute-start | bytes 3145736 | tf_op jit(solution)/shard_map/ppermute | solution.py:43
  42.1 47.4 %collective-permute-start.6 = (bf16[256,2048]{1,0:T(8,128)(2,1)}, bf16[256,2048]{1,0:T(8,128)(2,1)}, u32[]{:S(2)}, u32[]{:S(2)}) collective-permute-start(bf16[256,2048]{1,0:T(8,128)(2,1)} %collective-permute-done.refs_0_), channel_id=1, source_target_pairs={{0,96},{1,97},{2,98},{3,99},{4,100},{5,101},{6,102},{7,103},{8,104... | collective-permute-start | bytes 3145736 | tf_op jit(solution)/shard_map/ppermute | solution.py:43
  44.8 44.7 %collective-permute-start.8 = (bf16[256,2048]{1,0:T(8,128)(2,1)}, bf16[256,2048]{1,0:T(8,128)(2,1)}, u32[]{:S(2)}, u32[]{:S(2)}) collective-permute-start(bf16[256,2048]{1,0:T(8,128)(2,1)} %collective-permute-done.4.refs_2_), channel_id=1, source_target_pairs={{0,120},{1,121},{2,122},{3,123},{4,124},{5,125},{6,126},{7,127},{8... | collective-permute-start | bytes 3145736 | tf_op jit(solution)/shard_map/ppermute | solution.py:43
  44.8 1.0 copy-start.1
  45.8 45.7 %collective-permute-start.3 = (bf16[256,2048]{1,0:T(8,128)(2,1)}, bf16[256,2048]{1,0:T(8,128)(2,1)}, u32[]{:S(2)}, u32[]{:S(2)}) collective-permute-start(bf16[256,2048]{1,0:T(8,128)(2,1)} %collective-permute-done.refs_0_), channel_id=1, source_target_pairs={{0,1},{1,0},{2,3},{3,2},{4,5},{5,4},{6,7},{7,6},{8,9},{9,8},{10,11... | collective-permute-start | bytes 3145736 | tf_op jit(solution)/shard_map/ppermute | solution.py:43
  66.2 25.7 %all-to-all-start.1 = ((bf16[16,2,128,128]{3,2,1,0:T(8,128)(2,1)}), bf16[16,2,128,128]{3,2,1,0:T(8,128)(2,1)S(1)}, u32[]{:S(2)}, u32[]{:S(2)}) async-start(bf16[16,2,128,128]{3,2,1,0:T(8,128)(2,1)} %attention.1), calls=%async_computation.1 | async-start | bytes 2097152 | tf_op jit(solution)/shard_map/all_to_all | solution.py:402
  89.5 8.1 %collective-permute-start.10 = (bf16[256,2048]{1,0:T(8,128)(2,1)}, bf16[256,2048]{1,0:T(8,128)(2,1)}, u32[]{:S(2)}, u32[]{:S(2)}) collective-permute-start(bf16[256,2048]{1,0:T(8,128)(2,1)} %collective-permute-done.9.refs_3_), channel_id=1, source_target_pairs={{0,1},{1,0},{2,3},{3,2},{4,5},{5,4},{6,7},{7,6},{8,9},{9,8},{10,11... | collective-permute-start | bytes 3145736 | tf_op jit(solution)/shard_map/ppermute | solution.py:43
  90.9 6.7 %collective-permute-start.11 = (bf16[256,2048]{1,0:T(8,128)(2,1)}, bf16[256,2048]{1,0:T(8,128)(2,1)}, u32[]{:S(2)}, u32[]{:S(2)}) collective-permute-start(bf16[256,2048]{1,0:T(8,128)(2,1)} %collective-permute-done.6.refs_4_), channel_id=1, source_target_pairs={{0,1},{1,0},{2,3},{3,2},{4,5},{5,4},{6,7},{7,6},{8,9},{9,8},{10,11... | collective-permute-start | bytes 3145736 | tf_op jit(solution)/shard_map/ppermute | solution.py:43
  90.9 6.7 %collective-permute-start.12 = (bf16[256,2048]{1,0:T(8,128)(2,1)}, bf16[256,2048]{1,0:T(8,128)(2,1)}, u32[]{:S(2)}, u32[]{:S(2)}) collective-permute-start(bf16[256,2048]{1,0:T(8,128)(2,1)} %collective-permute-done.7.refs_5_), channel_id=1, source_target_pairs={{0,1},{1,0},{2,3},{3,2},{4,5},{5,4},{6,7},{7,6},{8,9},{9,8},{10,11... | collective-permute-start | bytes 3145736 | tf_op jit(solution)/shard_map/ppermute | solution.py:43
  91.4 6.6 %collective-permute-start.13 = (bf16[256,2048]{1,0:T(8,128)(2,1)}, bf16[256,2048]{1,0:T(8,128)(2,1)}, u32[]{:S(2)}, u32[]{:S(2)}) collective-permute-start(bf16[256,2048]{1,0:T(8,128)(2,1)} %collective-permute-done.8.refs_6_), channel_id=1, source_target_pairs={{0,1},{1,0},{2,3},{3,2},{4,5},{5,4},{6,7},{7,6},{8,9},{9,8},{10,11... | collective-permute-start | bytes 3145736 | tf_op jit(solution)/shard_map/ppermute | solution.py:43
  91.4 8.1 %collective-permute-start.5 = (bf16[256,2048]{1,0:T(8,128)(2,1)}, bf16[256,2048]{1,0:T(8,128)(2,1)}, u32[]{:S(2)}, u32[]{:S(2)}) collective-permute-start(bf16[256,2048]{1,0:T(8,128)(2,1)} %collective-permute-done.4.refs_2_), channel_id=1, source_target_pairs={{0,1},{1,0},{2,3},{3,2},{4,5},{5,4},{6,7},{7,6},{8,9},{9,8},{10,11... | collective-permute-start | bytes 3145736 | tf_op jit(solution)/shard_map/ppermute | solution.py:43
  92.0 7.6 %copy-start.2 = (bf16[256,2048]{1,0:T(8,128)(2,1)S(1)}, bf16[256,2048]{1,0:T(8,128)(2,1)}, u32[]{:S(2)}) copy-start(bf16[256,2048]{1,0:T(8,128)(2,1)} %copy-done.1) | copy-start | bytes 3145732

commit v5 on v4

--- a/solution.py
+++ b/solution.py
@@ -393,12 +393,14 @@
         (2, 1): send(mine[1, 0], x_over_y_down),
     }
     before = mine[3, 0]
-    for at in (3, 0), (0, 1), (1, 0):
+    for at in (3, 0), (0, 1):
         piece, _ = lax.optimization_barrier((mine[at], before))
         other[at] = before = send(piece, core_over)
 
     attended = attention(packed)
-    second, _ = lax.optimization_barrier((second, attended))
+    piece, _ = lax.optimization_barrier((mine[1, 0], (attended, before)))
+    other[1, 0] = send(piece, core_over)
+    second, _ = lax.optimization_barrier((second, other[1, 0]))
     attended = lax.all_to_all(attended, OWNERS, 0, 0, tiled=True)
     for at in second:
         mine[at] = second[at]

time: 105 us -> 104 us (level)
  waiting for transfers between devices: 45.6 us -> 43.4 us
    ppermute x14, waiting for transfers between devices: 41.5 us -> 39.3 us  [send(): lax.ppermute(array, AXES, [(index[p], index[move(*p)]) for p in places])]
  transfers between devices with their start and end apart: 16 -> 16, of which waited for: 5 -> 4; matrix products, arithmetic and copies ran while one was open for 0% -> 0% of each run, Pallas kernels for 19% -> 20%
where the time goes in v5:
time: 104 us
  waiting for transfers between devices  43.4 us (42%)
  Pallas kernels  30 us (29%)
  starting transfers between devices  27.7 us (27%)
  local copies, waits for them, and re-layouts  2.18 us (2%)
    ppermute x14, waiting for transfers between devices, send(): lax.ppermute(array, AXES, [(index[p], index[move(*p)]) for p in places])  39.3 us
    ppermute x14, starting transfers between devices, send(): lax.ppermute(array, AXES, [(index[p], index[move(*p)]) for p in places])  15.7 us
    pallas_call x1, Pallas kernels, attention(): pl.pallas_call(functools.partial(attention_kernel, tq=tq, width=width), o...  14.7 us
    pallas_call x2, Pallas kernels, project(): pl.pallas_call(functools.partial(project_kernel, half=half), in_specs=[pl...  10.9 us
    all_to_all x1, starting transfers between devices, shards(): packed = lax.all_to_all(packed, OWNERS, 0, 0, tiled=True)  7.9 us
    pallas_call x1, Pallas kernels, pack(): pl.pallas_call(pack_kernel, in_specs=[pl.BlockSpec(memory_space=pltpu.SME...  4.42 us
    all_to_all x1, starting transfers between devices, shards(): attended = lax.all_to_all(attended, OWNERS, 0, 0, tiled=True)  4.11 us
    all_to_all x1, waiting for transfers between devices, shards(): packed = lax.all_to_all(packed, OWNERS, 0, 0, tiled=True)  4.05 us
  transfers between devices with their start and end apart: 16, of which 4 were waited for; matrix products, arithmetic and copies ran while one was open for 0% of the time, Pallas kernels for 20%

profile of v5, /device:TPU:1, one launch (start us, length us, event | category | flops | bytes accessed | tf_op | source)
XLA Modules:
  0.0 103.5 jit_solution(446590213152360481)
XLA Ops:
  0.0 4.4 %pack.1 = bf16[16,2,400,128]{3,2,1,0:T(8,128)(2,1)} custom-call(s32[2]{0:T(128)} %starts.1, bf16[256,2048]{1,0:T(8,128)(2,1)} %bitcast.16, bf16[256,2048]{1,0:T(8,128)(2,1)} %bitcast.17, bf16[256,2048]{1,0:T(8,128)(2,1)} %bitcast.18, f32[4096,128]{1,0:T(8,128)} %constant.84.clone.cos_ref, f32[4096,128]{1,0:T(8,128)} %constant.85.clone.sin_ref), custom_call_target="tpu_custom_call" | custom-call | tf_op jit(solution)/shard_map/pack/pallas_call | solution.py:129
  4.4 0.0 copy-start
  4.4 7.9 %all-to-all-start = ((bf16[16,2,400,128]{3,2,1,0:T(8,128)(2,1)}), bf16[16,2,400,128]{3,2,1,0:T(8,128)(2,1)}, u32[]{:S(2)}, u32[]{:S(2)}) async-start(bf16[16,2,400,128]{3,2,1,0:T(8,128)(2,1)} %pack.1), calls=%async_computation | async-start | bytes 6553600 | tf_op jit(solution)/shard_map/all_to_all | solution.py:382
  12.3 0.0 copy-done
  12.3 0.1 constant_dynamic-slice_fusion
  12.5 1.4 %collective-permute-start.1 = (bf16[256,2048]{1,0:T(8,128)(2,1)S(1)}, bf16[256,2048]{1,0:T(8,128)(2,1)}, u32[]{:S(2)}, u32[]{:S(2)}) collective-permute-start(bf16[256,2048]{1,0:T(8,128)(2,1)S(1)} %constant_dynamic-slice_fusion), channel_id=1, source_target_pairs={{0,32},{1,33},{2,34},{3,35},{4,36},{5,37},{6,38},{7,39},{8,40},{9,... | collective-permute-start | bytes 3145736 | tf_op jit(solution)/shard_map/ppermute | solution.py:43
  13.8 2.7 %collective-permute-start = (bf16[256,2048]{1,0:T(8,128)(2,1)S(1)}, bf16[256,2048]{1,0:T(8,128)(2,1)}, u32[]{:S(2)}, u32[]{:S(2)}) collective-permute-start(bf16[256,2048]{1,0:T(8,128)(2,1)S(1)} %constant_dynamic-slice_fusion), channel_id=1, source_target_pairs={{0,24},{1,25},{2,26},{3,27},{4,28},{5,29},{6,30},{7,31},{8,16},{9,... | collective-permute-start | bytes 3145736 | tf_op jit(solution)/shard_map/ppermute | solution.py:43
  16.5 1.5 %collective-permute-start.4 = (bf16[256,2048]{1,0:T(8,128)(2,1)S(1)}, bf16[256,2048]{1,0:T(8,128)(2,1)}, u32[]{:S(2)}, u32[]{:S(2)}) collective-permute-start(bf16[256,2048]{1,0:T(8,128)(2,1)S(1)} %constant_dynamic-slice_fusion), channel_id=1, source_target_pairs={{0,96},{1,97},{2,98},{3,99},{4,100},{5,101},{6,102},{7,103},{8,104... | collective-permute-start | bytes 3145736 | tf_op jit(solution)/shard_map/ppermute | solution.py:43
  18.0 20.6 %collective-permute-done.1.refs_1_ = bf16[256,2048]{1,0:T(8,128)(2,1)} collective-permute-done((bf16[256,2048]{1,0:T(8,128)(2,1)S(1)}, bf16[256,2048]{1,0:T(8,128)(2,1)}, u32[]{:S(2)}, u32[]{:S(2)}) %collective-permute-start.1) | collective-permute-done | bytes 1048608 | tf_op jit(solution)/shard_map/ppermute | solution.py:43
  38.6 0.9 collective-permute-start.2
  39.5 0.0 collective-permute-start.7
  39.5 2.7 %collective-permute-start.9 = (bf16[256,2048]{1,0:T(8,128)(2,1)}, bf16[256,2048]{1,0:T(8,128)(2,1)}, u32[]{:S(2)}, u32[]{:S(2)}) collective-permute-start(bf16[256,2048]{1,0:T(8,128)(2,1)} %collective-permute-done.1.refs_1_), channel_id=1, source_target_pairs={{0,24},{1,25},{2,26},{3,27},{4,28},{5,29},{6,30},{7,31},{8,16},{9,... | collective-permute-start | bytes 3145736 | tf_op jit(solution)/shard_map/ppermute | solution.py:43
  42.2 0.0 collective-permute-done.refs_0_
  42.2 2.7 %collective-permute-start.6 = (bf16[256,2048]{1,0:T(8,128)(2,1)}, bf16[256,2048]{1,0:T(8,128)(2,1)}, u32[]{:S(2)}, u32[]{:S(2)}) collective-permute-start(bf16[256,2048]{1,0:T(8,128)(2,1)} %collective-permute-done.refs_0_), channel_id=1, source_target_pairs={{0,96},{1,97},{2,98},{3,99},{4,100},{5,101},{6,102},{7,103},{8,104... | collective-permute-start | bytes 3145736 | tf_op jit(solution)/shard_map/ppermute | solution.py:43
  44.8 0.0 collective-permute-done.4.refs_2_
  44.8 0.0 collective-permute-start.8
  44.8 0.0 collective-permute-done.2.refs_1_
  44.8 0.0 copy-start.1
  44.8 1.0 copy-done.1
  45.8 1.7 %collective-permute-start.3 = (bf16[256,2048]{1,0:T(8,128)(2,1)}, bf16[256,2048]{1,0:T(8,128)(2,1)S(1)}, u32[]{:S(2)}, u32[]{:S(2)}) collective-permute-start(bf16[256,2048]{1,0:T(8,128)(2,1)} %collective-permute-done.refs_0_), channel_id=1, source_target_pairs={{0,1},{1,0},{2,3},{3,2},{4,5},{5,4},{6,7},{7,6},{8,9},{9,8},{10,11... | collective-permute-start | bytes 3145736 | tf_op jit(solution)/shard_map/ppermute | solution.py:43
  47.5 4.1 %all-to-all-done.packed = bf16[16,2,400,128]{3,2,1,0:T(8,128)(2,1)} async-done(((bf16[16,2,400,128]{3,2,1,0:T(8,128)(2,1)}), bf16[16,2,400,128]{3,2,1,0:T(8,128)(2,1)}, u32[]{:S(2)}, u32[]{:S(2)}) %all-to-all-start) | async-done | bytes 3276832 | tf_op jit(solution)/shard_map/all_to_all | solution.py:382
  51.6 14.7 %attention.1 = bf16[16,2,128,128]{3,2,1,0:T(8,128)(2,1)} custom-call(bf16[16,2,400,128]{3,2,1,0:T(8,128)(2,1)} %all-to-all-done.packed), custom_call_target="tpu_custom_call" | custom-call | flops 17179869184 | bytes 4194304 | tf_op jit(solution)/shard_map/attention/pallas_call | solution.py:249
  66.3 0.0 collective-permute-done.3.refs_0_
  66.3 0.0 copy-start.3
  66.3 1.0 copy-done.3
  67.3 0.2 collective-permute-start.5
  67.5 4.1 %all-to-all-start.1 = ((bf16[16,2,128,128]{3,2,1,0:T(8,128)(2,1)}), bf16[16,2,128,128]{3,2,1,0:T(8,128)(2,1)S(1)}, u32[]{:S(2)}, u32[]{:S(2)}) async-start(bf16[16,2,128,128]{3,2,1,0:T(8,128)(2,1)} %attention.1), calls=%async_computation.1 | async-start | bytes 2097152 | tf_op jit(solution)/shard_map/all_to_all | solution.py:404
  71.6 0.1 stack.39.place
  71.7 0.0 collective-permute-done.7.refs_5_
  71.7 0.0 collective-permute-done.9.refs_3_
  71.7 17.9 %collective-permute-done.6.refs_4_ = bf16[256,2048]{1,0:T(8,128)(2,1)} collective-permute-done((bf16[256,2048]{1,0:T(8,128)(2,1)}, bf16[256,2048]{1,0:T(8,128)(2,1)}, u32[]{:S(2)}, u32[]{:S(2)}) %collective-permute-start.6) | collective-permute-done | bytes 1048608 | tf_op jit(solution)/shard_map/ppermute | solution.py:43
  89.6 0.0 collective-permute-done.8.refs_6_
  89.6 0.0 collective-permute-done.5.refs_2_
  89.6 1.4 %collective-permute-start.10 = (bf16[256,2048]{1,0:T(8,128)(2,1)}, bf16[256,2048]{1,0:T(8,128)(2,1)}, u32[]{:S(2)}, u32[]{:S(2)}) collective-permute-start(bf16[256,2048]{1,0:T(8,128)(2,1)} %collective-permute-done.9.refs_3_), channel_id=1, source_target_pairs={{0,1},{1,0},{2,3},{3,2},{4,5},{5,4},{6,7},{7,6},{8,9},{9,8},{10,11... | collective-permute-start | bytes 3145736 | tf_op jit(solution)/shard_map/ppermute | solution.py:43
  91.0 0.1 collective-permute-start.11
  91.1 0.4 collective-permute-start.12
  91.5 0.1 collective-permute-start.13
  91.6 0.0 all-to-all-done.1.att_ref
  91.6 0.0 copy-start.2
  91.6 0.0 copy-start.4
  91.6 5.7 %project.2.refs_7_ = bf16[256,4096]{1,0:T(8,128)(2,1)} custom-call(s32[9]{0:T(128)S(1)} %stack.39.place, bf16[16,2,128,128]{3,2,1,0:T(8,128)(2,1)S(1)} %arrive.1.att_ref, bf16[256,4096]{1,0:T(8,128)(2,1)} %bitcast.14, bf16[256,4096]{1,0:T(8,128)(2,1)S(1)} %copy-done, bf16[256,2048]{1,0:T(8,128)(2,1)} %collective-permute-done.refs_0_, ...), custom_call_target="tpu_custom_call" | custom-call | flops 2147483648 | bytes 12582912 | tf_op jit(solution)/shard_map/project/pallas_call | solution.py:333
  97.3 0.0 collective-permute-done.10.refs_3_
  97.3 0.0 collective-permute-done.11.refs_4_
  97.3 0.0 collective-permute-done.12.refs_5_
  97.3 0.8 collective-permute-done.13.refs_6_
  98.1 0.0 copy-done.2
  98.1 0.0 copy-done.4
  98.1 5.2 %project.3 = bf16[256,4096]{1,0:T(8,128)(2,1)} custom-call(s32[9]{0:T(128)S(1)} %stack.39.place, bf16[16,2,128,128]{3,2,1,0:T(8,128)(2,1)S(1)} %arrive.1.att_ref, bf16[256,4096]{1,0:T(8,128)(2,1)} %bitcast.15, bf16[256,4096]{1,0:T(8,128)(2,1)S(1)} %copy-done, bf16[256,2048]{1,0:T(8,128)(2,1)S(1)} %copy-done.4, ...), custom_call_target="tpu_custom_call", output_to_operand_aliasing={{}: (11, {})} | custom-call | flops 2147483648 | bytes 12582912 | tf_op jit(solution)/shard_map/project/pallas_call | solution.py:333
  (1 shorter events, 0.0 us)
Async XLA Ops:
  4.4 7.9 %copy-start = (bf16[256,4096]{1,0:T(8,128)(2,1)S(1)}, bf16[256,4096]{1,0:T(8,128)(2,1)}, u32[]{:S(2)}) copy-start(bf16[256,4096]{1,0:T(8,128)(2,1)} %own_ref.3) | copy-start | bytes 6291460
  4.4 47.2 %all-to-all-start = ((bf16[16,2,400,128]{3,2,1,0:T(8,128)(2,1)}), bf16[16,2,400,128]{3,2,1,0:T(8,128)(2,1)}, u32[]{:S(2)}, u32[]{:S(2)}) async-start(bf16[16,2,400,128]{3,2,1,0:T(8,128)(2,1)} %pack.1), calls=%async_computation | async-start | bytes 6553600 | tf_op jit(solution)/shard_map/all_to_all | solution.py:382
  12.5 26.1 %collective-permute-start.1 = (bf16[256,2048]{1,0:T(8,128)(2,1)S(1)}, bf16[256,2048]{1,0:T(8,128)(2,1)}, u32[]{:S(2)}, u32[]{:S(2)}) collective-permute-start(bf16[256,2048]{1,0:T(8,128)(2,1)S(1)} %constant_dynamic-slice_fusion), channel_id=1, source_target_pairs={{0,32},{1,33},{2,34},{3,35},{4,36},{5,37},{6,38},{7,39},{8,40},{9,... | collective-permute-start | bytes 3145736 | tf_op jit(solution)/shard_map/ppermute | solution.py:43
  13.8 28.3 %collective-permute-start = (bf16[256,2048]{1,0:T(8,128)(2,1)S(1)}, bf16[256,2048]{1,0:T(8,128)(2,1)}, u32[]{:S(2)}, u32[]{:S(2)}) collective-permute-start(bf16[256,2048]{1,0:T(8,128)(2,1)S(1)} %constant_dynamic-slice_fusion), channel_id=1, source_target_pairs={{0,24},{1,25},{2,26},{3,27},{4,28},{5,29},{6,30},{7,31},{8,16},{9,... | collective-permute-start | bytes 3145736 | tf_op jit(solution)/shard_map/ppermute | solution.py:43
  16.5 28.3 %collective-permute-start.4 = (bf16[256,2048]{1,0:T(8,128)(2,1)S(1)}, bf16[256,2048]{1,0:T(8,128)(2,1)}, u32[]{:S(2)}, u32[]{:S(2)}) collective-permute-start(bf16[256,2048]{1,0:T(8,128)(2,1)S(1)} %constant_dynamic-slice_fusion), channel_id=1, source_target_pairs={{0,96},{1,97},{2,98},{3,99},{4,100},{5,101},{6,102},{7,103},{8,104... | collective-permute-start | bytes 3145736 | tf_op jit(solution)/shard_map/ppermute | solution.py:43
  38.6 6.2 %collective-permute-start.2 = (bf16[256,2048]{1,0:T(8,128)(2,1)}, bf16[256,2048]{1,0:T(8,128)(2,1)S(1)}, u32[]{:S(2)}, u32[]{:S(2)}) collective-permute-start(bf16[256,2048]{1,0:T(8,128)(2,1)} %collective-permute-done.1.refs_1_), channel_id=1, source_target_pairs={{0,1},{1,0},{2,3},{3,2},{4,5},{5,4},{6,7},{7,6},{8,9},{9,8},{10,11... | collective-permute-start | bytes 3145736 | tf_op jit(solution)/shard_map/ppermute | solution.py:43
  39.5 32.2 %collective-permute-start.7 = (bf16[256,2048]{1,0:T(8,128)(2,1)}, bf16[256,2048]{1,0:T(8,128)(2,1)}, u32[]{:S(2)}, u32[]{:S(2)}) collective-permute-start(bf16[256,2048]{1,0:T(8,128)(2,1)} %collective-permute-done.1.refs_1_), channel_id=1, source_target_pairs={{0,32},{1,33},{2,34},{3,35},{4,36},{5,37},{6,38},{7,39},{8,40},{9,... | collective-permute-start | bytes 3145736 | tf_op jit(solution)/shard_map/ppermute | solution.py:43
  39.5 32.2 %collective-permute-start.9 = (bf16[256,2048]{1,0:T(8,128)(2,1)}, bf16[256,2048]{1,0:T(8,128)(2,1)}, u32[]{:S(2)}, u32[]{:S(2)}) collective-permute-start(bf16[256,2048]{1,0:T(8,128)(2,1)} %collective-permute-done.1.refs_1_), channel_id=1, source_target_pairs={{0,24},{1,25},{2,26},{3,27},{4,28},{5,29},{6,30},{7,31},{8,16},{9,... | collective-permute-start | bytes 3145736 | tf_op jit(solution)/shard_map/ppermute | solution.py:43
  42.2 47.4 %collective-permute-start.6 = (bf16[256,2048]{1,0:T(8,128)(2,1)}, bf16[256,2048]{1,0:T(8,128)(2,1)}, u32[]{:S(2)}, u32[]{:S(2)}) collective-permute-start(bf16[256,2048]{1,0:T(8,128)(2,1)} %collective-permute-done.refs_0_), channel_id=1, source_target_pairs={{0,96},{1,97},{2,98},{3,99},{4,100},{5,101},{6,102},{7,103},{8,104... | collective-permute-start | bytes 3145736 | tf_op jit(solution)/shard_map/ppermute | solution.py:43
  44.8 44.7 %collective-permute-start.8 = (bf16[256,2048]{1,0:T(8,128)(2,1)}, bf16[256,2048]{1,0:T(8,128)(2,1)}, u32[]{:S(2)}, u32[]{:S(2)}) collective-permute-start(bf16[256,2048]{1,0:T(8,128)(2,1)} %collective-permute-done.4.refs_2_), channel_id=1, source_target_pairs={{0,120},{1,121},{2,122},{3,123},{4,124},{5,125},{6,126},{7,127},{8... | collective-permute-start | bytes 3145736 | tf_op jit(solution)/shard_map/ppermute | solution.py:43
  44.8 1.0 copy-start.1
  45.8 20.4 %collective-permute-start.3 = (bf16[256,2048]{1,0:T(8,128)(2,1)}, bf16[256,2048]{1,0:T(8,128)(2,1)S(1)}, u32[]{:S(2)}, u32[]{:S(2)}) collective-permute-start(bf16[256,2048]{1,0:T(8,128)(2,1)} %collective-permute-done.refs_0_), channel_id=1, source_target_pairs={{0,1},{1,0},{2,3},{3,2},{4,5},{5,4},{6,7},{7,6},{8,9},{9,8},{10,11... | collective-permute-start | bytes 3145736 | tf_op jit(solution)/shard_map/ppermute | solution.py:43
  66.3 1.0 copy-start.3
  67.3 22.3 %collective-permute-start.5 = (bf16[256,2048]{1,0:T(8,128)(2,1)}, bf16[256,2048]{1,0:T(8,128)(2,1)}, u32[]{:S(2)}, u32[]{:S(2)}) collective-permute-start(bf16[256,2048]{1,0:T(8,128)(2,1)} %collective-permute-done.4.refs_2_), channel_id=1, source_target_pairs={{0,1},{1,0},{2,3},{3,2},{4,5},{5,4},{6,7},{7,6},{8,9},{9,8},{10,11... | collective-permute-start | bytes 3145736 | tf_op jit(solution)/shard_map/ppermute | solution.py:43
  67.5 24.1 %all-to-all-start.1 = ((bf16[16,2,128,128]{3,2,1,0:T(8,128)(2,1)}), bf16[16,2,128,128]{3,2,1,0:T(8,128)(2,1)S(1)}, u32[]{:S(2)}, u32[]{:S(2)}) async-start(bf16[16,2,128,128]{3,2,1,0:T(8,128)(2,1)} %attention.1), calls=%async_computation.1 | async-start | bytes 2097152 | tf_op jit(solution)/shard_map/all_to_all | solution.py:404
  89.6 7.7 %collective-permute-start.10 = (bf16[256,2048]{1,0:T(8,128)(2,1)}, bf16[256,2048]{1,0:T(8,128)(2,1)}, u32[]{:S(2)}, u32[]{:S(2)}) collective-permute-start(bf16[256,2048]{1,0:T(8,128)(2,1)} %collective-permute-done.9.refs_3_), channel_id=1, source_target_pairs={{0,1},{1,0},{2,3},{3,2},{4,5},{5,4},{6,7},{7,6},{8,9},{9,8},{10,11... | collective-permute-start | bytes 3145736 | tf_op jit(solution)/shard_map/ppermute | solution.py:43
  91.0 6.3 %collective-permute-start.11 = (bf16[256,2048]{1,0:T(8,128)(2,1)}, bf16[256,2048]{1,0:T(8,128)(2,1)}, u32[]{:S(2)}, u32[]{:S(2)}) collective-permute-start(bf16[256,2048]{1,0:T(8,128)(2,1)} %collective-permute-done.6.refs_4_), channel_id=1, source_target_pairs={{0,1},{1,0},{2,3},{3,2},{4,5},{5,4},{6,7},{7,6},{8,9},{9,8},{10,11... | collective-permute-start | bytes 3145736 | tf_op jit(solution)/shard_map/ppermute | solution.py:43
  91.1 6.2 %collective-permute-start.12 = (bf16[256,2048]{1,0:T(8,128)(2,1)}, bf16[256,2048]{1,0:T(8,128)(2,1)}, u32[]{:S(2)}, u32[]{:S(2)}) collective-permute-start(bf16[256,2048]{1,0:T(8,128)(2,1)} %collective-permute-done.7.refs_5_), channel_id=1, source_target_pairs={{0,1},{1,0},{2,3},{3,2},{4,5},{5,4},{6,7},{7,6},{8,9},{9,8},{10,11... | collective-permute-start | bytes 3145736 | tf_op jit(solution)/shard_map/ppermute | solution.py:43
  91.5 6.6 %collective-permute-start.13 = (bf16[256,2048]{1,0:T(8,128)(2,1)}, bf16[256,2048]{1,0:T(8,128)(2,1)}, u32[]{:S(2)}, u32[]{:S(2)}) collective-permute-start(bf16[256,2048]{1,0:T(8,128)(2,1)} %collective-permute-done.8.refs_6_), channel_id=1, source_target_pairs={{0,1},{1,0},{2,3},{3,2},{4,5},{5,4},{6,7},{7,6},{8,9},{9,8},{10,11... | collective-permute-start | bytes 3145736 | tf_op jit(solution)/shard_map/ppermute | solution.py:43
  91.6 6.5 %copy-start.2 = (bf16[256,2048]{1,0:T(8,128)(2,1)S(1)}, bf16[256,2048]{1,0:T(8,128)(2,1)}, u32[]{:S(2)}) copy-start(bf16[256,2048]{1,0:T(8,128)(2,1)} %copy-done.1) | copy-start | bytes 3145732
  91.6 6.5 %copy-start.4 = (bf16[256,2048]{1,0:T(8,128)(2,1)S(1)}, bf16[256,2048]{1,0:T(8,128)(2,1)}, u32[]{:S(2)}) copy-start(bf16[256,2048]{1,0:T(8,128)(2,1)} %copy-done.3) | copy-start | bytes 3145732
